TPU v7x, 32 devices: a whole 2x2x4 slice. The times are simulated.
32 devices in a mesh: req: 4 (over x, core), blk: 8 (over z, y).
Axes of the slice: x: 2, y: 2, z: 4, core: 2. Of those that a mesh axis runs over, the one named last changes fastest.
Arguments:
- queries: bfloat16 [4, 8, 512, 512], P('req', 'blk'), may hold values from -6 to 6
- keys: bfloat16 [4, 8, 512, 256], P('req', 'blk'), may hold values from -25 to 25
- values: bfloat16 [4, 8, 512, 256], P('req', 'blk'), may hold values from -6 to 6
- block_map: int32 [4, 2, 2], P('req'), may hold values from 0 to 3, as said below
- lengths: int32 [4], P('req'), may hold values from 256 to 1024
- group_of_prompt: int32 [4], replicated, may hold values from 0 to 3, each once
- decode_rank: int32 [4, 8], P('req'), may hold values from 0 to 7, as said below
Outputs:
- attended: bfloat16 [4, 8, 512, 512], P('req', 'blk')
- cache: bfloat16 [4, 1024, 2048], P('req', 'blk')
Inputs may be any that keep to these rules, and one draw needn't show every extreme that they name: In each group, block_map[g] holds each of 0 to 3 once, and the two halves of each slot hold blocks b and 3 - b, in either order. `decode_rank`: each group's row holds each of 0 to 7 once.
All inputs are finite; a program needn't handle non-finite values.
Results may differ from a plain program's by a relative error of at most 0.0098.
Values may be sent and summed in bfloat16 or wider, within the bound.
No kernel may reach another device: no remote copies, remote signals or barrier semaphores. Data moves between devices by JAX's collectives and lax.ppermute only.
A program may use at most 64 MiB of HBM per device.

v0:
```python
import math

import jax
import jax.numpy as jnp
import numpy as np
from jax import lax
from jax.experimental import pallas as pl
from jax.experimental.pallas import tpu as pltpu
from jax.sharding import PartitionSpec as P

QUERY_HEADS = 16
KEY_VALUE_HEADS = 8
HEAD_SIZE = 128
HEAD_DIVISIONS = 4
Q_DEV = 4
KV_DEV = 2
KV_WIDTH = KV_DEV * HEAD_SIZE

cap_value = 50.0
query_scale = 1.0 / 12.0
rope_base = 10000.0
VMEM_BYTES = 48 * 1024 * 1024

f32 = jnp.float32
bf16 = jnp.bfloat16
SMEM = pl.BlockSpec(memory_space=pltpu.SMEM)
VMEM = pl.BlockSpec(memory_space=pltpu.VMEM)
HBM = pl.BlockSpec(memory_space=pltpu.HBM)


def shifted(shard, axis, by):
    peers = lax.axis_size(axis)
    return lax.ppermute(shard, axis, [(i, (i + by) % peers) for i in range(peers)])


def crossed(shard, axis, by):
    peers = lax.axis_size(axis)
    return lax.ppermute(shard, axis, [(i, i ^ by) for i in range(peers)])


def rotary_tables(block_len, block_count):
    half = HEAD_SIZE // 2
    frequency = np.exp(
        np.float32(-math.log(rope_base)) * (2.0 * np.arange(half, dtype=np.float32)) / HEAD_SIZE
    ).astype(np.float64)

    def table(positions):
        angles = positions.astype(np.float64)[:, None] * frequency[None, :]
        cosine, sine = np.cos(angles), np.sin(angles)
        return np.stack(
            [np.concatenate([cosine, cosine], 1), np.concatenate([-sine, sine], 1)]
        ).astype(np.float32)

    return table(np.arange(block_len)), table(np.arange(block_count) * block_len)


def block_angles(row_table, block_table, block):
    row_cos, row_sin = row_table[0], row_table[1]
    blk_cos, blk_sin = block_table[0, pl.ds(block, 1)], block_table[1, pl.ds(block, 1)]
    return row_cos * blk_cos - row_sin * blk_sin, row_sin * blk_cos + row_cos * blk_sin


def turned(head, angles):
    x = head.astype(f32)
    return x * angles[0] + pltpu.roll(x, HEAD_SIZE // 2, 1) * angles[1]


def order_matrix(rank_of, slot, head_group, out_rows, rows, residues):
    row_ids = lax.broadcasted_iota(jnp.int32, (1, rows), 1)
    residue = row_ids % residues
    rank = jnp.zeros_like(row_ids)
    for r in range(residues):
        rank = jnp.where(residue == r, rank_of(r), rank)
    ahead = (rank - HEAD_DIVISIONS * slot + residues) % residues
    ahead = jnp.where(ahead < HEAD_DIVISIONS, ahead ^ head_group, ahead)
    index = ahead * (rows // residues) + row_ids // residues
    out_ids = lax.broadcasted_iota(jnp.int32, (out_rows, rows), 0)
    return jnp.where(out_ids == index, 1.0, 0.0).astype(bf16)


def dot(a, b):
    return jnp.dot(a, b, preferred_element_type=f32)


def dot_t(a, b):
    return lax.dot_general(a, b, (((1,), (1,)), ((), ())), preferred_element_type=f32)


def expo_of(scores):
    return jnp.exp2(cap_value * math.log2(math.e) * jnp.tanh(scores * (1.0 / cap_value)))


def columns(index, width=HEAD_SIZE):
    return slice(index * width, (index + 1) * width)


def call(body, out_shape, in_specs, name, scratch=(), out_specs=None, cost=1000):
    return pl.pallas_call(
        body,
        out_shape=out_shape,
        in_specs=in_specs,
        out_specs=jax.tree.map(lambda _: VMEM, out_shape) if out_specs is None else out_specs,
        scratch_shapes=scratch,
        compiler_params=pltpu.CompilerParams(vmem_limit_bytes=VMEM_BYTES),
        cost_estimate=pl.CostEstimate(flops=cost, bytes_accessed=1000, transcendentals=0),
        name=name,
    )


def in_hbm(arrays):
    return [pltpu.with_memory_space_constraint(x, pltpu.HBM) for x in arrays]


def rows_at(index, size):
    return pl.ds(pl.multiple_of(index * size, size), size)


def beside_ones(values):
    return jnp.concatenate([values, jnp.ones(values.shape, bf16)], axis=1)


class Facts:
    def __init__(self, ref, slots, residues, groups):
        self.ref, self.slots, self.residues, self.groups = ref, slots, residues, groups
        self.size = 2 * slots + residues + groups

    def block(self, slot, half):
        return self.ref[0, 2 * slot + half]

    def rank(self, residue):
        return self.ref[0, 2 * self.slots + residue]

    def owner(self, prompt):
        return self.ref[0, 2 * self.slots + self.residues + prompt]

    def store(self, map_ref, rank_ref, owner_ref):
        for slot in range(self.slots):
            for half in range(2):
                self.ref[0, 2 * slot + half] = map_ref[0, slot, half]
        for residue in range(self.residues):
            self.ref[0, 2 * self.slots + residue] = rank_ref[0, residue]
        for prompt in range(self.groups):
            self.ref[0, 2 * self.slots + self.residues + prompt] = owner_ref[prompt]

    def halves(self, slot):
        high = jnp.where(self.block(slot, 1) > self.block(slot, 0), 1, 0)
        return 1 - high, high


def slot_and_head_group():
    member = lax.axis_index("blk")
    return member // HEAD_DIVISIONS, member % HEAD_DIVISIONS


def prepare(queries, keys, values, table, decode_rank, owner, tables, own_length, near_length):
    rows, width = keys.shape
    block_len = rows // 2
    slots = table.shape[1]
    residues = decode_rank.shape[1]
    piece = rows // residues
    arrays = (keys, values, queries, *tables, table, decode_rank, owner)
    count = len(arrays)
    facts_of = lambda ref: Facts(ref, slots, residues, owner.shape[0])

    def body(own_ref, near_ref, *refs):
        inputs, refs = refs[:count], refs[count:]
        facts_ref, pair_ref, qr_ref, kr_ref, v_ref, select_ref, angle_ref = refs[:7]
        e_refs, refs = refs[7:11], refs[11:]
        k_ref, q_ref, row_ref, blk_ref, map_ref, rank_ref, owner_ref, sems = refs
        targets = (k_ref, v_ref, q_ref, row_ref, blk_ref, map_ref, rank_ref, owner_ref)
        copies = []
        for index in range(count):
            copies.append(pltpu.make_async_copy(inputs[index], targets[index], sems.at[index]))
            copies[-1].start()
        slot, head_group = slot_and_head_group()
        odd = lax.axis_index("req") % 2 == 1
        pair_ref[0] = jnp.where(odd, near_ref[0], own_ref[0])
        pair_ref[1] = jnp.where(odd, own_ref[0], near_ref[0])
        for copy in copies:
            copy.wait()
        facts_of(facts_ref).store(map_ref, rank_ref, owner_ref)
        for half in range(2):
            part = columns(half, block_len)
            angles = block_angles(row_ref, blk_ref, map_ref[0, slot, half])
            for head in range(KV_DEV):
                kr_ref[part, columns(head)] = turned(k_ref[part, columns(head)], angles).astype(bf16)
            for head in range(Q_DEV):
                qr_ref[part, columns(head)] = (
                    turned(q_ref[part, columns(head)], angles) * query_scale
                ).astype(bf16)
            for turn in range(1, slots):
                other = block_angles(row_ref, blk_ref, map_ref[0, (slot - turn + slots) % slots, half])
                angle_ref[turn - 1, half, 0] = other[0]
                angle_ref[turn - 1, half, 1] = other[1]
        select = order_matrix(
            lambda r: rank_ref[0, r], slot, head_group, rows // slots, rows, residues
        )
        select_ref[...] = select
        for kind, source in enumerate((kr_ref, v_ref)):
            chosen = dot(select, source[...]).astype(bf16)
            for m in range(HEAD_DIVISIONS):
                e_refs[m][columns(kind, piece)] = chosen[columns(m, piece)]

    shapes = [
        jax.ShapeDtypeStruct((1, facts_of(None).size), jnp.int32),
        jax.ShapeDtypeStruct((2,), jnp.int32),
        jax.ShapeDtypeStruct(queries.shape, bf16),
        jax.ShapeDtypeStruct(keys.shape, bf16),
        jax.ShapeDtypeStruct(values.shape, bf16),
        jax.ShapeDtypeStruct((rows // slots, rows), bf16),
        jax.ShapeDtypeStruct((slots - 1, 2, 2, block_len, HEAD_SIZE), f32),
    ]
    shapes += [jax.ShapeDtypeStruct((2 * piece, width), bf16) for _ in range(HEAD_DIVISIONS)]
    scratch = [pltpu.VMEM(x.shape, x.dtype) for x in (keys, queries, *tables)]
    scratch += [pltpu.SMEM(x.shape, x.dtype) for x in (table, decode_rank, owner)]
    scratch.append(pltpu.SemaphoreType.DMA((count,)))
    outs = call(
        body,
        shapes,
        [SMEM] * 2 + [HBM] * count,
        "prepare",
        scratch,
        out_specs=[SMEM] * 2 + [VMEM] * (len(shapes) - 2),
    )(own_length, near_length, *in_hbm(arrays))
    return outs[0], facts_of, outs[1], outs[2:5], outs[5:7], outs[7:]


def own_part(facts_row, facts_of, operands, lens):
    query_rot, key_rot, values = operands
    rows = query_rot.shape[0]
    block_len = rows // 2
    sizes = facts_of(None)
    slots, residues, groups = sizes.slots, sizes.residues, sizes.groups
    run = block_len // residues
    cache_rows = 2 * slots * run

    def body(facts_ref, here_ref, there_ref, qr_ref, kr_ref, v_ref, acc_ref, kept_ref, live_ref):
        facts = facts_of(facts_ref)
        slot = slot_and_head_group()[0]
        group = lax.axis_index("req")
        low, high = facts.halves(slot)
        low, high = rows_at(low, block_len), rows_at(high, block_len)
        row = lax.broadcasted_iota(jnp.int32, (block_len, block_len), 0)
        col = lax.broadcasted_iota(jnp.int32, (block_len, block_len), 1)
        for head in range(Q_DEV):
            key_head = columns(head * KV_DEV // Q_DEV)
            both = columns(head, 2 * HEAD_SIZE)

            def tile(q_part, k_part, diagonal):
                expo = expo_of(dot_t(qr_ref[q_part, columns(head)], kr_ref[k_part, key_head]))
                if diagonal:
                    expo = jnp.where(col <= row, expo, 0.0)
                return dot(expo.astype(bf16), beside_ones(v_ref[k_part, key_head]))

            acc_ref[low, both] = tile(low, low, True)
            acc_ref[high, both] = tile(high, high, True) + tile(high, low, False)

        col = lax.broadcasted_iota(jnp.int32, (1, cache_rows), 1)
        part, offset = col // run, col % run
        target = jnp.zeros_like(col)
        for turn in range(slots):
            for half in range(2):
                block = facts.block((slot - turn + slots) % slots, half)
                target = jnp.where(part == 2 * turn + half, block * run + offset, target)
        length = 0
        half_count = groups // 2
        for index in range(half_count):
            same = (group & half_count) | index
            length = length + jnp.where(facts.owner(same) == group, here_ref[index], 0)
            other = same ^ half_count
            length = length + jnp.where(facts.owner(other) == group, there_ref[index], 0)
        residue = 0
        for r in range(1, residues):
            residue = jnp.where(facts.rank(r) == lax.axis_index("blk"), r, residue)
        target = jnp.where(target * residues + residue < length, target, -1)
        row = lax.broadcasted_iota(jnp.int32, (cache_rows, cache_rows), 0)
        kept_ref[...] = jnp.where(row == target, 1.0, 0.0).astype(bf16)
        for half in range(2):
            offset = lax.broadcasted_iota(jnp.int32, (block_len, HEAD_SIZE), 0)
            at = facts.block(slot, half) * block_len + offset
            live_ref[columns(half, block_len)] = jnp.where(at < length, 1.0, 0.0)

    shapes = [
        jax.ShapeDtypeStruct((rows, 2 * Q_DEV * HEAD_SIZE), f32),
        jax.ShapeDtypeStruct((cache_rows, cache_rows), bf16),
        jax.ShapeDtypeStruct((rows, HEAD_SIZE), f32),
    ]
    return call(body, shapes, [SMEM] * 3 + [VMEM] * 3, "own_part")(facts_row, *lens, *operands)


def receive(key_in, value_in, select, angles):
    others = len(key_in)
    rows, width = key_in[0].shape
    block_len = rows // 2
    piece = select.shape[0] // HEAD_DIVISIONS

    def body(select_ref, angle_ref, *refs):
        k_refs, v_refs, refs = refs[:others], refs[others : 2 * others], refs[2 * others :]
        kr_refs, e_refs = refs[:others], refs[others:]
        for turn in range(others):
            for half in range(2):
                part = columns(half, block_len)
                there = angle_ref[turn, half, 0], angle_ref[turn, half, 1]
                for head in range(KV_DEV):
                    kr_refs[turn][part, columns(head)] = turned(
                        k_refs[turn][part, columns(head)], there
                    ).astype(bf16)
            for kind, source in enumerate((kr_refs[turn], v_refs[turn])):
                chosen = dot(select_ref[...], source[...]).astype(bf16)
                for m in range(HEAD_DIVISIONS):
                    e_refs[m][columns(kind * others + turn, piece)] = chosen[columns(m, piece)]

    shapes = [jax.ShapeDtypeStruct((rows, width), bf16) for _ in range(others)]
    shapes += [
        jax.ShapeDtypeStruct((2 * others * piece, width), bf16) for _ in range(HEAD_DIVISIONS)
    ]
    outs = call(body, shapes, [VMEM] * (2 + 2 * others), "receive")(
        select, angles, *key_in, *value_in
    )
    return outs[:others], outs[others:]


def attend(facts_row, facts_of, query_rot, acc, key_rot, value_in, live):
    rows = query_rot.shape[0]
    block_len = rows // 2
    others = len(key_rot)
    slots = facts_of(None).slots

    def body(facts_ref, q_ref, acc_ref, live_ref, *refs):
        k_refs, v_refs, out_ref = refs[:others], refs[others : 2 * others], refs[2 * others]
        facts = facts_of(facts_ref)
        slot = slot_and_head_group()[0]
        low, high = facts.halves(slot)
        low_rows, high_rows = rows_at(low, block_len), rows_at(high, block_len)
        for head in range(Q_DEV):
            key_head = columns(head * KV_DEV // Q_DEV)
            both = columns(head, 2 * HEAD_SIZE)
            low_sum, high_sum = acc_ref[low_rows, both], acc_ref[high_rows, both]
            for turn in range(1, slots):
                source = (slot - turn + slots) % slots
                source_low, source_high = facts.halves(source)
                outer = facts.block(slot, low) < facts.block(source, source_low)

                def tile(half, other):
                    queries = q_ref[rows_at(half, block_len), columns(head)]
                    there = rows_at(other, block_len)
                    expo = expo_of(dot_t(queries, k_refs[turn - 1][there, key_head]))
                    return dot(expo.astype(bf16), beside_ones(v_refs[turn - 1][there, key_head]))

                either = tile(jnp.where(outer, high, low), source_low)
                upper = tile(high, jnp.where(outer, source_high, source_low))
                low_sum = low_sum + jnp.where(outer, 0.0, either)
                high_sum = high_sum + upper + jnp.where(outer, either, 0.0)
            for part, total in ((low_rows, low_sum), (high_rows, high_sum)):
                scale = live_ref[part] / total[:, HEAD_SIZE:]
                out_ref[part, columns(head)] = (total[:, :HEAD_SIZE] * scale).astype(bf16)

    shape = jax.ShapeDtypeStruct(query_rot.shape, bf16)
    specs = [SMEM] + [VMEM] * (3 + 2 * others)
    return call(body, shape, specs, "attend", cost=10**10)(
        facts_row, query_rot, acc, live, *key_rot, *value_in
    )


def cache_part(early, late, kept):
    cache_rows = kept.shape[0]
    piece = early[0].shape[0] // 2
    width = early[0].shape[1]

    def body(kept_ref, *refs):
        f_refs, s_refs, out_ref = refs[:4], refs[4:8], refs[8]
        head_group = slot_and_head_group()[1]
        later = cache_rows - piece
        for m in range(HEAD_DIVISIONS):
            for kind in range(2):
                lines = jnp.concatenate(
                    [f_refs[m][columns(kind, piece)], s_refs[m][columns(kind, later)]], axis=0
                )
                column = ((head_group ^ m) + kind * HEAD_DIVISIONS) * width
                out_ref[:, pl.ds(pl.multiple_of(column, HEAD_SIZE), width)] = dot(
                    kept_ref[...], lines
                ).astype(bf16)

    shape = jax.ShapeDtypeStruct((cache_rows, 2 * HEAD_DIVISIONS * width), bf16)
    return call(body, shape, [VMEM] * 9, "cache_part")(kept, *early, *late)


def on_device(queries, keys, values, block_map, lengths, group_of_prompt, decode_rank):
    block_len = queries.shape[2] // 2
    slots = block_map.shape[1]
    q, k, v = queries[0, 0], keys[0, 0], values[0, 0]
    tables = rotary_tables(block_len, 2 * slots)

    def to_slots(part):
        return [shifted(part, "blk", HEAD_DIVISIONS * t) for t in range(1, slots)]

    def hand_on(pieces):
        return [pieces[0]] + [crossed(pieces[m], "blk", m) for m in range(1, HEAD_DIVISIONS)]

    key_in, value_in = to_slots(k), to_slots(v)
    facts_row, facts_of, block, operands, (select, angles), early = prepare(
        q,
        k,
        v,
        block_map,
        decode_rank,
        group_of_prompt,
        tables,
        lengths,
        crossed(lengths, "req", 1),
    )
    early = hand_on(early)
    span, groups = 2, lax.axis_size("req")
    while 2 * span < groups:
        other = crossed(block, "req", span)
        upper = (lax.axis_index("req") & span) > 0
        block = jnp.where(
            upper, jnp.concatenate([other, block]), jnp.concatenate([block, other])
        )
        span = 2 * span
    lens = (block, crossed(block, "req", span))
    acc, kept, live = own_part(facts_row, facts_of, operands, lens)
    key_rot, late = receive(key_in, value_in, select, angles)
    late = hand_on(late)
    attended = attend(facts_row, facts_of, operands[0], acc, key_rot, value_in, live)
    cache = cache_part(early, late, kept)
    return (attended[None, None], cache[None])


def solution(mesh):
    placed = (
        P("req", "blk", None, None),
        P("req", "blk", None, None),
        P("req", "blk", None, None),
        P("req", None, None),
        P("req"),
        P(),
        P("req", None),
    )
    return jax.shard_map(
        on_device,
        mesh=mesh,
        in_specs=placed,
        out_specs=(P("req", "blk", None, None), P("req", "blk", None)),
        check_vma=False,
    )
```

profile of v0, /device:TPU:0, one launch (start us, length us, event | category | flops | bytes accessed | tf_op | source)
XLA Modules:
  0.0 37.2 jit_solution(6923861758706278797)
XLA Ops:
  0.6 4.1 %collective-permute-start.2 = (bf16[512,256]{1,0:T(8,128)(2,1)}, bf16[512,256]{1,0:T(8,128)(2,1)S(1)}, u32[]{:S(2)}, u32[]{:S(2)}) collective-permute-start(bf16[512,256]{1,0:T(8,128)(2,1)} %bitcast.7), channel_id=1, source_target_pairs={{0,4},{1,5},{2,6},{3,7},{4,0},{5,1},{6,2},{7,3},{8,12},{9,13},{10,... | collective-permute-start | bytes 786440 | tf_op jit(solution)/shard_map/ppermute | solution.py:33
  4.7 0.1 collective-permute-start.3
  4.8 0.0 collective-permute-start
  5.5 0.7 %collective-permute-done.near_ref = s32[1]{0:T(128)} collective-permute-done((s32[1]{0:T(128)}, s32[1]{0:T(128)}, u32[]{:S(2)}, u32[]{:S(2)}) %collective-permute-start) | collective-permute-done | bytes 36 | tf_op jit(solution)/shard_map/ppermute | solution.py:38
  6.2 3.2 %prepare.1 = (s32[1,16]{1,0:T(1,128)S(1)}, s32[2]{0:T(128)S(1)}, bf16[512,512]{1,0:T(8,128)(2,1)S(1)}, bf16[512,256]{1,0:T(8,128)(2,1)S(1)}, bf16[512,256]{1,0:T...) custom-call(s32[1]{0:T(128)S(6)} %copy.11.own_ref, ...), custom_call_target="tpu_custom_call" | custom-call | flops 1000 | bytes 1000 | tf_op jit(solution)/shard_map/prepare/pallas_call | solution.py:217
  9.4 1.8 %collective-permute-start.4 = (bf16[128,256]{1,0:T(8,128)(2,1)S(1)}, bf16[128,256]{1,0:T(8,128)(2,1)S(1)}, u32[]{:S(2)}, u32[]{:S(2)}) collective-permute-start(bf16[128,256]{1,0:T(8,128)(2,1)S(1)} %get-tuple-element.33), channel_id=1, source_target_pairs={{0,1},{1,0},{2,3},{3,2},{4,5},{5,4},{6,7},{7,6},{8,9},{9,8},{10,11... | collective-permute-start | bytes 196616 | tf_op jit(solution)/shard_map/ppermute | solution.py:38
  11.3 1.5 %collective-permute-start.1 = (s32[2]{0:T(128)S(1)}, s32[2]{0:T(128)S(1)}, u32[]{:S(2)}, u32[]{:S(2)}) collective-permute-start(s32[2]{0:T(128)S(1)} %get-tuple-element.23.here_ref), channel_id=1, source_target_pairs={{0,16},{8,24},{16,0},{24,8},{1,17},{9,25},{17,1},{25,9},{2,18},{10... | collective-permute-start | bytes 32 | tf_op jit(solution)/shard_map/ppermute | solution.py:38
  12.8 1.6 %collective-permute-start.5 = (bf16[128,256]{1,0:T(8,128)(2,1)S(1)}, bf16[128,256]{1,0:T(8,128)(2,1)S(1)}, u32[]{:S(2)}, u32[]{:S(2)}) collective-permute-start(bf16[128,256]{1,0:T(8,128)(2,1)S(1)} %get-tuple-element.34), channel_id=1, source_target_pairs={{0,2},{1,3},{2,0},{3,1},{4,6},{5,7},{6,4},{7,5},{8,10},{9,11},{10,... | collective-permute-start | bytes 196616 | tf_op jit(solution)/shard_map/ppermute | solution.py:38
  14.4 0.5 %collective-permute-done.1.there_ref = s32[2]{0:T(128)S(1)} collective-permute-done((s32[2]{0:T(128)S(1)}, s32[2]{0:T(128)S(1)}, u32[]{:S(2)}, u32[]{:S(2)}) %collective-permute-start.1) | collective-permute-done | bytes 40 | tf_op jit(solution)/shard_map/ppermute | solution.py:38
  14.8 1.5 %collective-permute-start.6 = (bf16[128,256]{1,0:T(8,128)(2,1)S(1)}, bf16[128,256]{1,0:T(8,128)(2,1)S(1)}, u32[]{:S(2)}, u32[]{:S(2)}) collective-permute-start(bf16[128,256]{1,0:T(8,128)(2,1)S(1)} %get-tuple-element.35), channel_id=1, source_target_pairs={{0,3},{1,2},{2,1},{3,0},{4,7},{5,6},{6,5},{7,4},{8,11},{9,10},{10,... | collective-permute-start | bytes 196616 | tf_op jit(solution)/shard_map/ppermute | solution.py:38
  16.3 2.1 %own_part.1 = (f32[512,1024]{1,0:T(8,128)S(1)}, bf16[128,128]{1,0:T(8,128)(2,1)S(1)}, f32[512,128]{1,0:T(8,128)S(1)}) custom-call(s32[1,16]{1,0:T(1,128)S(1)} %get-tuple-element.21.facts_ref, s32[2]{0:T(128)S(1)} %get-tuple-element.23.here_ref, s32[2]{0:T(128)S(1)} %collective-permute-done.1.there_ref, bf16[512,512]{1,0:T(8,128)(2,1)S(1)} %get-tuple-element.22.qr_ref.q_ref, ...), custom_call_target="tpu_custom_call" | custom-call | flops 1000 | bytes 1000 | tf_op jit(solution)/shard_map/own_part/pallas_call | solution.py:288
  18.5 5.0 %collective-permute-done.2.refs_0_ = bf16[512,256]{1,0:T(8,128)(2,1)S(1)} collective-permute-done((bf16[512,256]{1,0:T(8,128)(2,1)}, bf16[512,256]{1,0:T(8,128)(2,1)S(1)}, u32[]{:S(2)}, u32[]{:S(2)}) %collective-permute-start.2) | collective-permute-done | bytes 262176 | tf_op jit(solution)/shard_map/ppermute | solution.py:33
  23.4 4.8 %collective-permute-done.3.refs_1_ = bf16[512,256]{1,0:T(8,128)(2,1)S(1)} collective-permute-done((bf16[512,256]{1,0:T(8,128)(2,1)}, bf16[512,256]{1,0:T(8,128)(2,1)S(1)}, u32[]{:S(2)}, u32[]{:S(2)}) %collective-permute-start.3) | collective-permute-done | bytes 262176 | tf_op jit(solution)/shard_map/ppermute | solution.py:33
  28.2 0.4 %receive.1 = (bf16[512,256]{1,0:T(8,128)(2,1)S(1)}, bf16[128,256]{1,0:T(8,128)(2,1)S(1)}, bf16[128,256]{1,0:T(8,128)(2,1)S(1)}, bf16[128,256]{1,0:T(8,128)(2,1)S(1)}, bf16[128,256]{1,0:T(8,128)(2,1)S(1)}) custom-call(bf16[256,512]{1,0:T(8,128)(2,1)S(1)} %get-tuple-element.28.select_ref, f32[1,2,2,256,128]{4,3,2,1,0:T(8,128)S(1)} %get-tuple-element.29.angle_ref, ...), custom_call_target="tpu_custom_call" | custom-call | flops 1000 | bytes 1000 | tf_op jit(solution)/shard_map/receive/pallas_call | solution.py:317
  28.6 1.6 %collective-permute-start.7 = (bf16[128,256]{1,0:T(8,128)(2,1)S(1)}, bf16[128,256]{1,0:T(8,128)(2,1)S(1)}, u32[]{:S(2)}, u32[]{:S(2)}) collective-permute-start(bf16[128,256]{1,0:T(8,128)(2,1)S(1)} %get-tuple-element.37), channel_id=1, source_target_pairs={{0,1},{1,0},{2,3},{3,2},{4,5},{5,4},{6,7},{7,6},{8,9},{9,8},{10,11... | collective-permute-start | bytes 196616 | tf_op jit(solution)/shard_map/ppermute | solution.py:38
  30.3 0.7 %collective-permute-start.8 = (bf16[128,256]{1,0:T(8,128)(2,1)S(1)}, bf16[128,256]{1,0:T(8,128)(2,1)S(1)}, u32[]{:S(2)}, u32[]{:S(2)}) collective-permute-start(bf16[128,256]{1,0:T(8,128)(2,1)S(1)} %get-tuple-element.38), channel_id=1, source_target_pairs={{0,2},{1,3},{2,0},{3,1},{4,6},{5,7},{6,4},{7,5},{8,10},{9,11},{10,... | collective-permute-start | bytes 196616 | tf_op jit(solution)/shard_map/ppermute | solution.py:38
  31.0 0.0 collective-permute-done.4.refs_1_
  31.0 1.2 %collective-permute-start.9 = (bf16[128,256]{1,0:T(8,128)(2,1)S(1)}, bf16[128,256]{1,0:T(8,128)(2,1)S(1)}, u32[]{:S(2)}, u32[]{:S(2)}) collective-permute-start(bf16[128,256]{1,0:T(8,128)(2,1)S(1)} %get-tuple-element.39), channel_id=1, source_target_pairs={{0,3},{1,2},{2,1},{3,0},{4,7},{5,6},{6,5},{7,4},{8,11},{9,10},{10,... | collective-permute-start | bytes 196616 | tf_op jit(solution)/shard_map/ppermute | solution.py:38
  32.2 2.4 %attend.1 = bf16[512,512]{1,0:T(8,128)(2,1)} custom-call(s32[1,16]{1,0:T(1,128)S(1)} %get-tuple-element.21.facts_ref, bf16[512,512]{1,0:T(8,128)(2,1)S(1)} %get-tuple-element.22.qr_ref.q_ref, f32[512,1024]{1,0:T(8,128)S(1)} %get-tuple-element.26.acc_ref, f32[512,128]{1,0:T(8,128)S(1)} %get-tuple-element.27.live_ref, ...), custom_call_target="tpu_custom_call" | custom-call | flops 10000000000 | bytes 1000 | tf_op jit(solution)/shard_map/attend/pallas_call | solution.py:360
  34.6 0.0 collective-permute-done.5.refs_2_
  34.6 0.0 collective-permute-done.6.refs_3_
  34.6 0.0 collective-permute-done.7.refs_5_
  34.6 0.0 collective-permute-done.8.refs_6_
  34.6 1.6 %collective-permute-done.9.refs_7_ = bf16[128,256]{1,0:T(8,128)(2,1)S(1)} collective-permute-done((bf16[128,256]{1,0:T(8,128)(2,1)S(1)}, bf16[128,256]{1,0:T(8,128)(2,1)S(1)}, u32[]{:S(2)}, u32[]{:S(2)}) %collective-permute-start.9) | collective-permute-done | bytes 65568 | tf_op jit(solution)/shard_map/ppermute | solution.py:38
  36.1 1.1 %cache_part.1 = bf16[128,2048]{1,0:T(8,128)(2,1)} custom-call(bf16[128,128]{1,0:T(8,128)(2,1)S(1)} %get-tuple-element.31.kept_ref, bf16[128,256]{1,0:T(8,128)(2,1)S(1)} %get-tuple-element.32.refs_0_, bf16[128,256]{1,0:T(8,128)(2,1)S(1)} %collective-permute-done.4.refs_1_, bf16[128,256]{1,0:T(8,128)(2,1)S(1)} %collective-permute-done.5.refs_2_, ...), custom_call_target="tpu_custom_call" | custom-call | flops 1000 | bytes 1000 | tf_op jit(solution)/shard_map/cache_part/pallas_call | solution.py:385
Async XLA Ops:
  0.6 22.8 %collective-permute-start.2 = (bf16[512,256]{1,0:T(8,128)(2,1)}, bf16[512,256]{1,0:T(8,128)(2,1)S(1)}, u32[]{:S(2)}, u32[]{:S(2)}) collective-permute-start(bf16[512,256]{1,0:T(8,128)(2,1)} %bitcast.7), channel_id=1, source_target_pairs={{0,4},{1,5},{2,6},{3,7},{4,0},{5,1},{6,2},{7,3},{8,12},{9,13},{10,... | collective-permute-start | bytes 786440 | tf_op jit(solution)/shard_map/ppermute | solution.py:33
  4.7 23.5 %collective-permute-start.3 = (bf16[512,256]{1,0:T(8,128)(2,1)}, bf16[512,256]{1,0:T(8,128)(2,1)S(1)}, u32[]{:S(2)}, u32[]{:S(2)}) collective-permute-start(bf16[512,256]{1,0:T(8,128)(2,1)} %bitcast.9), channel_id=1, source_target_pairs={{0,4},{1,5},{2,6},{3,7},{4,0},{5,1},{6,2},{7,3},{8,12},{9,13},{10,... | collective-permute-start | bytes 786440 | tf_op jit(solution)/shard_map/ppermute | solution.py:33
  4.8 1.4 %collective-permute-start = (s32[1]{0:T(128)}, s32[1]{0:T(128)}, u32[]{:S(2)}, u32[]{:S(2)}) collective-permute-start(s32[1]{0:T(128)} %param.13), channel_id=1, source_target_pairs={{0,8},{8,0},{16,24},{24,16},{1,9},{9,1},{17,25},{25,17},{2,10},{10... | collective-permute-start | bytes 20 | tf_op jit(solution)/shard_map/ppermute | solution.py:38
  9.4 21.5 %collective-permute-start.4 = (bf16[128,256]{1,0:T(8,128)(2,1)S(1)}, bf16[128,256]{1,0:T(8,128)(2,1)S(1)}, u32[]{:S(2)}, u32[]{:S(2)}) collective-permute-start(bf16[128,256]{1,0:T(8,128)(2,1)S(1)} %get-tuple-element.33), channel_id=1, source_target_pairs={{0,1},{1,0},{2,3},{3,2},{4,5},{5,4},{6,7},{7,6},{8,9},{9,8},{10,11... | collective-permute-start | bytes 196616 | tf_op jit(solution)/shard_map/ppermute | solution.py:38
  11.3 3.5 %collective-permute-start.1 = (s32[2]{0:T(128)S(1)}, s32[2]{0:T(128)S(1)}, u32[]{:S(2)}, u32[]{:S(2)}) collective-permute-start(s32[2]{0:T(128)S(1)} %get-tuple-element.23.here_ref), channel_id=1, source_target_pairs={{0,16},{8,24},{16,0},{24,8},{1,17},{9,25},{17,1},{25,9},{2,18},{10... | collective-permute-start | bytes 32 | tf_op jit(solution)/shard_map/ppermute | solution.py:38
  12.8 21.8 %collective-permute-start.5 = (bf16[128,256]{1,0:T(8,128)(2,1)S(1)}, bf16[128,256]{1,0:T(8,128)(2,1)S(1)}, u32[]{:S(2)}, u32[]{:S(2)}) collective-permute-start(bf16[128,256]{1,0:T(8,128)(2,1)S(1)} %get-tuple-element.34), channel_id=1, source_target_pairs={{0,2},{1,3},{2,0},{3,1},{4,6},{5,7},{6,4},{7,5},{8,10},{9,11},{10,... | collective-permute-start | bytes 196616 | tf_op jit(solution)/shard_map/ppermute | solution.py:38
  14.8 19.7 %collective-permute-start.6 = (bf16[128,256]{1,0:T(8,128)(2,1)S(1)}, bf16[128,256]{1,0:T(8,128)(2,1)S(1)}, u32[]{:S(2)}, u32[]{:S(2)}) collective-permute-start(bf16[128,256]{1,0:T(8,128)(2,1)S(1)} %get-tuple-element.35), channel_id=1, source_target_pairs={{0,3},{1,2},{2,1},{3,0},{4,7},{5,6},{6,5},{7,4},{8,11},{9,10},{10,... | collective-permute-start | bytes 196616 | tf_op jit(solution)/shard_map/ppermute | solution.py:38
  28.6 5.9 %collective-permute-start.7 = (bf16[128,256]{1,0:T(8,128)(2,1)S(1)}, bf16[128,256]{1,0:T(8,128)(2,1)S(1)}, u32[]{:S(2)}, u32[]{:S(2)}) collective-permute-start(bf16[128,256]{1,0:T(8,128)(2,1)S(1)} %get-tuple-element.37), channel_id=1, source_target_pairs={{0,1},{1,0},{2,3},{3,2},{4,5},{5,4},{6,7},{7,6},{8,9},{9,8},{10,11... | collective-permute-start | bytes 196616 | tf_op jit(solution)/shard_map/ppermute | solution.py:38
  30.3 4.3 %collective-permute-start.8 = (bf16[128,256]{1,0:T(8,128)(2,1)S(1)}, bf16[128,256]{1,0:T(8,128)(2,1)S(1)}, u32[]{:S(2)}, u32[]{:S(2)}) collective-permute-start(bf16[128,256]{1,0:T(8,128)(2,1)S(1)} %get-tuple-element.38), channel_id=1, source_target_pairs={{0,2},{1,3},{2,0},{3,1},{4,6},{5,7},{6,4},{7,5},{8,10},{9,11},{10,... | collective-permute-start | bytes 196616 | tf_op jit(solution)/shard_map/ppermute | solution.py:38
  31.0 5.2 %collective-permute-start.9 = (bf16[128,256]{1,0:T(8,128)(2,1)S(1)}, bf16[128,256]{1,0:T(8,128)(2,1)S(1)}, u32[]{:S(2)}, u32[]{:S(2)}) collective-permute-start(bf16[128,256]{1,0:T(8,128)(2,1)S(1)} %get-tuple-element.39), channel_id=1, source_target_pairs={{0,3},{1,2},{2,1},{3,0},{4,7},{5,6},{6,5},{7,4},{8,11},{9,10},{10,... | collective-permute-start | bytes 196616 | tf_op jit(solution)/shard_map/ppermute | solution.py:38
where the time goes:
time: 37.4 us; the launch traced here: 37.2 us
  starting transfers between devices  14.2 us (38%)
  waiting for transfers between devices  12.5 us (33%)
  Pallas kernels  9.22 us (25%)
  between operations  1.33 us (4%)
    ppermute x8, starting transfers between devices, crossed(): return lax.ppermute(shard, axis, [(i, i ^ by) for i in range(peers)])  9.99 us
    ppermute x2, waiting for transfers between devices, shifted(): lax.ppermute(shard, axis, [(i, (i + by) % peers) for i in range(peers)])  9.74 us
    ppermute x2, starting transfers between devices, shifted(): lax.ppermute(shard, axis, [(i, (i + by) % peers) for i in range(peers)])  4.18 us
    pallas_call x1, Pallas kernels, prepare(): call(body, shapes, [SMEM] * 2 + [HBM] * count, 'prepare', scratch, out_sp...  3.23 us
    ppermute x8, waiting for transfers between devices, crossed(): return lax.ppermute(shard, axis, [(i, i ^ by) for i in range(peers)])  2.79 us
    pallas_call x1, Pallas kernels, attend(): call(body, shape, specs, 'attend', cost=10 ** 10)  2.37 us
    pallas_call x1, Pallas kernels, own_part(): call(body, shapes, [SMEM] * 3 + [VMEM] * 3, 'own_part')  2.11 us
    pallas_call x1, Pallas kernels, cache_part(): return call(body, shape, [VMEM] * 9, 'cache_part')(kept, *early, *late)  1.09 us
  transfers between devices with their start and end apart: 10, of which 5 were waited for; matrix products, arithmetic and copies ran while one was open for 0% of the time, Pallas kernels for 22%

commit v1 on v0

--- a/solution.py
+++ b/solution.py
@@ -18,6 +18,7 @@
 
 cap_value = 50.0
 query_scale = 1.0 / 12.0
+HAND_ORDER = (0, 2, 3, 1)
 rope_base = 10000.0
 VMEM_BYTES = 48 * 1024 * 1024
 
@@ -164,9 +165,9 @@
 
     def body(own_ref, near_ref, *refs):
         inputs, refs = refs[:count], refs[count:]
-        facts_ref, pair_ref, qr_ref, kr_ref, v_ref, select_ref, angle_ref = refs[:7]
-        e_refs, refs = refs[7:11], refs[11:]
-        k_ref, q_ref, row_ref, blk_ref, map_ref, rank_ref, owner_ref, sems = refs
+        facts_ref, pair_ref, q_ref, kr_ref, v_ref, row_ref, blk_ref, select_ref = refs[:8]
+        e_refs, refs = refs[8:12], refs[12:]
+        k_ref, map_ref, rank_ref, owner_ref, sems = refs
         targets = (k_ref, v_ref, q_ref, row_ref, blk_ref, map_ref, rank_ref, owner_ref)
         copies = []
         for index in range(count):
@@ -176,30 +177,24 @@
         odd = lax.axis_index("req") % 2 == 1
         pair_ref[0] = jnp.where(odd, near_ref[0], own_ref[0])
         pair_ref[1] = jnp.where(odd, own_ref[0], near_ref[0])
-        for copy in copies:
-            copy.wait()
+        for index in (0, 3, 4, 5, 6, 7):
+            copies[index].wait()
         facts_of(facts_ref).store(map_ref, rank_ref, owner_ref)
         for half in range(2):
             part = columns(half, block_len)
             angles = block_angles(row_ref, blk_ref, map_ref[0, slot, half])
             for head in range(KV_DEV):
                 kr_ref[part, columns(head)] = turned(k_ref[part, columns(head)], angles).astype(bf16)
-            for head in range(Q_DEV):
-                qr_ref[part, columns(head)] = (
-                    turned(q_ref[part, columns(head)], angles) * query_scale
-                ).astype(bf16)
-            for turn in range(1, slots):
-                other = block_angles(row_ref, blk_ref, map_ref[0, (slot - turn + slots) % slots, half])
-                angle_ref[turn - 1, half, 0] = other[0]
-                angle_ref[turn - 1, half, 1] = other[1]
         select = order_matrix(
             lambda r: rank_ref[0, r], slot, head_group, rows // slots, rows, residues
         )
         select_ref[...] = select
+        copies[1].wait()
         for kind, source in enumerate((kr_ref, v_ref)):
             chosen = dot(select, source[...]).astype(bf16)
             for m in range(HEAD_DIVISIONS):
                 e_refs[m][columns(kind, piece)] = chosen[columns(m, piece)]
+        copies[2].wait()
 
     shapes = [
         jax.ShapeDtypeStruct((1, facts_of(None).size), jnp.int32),
@@ -207,11 +202,12 @@
         jax.ShapeDtypeStruct(queries.shape, bf16),
         jax.ShapeDtypeStruct(keys.shape, bf16),
         jax.ShapeDtypeStruct(values.shape, bf16),
+        jax.ShapeDtypeStruct(tables[0].shape, f32),
+        jax.ShapeDtypeStruct(tables[1].shape, f32),
         jax.ShapeDtypeStruct((rows // slots, rows), bf16),
-        jax.ShapeDtypeStruct((slots - 1, 2, 2, block_len, HEAD_SIZE), f32),
     ]
     shapes += [jax.ShapeDtypeStruct((2 * piece, width), bf16) for _ in range(HEAD_DIVISIONS)]
-    scratch = [pltpu.VMEM(x.shape, x.dtype) for x in (keys, queries, *tables)]
+    scratch = [pltpu.VMEM(keys.shape, keys.dtype)]
     scratch += [pltpu.SMEM(x.shape, x.dtype) for x in (table, decode_rank, owner)]
     scratch.append(pltpu.SemaphoreType.DMA((count,)))
     outs = call(
@@ -222,22 +218,35 @@
         scratch,
         out_specs=[SMEM] * 2 + [VMEM] * (len(shapes) - 2),
     )(own_length, near_length, *in_hbm(arrays))
-    return outs[0], facts_of, outs[1], outs[2:5], outs[5:7], outs[7:]
-
-
-def own_part(facts_row, facts_of, operands, lens):
-    query_rot, key_rot, values = operands
-    rows = query_rot.shape[0]
+    return outs[0], facts_of, outs[1], outs[2:5], outs[5:7], outs[7], outs[8:]
+
+
+def own_part(facts_row, facts_of, operands, tables, lens):
+    queries = operands[0]
+    rows = queries.shape[0]
     block_len = rows // 2
     sizes = facts_of(None)
     slots, residues, groups = sizes.slots, sizes.residues, sizes.groups
     run = block_len // residues
     cache_rows = 2 * slots * run
 
-    def body(facts_ref, here_ref, there_ref, qr_ref, kr_ref, v_ref, acc_ref, kept_ref, live_ref):
+    def body(facts_ref, here_ref, there_ref, q_ref, kr_ref, v_ref, row_ref, blk_ref, *refs):
+        qr_ref, acc_ref, kept_ref, live_ref, angle_ref = refs
         facts = facts_of(facts_ref)
         slot = slot_and_head_group()[0]
         group = lax.axis_index("req")
+        for half in range(2):
+            part = columns(half, block_len)
+            angles = block_angles(row_ref, blk_ref, facts.block(slot, half))
+            for head in range(Q_DEV):
+                qr_ref[part, columns(head)] = (
+                    turned(q_ref[part, columns(head)], angles) * query_scale
+                ).astype(bf16)
+            for turn in range(1, slots):
+                block = facts.block((slot - turn + slots) % slots, half)
+                other = block_angles(row_ref, blk_ref, block)
+                angle_ref[turn - 1, half, 0] = other[0]
+                angle_ref[turn - 1, half, 1] = other[1]
         low, high = facts.halves(slot)
         low, high = rows_at(low, block_len), rows_at(high, block_len)
         row = lax.broadcasted_iota(jnp.int32, (block_len, block_len), 0)
@@ -281,53 +290,92 @@
             live_ref[columns(half, block_len)] = jnp.where(at < length, 1.0, 0.0)
 
     shapes = [
+        jax.ShapeDtypeStruct(queries.shape, bf16),
         jax.ShapeDtypeStruct((rows, 2 * Q_DEV * HEAD_SIZE), f32),
         jax.ShapeDtypeStruct((cache_rows, cache_rows), bf16),
         jax.ShapeDtypeStruct((rows, HEAD_SIZE), f32),
+        jax.ShapeDtypeStruct((slots - 1, 2, 2, block_len, HEAD_SIZE), f32),
     ]
-    return call(body, shapes, [SMEM] * 3 + [VMEM] * 3, "own_part")(facts_row, *lens, *operands)
-
-
-def receive(key_in, value_in, select, angles):
+    return call(body, shapes, [SMEM] * 3 + [VMEM] * 5, "own_part")(
+        facts_row, *lens, *operands, *tables
+    )
+
+
+def tiles_of(facts, slot, source):
+    low, high = facts.halves(slot)
+    source_low, source_high = facts.halves(source)
+    outer = facts.block(slot, low) < facts.block(source, source_low)
+    first = (jnp.where(outer, high, low), source_low)
+    second = (high, jnp.where(outer, source_high, source_low))
+    return outer, first, second
+
+
+def receive_keys(facts_row, facts_of, key_in, query_rot, select, angles):
     others = len(key_in)
     rows, width = key_in[0].shape
     block_len = rows // 2
-    piece = select.shape[0] // HEAD_DIVISIONS
-
-    def body(select_ref, angle_ref, *refs):
-        k_refs, v_refs, refs = refs[:others], refs[others : 2 * others], refs[2 * others :]
-        kr_refs, e_refs = refs[:others], refs[others:]
-        for turn in range(others):
+    slots = facts_of(None).slots
+
+    def body(facts_ref, q_ref, select_ref, angle_ref, *refs):
+        k_refs, refs = refs[:others], refs[others:]
+        w_refs, chosen_ref, kr_ref = refs[:others], refs[others], refs[others + 1]
+        facts = facts_of(facts_ref)
+        slot = slot_and_head_group()[0]
+        for turn in range(1, slots):
             for half in range(2):
                 part = columns(half, block_len)
-                there = angle_ref[turn, half, 0], angle_ref[turn, half, 1]
+                there = angle_ref[turn - 1, half, 0], angle_ref[turn - 1, half, 1]
                 for head in range(KV_DEV):
-                    kr_refs[turn][part, columns(head)] = turned(
-                        k_refs[turn][part, columns(head)], there
+                    kr_ref[part, columns(head)] = turned(
+                        k_refs[turn - 1][part, columns(head)], there
                     ).astype(bf16)
-            for kind, source in enumerate((kr_refs[turn], v_refs[turn])):
-                chosen = dot(select_ref[...], source[...]).astype(bf16)
-                for m in range(HEAD_DIVISIONS):
-                    e_refs[m][columns(kind * others + turn, piece)] = chosen[columns(m, piece)]
-
-    shapes = [jax.ShapeDtypeStruct((rows, width), bf16) for _ in range(others)]
-    shapes += [
+            chosen_ref[turn - 1] = dot(select_ref[...], kr_ref[...]).astype(bf16)
+            _, *tiles = tiles_of(facts, slot, (slot - turn + slots) % slots)
+            for index, (half, other) in enumerate(tiles):
+                for head in range(Q_DEV):
+                    key_head = columns(head * KV_DEV // Q_DEV)
+                    queries = q_ref[rows_at(half, block_len), columns(head)]
+                    expo = expo_of(dot_t(queries, kr_ref[rows_at(other, block_len), key_head]))
+                    w_refs[turn - 1][index, head] = expo.astype(bf16)
+
+    shapes = [
+        jax.ShapeDtypeStruct((2, Q_DEV, block_len, block_len), bf16) for _ in range(others)
+    ]
+    shapes.append(jax.ShapeDtypeStruct((others, select.shape[0], width), bf16))
+    scratch = [pltpu.VMEM((rows, width), bf16)]
+    outs = call(body, shapes, [SMEM] + [VMEM] * (3 + others), "receive_keys", scratch)(
+        facts_row, query_rot, select, angles, *key_in
+    )
+    return outs[:others], outs[others]
+
+
+def receive_values(value_in, select, key_chosen):
+    others = len(value_in)
+    rows, width = value_in[0].shape
+    piece = select.shape[0] // HEAD_DIVISIONS
+
+    def body(select_ref, key_ref, *refs):
+        v_refs, e_refs = refs[:others], refs[others:]
+        for turn in range(others):
+            chosen = dot(select_ref[...], v_refs[turn][...]).astype(bf16)
+            for m in range(HEAD_DIVISIONS):
+                e_refs[m][columns(turn, piece)] = key_ref[turn, columns(m, piece)]
+                e_refs[m][columns(others + turn, piece)] = chosen[columns(m, piece)]
+
+    shapes = [
         jax.ShapeDtypeStruct((2 * others * piece, width), bf16) for _ in range(HEAD_DIVISIONS)
     ]
-    outs = call(body, shapes, [VMEM] * (2 + 2 * others), "receive")(
-        select, angles, *key_in, *value_in
-    )
-    return outs[:others], outs[others:]
-
-
-def attend(facts_row, facts_of, query_rot, acc, key_rot, value_in, live):
-    rows = query_rot.shape[0]
+    return call(body, shapes, [VMEM] * (2 + others), "receive_values")(select, key_chosen, *value_in)
+
+
+def attend(facts_row, facts_of, weights, acc, value_in, live):
+    rows = live.shape[0]
     block_len = rows // 2
-    others = len(key_rot)
+    others = len(weights)
     slots = facts_of(None).slots
 
-    def body(facts_ref, q_ref, acc_ref, live_ref, *refs):
-        k_refs, v_refs, out_ref = refs[:others], refs[others : 2 * others], refs[2 * others]
+    def body(facts_ref, acc_ref, live_ref, *refs):
+        w_refs, v_refs, out_ref = refs[:others], refs[others : 2 * others], refs[2 * others]
         facts = facts_of(facts_ref)
         slot = slot_and_head_group()[0]
         low, high = facts.halves(slot)
@@ -337,28 +385,24 @@
             both = columns(head, 2 * HEAD_SIZE)
             low_sum, high_sum = acc_ref[low_rows, both], acc_ref[high_rows, both]
             for turn in range(1, slots):
-                source = (slot - turn + slots) % slots
-                source_low, source_high = facts.halves(source)
-                outer = facts.block(slot, low) < facts.block(source, source_low)
-
-                def tile(half, other):
-                    queries = q_ref[rows_at(half, block_len), columns(head)]
-                    there = rows_at(other, block_len)
-                    expo = expo_of(dot_t(queries, k_refs[turn - 1][there, key_head]))
-                    return dot(expo.astype(bf16), beside_ones(v_refs[turn - 1][there, key_head]))
-
-                either = tile(jnp.where(outer, high, low), source_low)
-                upper = tile(high, jnp.where(outer, source_high, source_low))
+                outer, *tiles = tiles_of(facts, slot, (slot - turn + slots) % slots)
+                either, upper = [
+                    dot(
+                        w_refs[turn - 1][index, head],
+                        beside_ones(v_refs[turn - 1][rows_at(other, block_len), key_head]),
+                    )
+                    for index, (_, other) in enumerate(tiles)
+                ]
                 low_sum = low_sum + jnp.where(outer, 0.0, either)
                 high_sum = high_sum + upper + jnp.where(outer, either, 0.0)
             for part, total in ((low_rows, low_sum), (high_rows, high_sum)):
                 scale = live_ref[part] / total[:, HEAD_SIZE:]
                 out_ref[part, columns(head)] = (total[:, :HEAD_SIZE] * scale).astype(bf16)
 
-    shape = jax.ShapeDtypeStruct(query_rot.shape, bf16)
-    specs = [SMEM] + [VMEM] * (3 + 2 * others)
+    shape = jax.ShapeDtypeStruct((rows, Q_DEV * HEAD_SIZE), bf16)
+    specs = [SMEM] + [VMEM] * (2 + 2 * others)
     return call(body, shape, specs, "attend", cost=10**10)(
-        facts_row, query_rot, acc, live, *key_rot, *value_in
+        facts_row, acc, live, *weights, *value_in
     )
 
 
@@ -371,10 +415,10 @@
         f_refs, s_refs, out_ref = refs[:4], refs[4:8], refs[8]
         head_group = slot_and_head_group()[1]
         later = cache_rows - piece
-        for m in range(HEAD_DIVISIONS):
+        for index, m in enumerate(HAND_ORDER):
             for kind in range(2):
                 lines = jnp.concatenate(
-                    [f_refs[m][columns(kind, piece)], s_refs[m][columns(kind, later)]], axis=0
+                    [f_refs[index][columns(kind, piece)], s_refs[index][columns(kind, later)]], axis=0
                 )
                 column = ((head_group ^ m) + kind * HEAD_DIVISIONS) * width
                 out_ref[:, pl.ds(pl.multiple_of(column, HEAD_SIZE), width)] = dot(
@@ -395,10 +439,10 @@
         return [shifted(part, "blk", HEAD_DIVISIONS * t) for t in range(1, slots)]
 
     def hand_on(pieces):
-        return [pieces[0]] + [crossed(pieces[m], "blk", m) for m in range(1, HEAD_DIVISIONS)]
-
-    key_in, value_in = to_slots(k), to_slots(v)
-    facts_row, facts_of, block, operands, (select, angles), early = prepare(
+        return [pieces[0]] + [crossed(pieces[m], "blk", m) for m in HAND_ORDER[1:]]
+
+    key_in = to_slots(k)
+    facts_row, facts_of, block, operands, tables, select, early = prepare(
         q,
         k,
         v,
@@ -409,6 +453,7 @@
         lengths,
         crossed(lengths, "req", 1),
     )
+    value_in = to_slots(operands[2])
     early = hand_on(early)
     span, groups = 2, lax.axis_size("req")
     while 2 * span < groups:
@@ -419,10 +464,10 @@
         )
         span = 2 * span
     lens = (block, crossed(block, "req", span))
-    acc, kept, live = own_part(facts_row, facts_of, operands, lens)
-    key_rot, late = receive(key_in, value_in, select, angles)
-    late = hand_on(late)
-    attended = attend(facts_row, facts_of, operands[0], acc, key_rot, value_in, live)
+    query_rot, acc, kept, live, angles = own_part(facts_row, facts_of, operands, tables, lens)
+    weights, chosen = receive_keys(facts_row, facts_of, key_in, query_rot, select, angles)
+    late = hand_on(receive_values(value_in, select, chosen))
+    attended = attend(facts_row, facts_of, weights, acc, value_in, live)
     cache = cache_part(early, late, kept)
     return (attended[None, None], cache[None])
 

time: 37.4 us -> 37.6 us (level)
  waiting for transfers between devices: 12.5 us -> 11.5 us
  Pallas kernels: 9.22 us -> 10.2 us
    pallas_call x2 -> x3, Pallas kernels: 2.53 us -> 4.04 us  [the longest x1 2.36 us: own_part(): call(body, shapes, [SMEM] * 3 + [VMEM] * 5, 'own_part')]
    ppermute x2, waiting for transfers between devices: 9.74 us -> 8.95 us  [shifted(): lax.ppermute(shard, axis, [(i, (i + by) % peers) for i in range(peers)])]
    pallas_call x1, Pallas kernels: 2.37 us -> 1.9 us  [attend(): call(body, shape, specs, 'attend', cost=10 ** 10)]
  transfers between devices with their start and end apart: 10 -> 10, of which waited for: 5 -> 5; matrix products, arithmetic and copies ran while one was open for 0% -> 0% of each run, Pallas kernels for 22% -> 24%
where the time goes in v1:
time: 37.6 us; the launch traced here: 37.5 us
  starting transfers between devices  14.4 us (38%)
  waiting for transfers between devices  11.5 us (31%)
  Pallas kernels  10.2 us (27%)
  between operations  1.33 us (4%)
    ppermute x8, starting transfers between devices, crossed(): return lax.ppermute(shard, axis, [(i, i ^ by) for i in range(peers)])  10.1 us
    ppermute x2, waiting for transfers between devices, shifted(): lax.ppermute(shard, axis, [(i, (i + by) % peers) for i in range(peers)])  8.95 us
    ppermute x2, starting transfers between devices, shifted(): lax.ppermute(shard, axis, [(i, (i + by) % peers) for i in range(peers)])  4.37 us
    pallas_call x1, Pallas kernels, prepare(): call(body, shapes, [SMEM] * 2 + [HBM] * count, 'prepare', scratch, out_sp...  3.17 us
    ppermute x8, waiting for transfers between devices, crossed(): return lax.ppermute(shard, axis, [(i, i ^ by) for i in range(peers)])  2.56 us
    pallas_call x1, Pallas kernels, own_part(): call(body, shapes, [SMEM] * 3 + [VMEM] * 5, 'own_part')  2.36 us
    pallas_call x1, Pallas kernels, attend(): call(body, shape, specs, 'attend', cost=10 ** 10)  1.9 us
    pallas_call x1, Pallas kernels, receive_keys(): call(body, shapes, [SMEM] + [VMEM] * (3 + others), 'receive_keys', scratch)  1.46 us
  transfers between devices with their start and end apart: 10, of which 5 were waited for; matrix products, arithmetic and copies ran while one was open for 0% of the time, Pallas kernels for 24%

profile of v1, /device:TPU:0, one launch (start us, length us, event | category | flops | bytes accessed | tf_op | source)
XLA Modules:
  0.0 37.5 jit_solution(13930780062501199554)
XLA Ops:
  0.6 0.5 %collective-permute-start = (s32[1]{0:T(128)}, s32[1]{0:T(128)}, u32[]{:S(2)}, u32[]{:S(2)}) collective-permute-start(s32[1]{0:T(128)} %param.13), channel_id=1, source_target_pairs={{0,8},{8,0},{16,24},{24,16},{1,9},{9,1},{17,25},{25,17},{2,10},{10... | collective-permute-start | bytes 20 | tf_op jit(solution)/shard_map/ppermute | solution.py:39
  1.1 3.7 %collective-permute-start.2 = (bf16[512,256]{1,0:T(8,128)(2,1)}, bf16[512,256]{1,0:T(8,128)(2,1)S(1)}, u32[]{:S(2)}, u32[]{:S(2)}) collective-permute-start(bf16[512,256]{1,0:T(8,128)(2,1)} %bitcast.8), channel_id=1, source_target_pairs={{0,4},{1,5},{2,6},{3,7},{4,0},{5,1},{6,2},{7,3},{8,12},{9,13},{10,... | collective-permute-start | bytes 786440 | tf_op jit(solution)/shard_map/ppermute | solution.py:34
  5.5 0.0 collective-permute-done.near_ref
  5.5 3.2 %prepare.1 = (s32[1,16]{1,0:T(1,128)S(1)}, s32[2]{0:T(128)S(1)}, bf16[512,512]{1,0:T(8,128)(2,1)S(1)}, bf16[512,256]{1,0:T(8,128)(2,1)S(1)}, bf16[512,256]{1,0:T...) custom-call(s32[1]{0:T(128)S(6)} %copy.11.own_ref, ...), custom_call_target="tpu_custom_call" | custom-call | flops 1000 | bytes 1000 | tf_op jit(solution)/shard_map/prepare/pallas_call | solution.py:213
  8.7 0.7 %collective-permute-start.3 = (bf16[512,256]{1,0:T(8,128)(2,1)S(1)}, bf16[512,256]{1,0:T(8,128)(2,1)S(1)}, u32[]{:S(2)}, u32[]{:S(2)}) collective-permute-start(bf16[512,256]{1,0:T(8,128)(2,1)S(1)} %get-tuple-element.29.v_ref), channel_id=1, source_target_pairs={{0,4},{1,5},{2,6},{3,7},{4,0},{5,1},{6,2},{7,3},{8,12},{9,13},{10,... | collective-permute-start | bytes 786440 | tf_op jit(solution)/shard_map/ppermute | solution.py:34
  9.4 1.6 %collective-permute-start.4 = (bf16[128,256]{1,0:T(8,128)(2,1)S(1)}, bf16[128,256]{1,0:T(8,128)(2,1)S(1)}, u32[]{:S(2)}, u32[]{:S(2)}) collective-permute-start(bf16[128,256]{1,0:T(8,128)(2,1)S(1)} %get-tuple-element.40), channel_id=1, source_target_pairs={{0,2},{1,3},{2,0},{3,1},{4,6},{5,7},{6,4},{7,5},{8,10},{9,11},{10,... | collective-permute-start | bytes 196616 | tf_op jit(solution)/shard_map/ppermute | solution.py:39
  10.9 1.5 %collective-permute-start.1 = (s32[2]{0:T(128)S(1)}, s32[2]{0:T(128)S(1)}, u32[]{:S(2)}, u32[]{:S(2)}) collective-permute-start(s32[2]{0:T(128)S(1)} %get-tuple-element.26.here_ref), channel_id=1, source_target_pairs={{0,16},{8,24},{16,0},{24,8},{1,17},{9,25},{17,1},{25,9},{2,18},{10... | collective-permute-start | bytes 32 | tf_op jit(solution)/shard_map/ppermute | solution.py:39
  12.4 1.4 %collective-permute-start.5 = (bf16[128,256]{1,0:T(8,128)(2,1)S(1)}, bf16[128,256]{1,0:T(8,128)(2,1)S(1)}, u32[]{:S(2)}, u32[]{:S(2)}) collective-permute-start(bf16[128,256]{1,0:T(8,128)(2,1)S(1)} %get-tuple-element.41), channel_id=1, source_target_pairs={{0,3},{1,2},{2,1},{3,0},{4,7},{5,6},{6,5},{7,4},{8,11},{9,10},{10,... | collective-permute-start | bytes 196616 | tf_op jit(solution)/shard_map/ppermute | solution.py:39
  13.8 0.6 %collective-permute-done.1.there_ref = s32[2]{0:T(128)S(1)} collective-permute-done((s32[2]{0:T(128)S(1)}, s32[2]{0:T(128)S(1)}, u32[]{:S(2)}, u32[]{:S(2)}) %collective-permute-start.1) | collective-permute-done | bytes 40 | tf_op jit(solution)/shard_map/ppermute | solution.py:39
  14.5 1.5 %collective-permute-start.6 = (bf16[128,256]{1,0:T(8,128)(2,1)S(1)}, bf16[128,256]{1,0:T(8,128)(2,1)S(1)}, u32[]{:S(2)}, u32[]{:S(2)}) collective-permute-start(bf16[128,256]{1,0:T(8,128)(2,1)S(1)} %get-tuple-element.42), channel_id=1, source_target_pairs={{0,1},{1,0},{2,3},{3,2},{4,5},{5,4},{6,7},{7,6},{8,9},{9,8},{10,11... | collective-permute-start | bytes 196616 | tf_op jit(solution)/shard_map/ppermute | solution.py:39
  16.0 2.4 %own_part.1 = (bf16[512,512]{1,0:T(8,128)(2,1)S(1)}, f32[512,1024]{1,0:T(8,128)S(1)}, bf16[128,128]{1,0:T(8,128)(2,1)S(1)}, f32[512,128]{1,0:T(8,128)S(1)}, f32[1,2,2,256,128]{4,3,2,1,0:T(8,128)S(1)}) custom-call(s32[1,16]{1,0:T(1,128)S(1)} %get-tuple-element.25.facts_ref, s32[2]{0:T(128)S(1)} %get-tuple-element.26.here_ref, ...), custom_call_target="tpu_custom_call" | custom-call | flops 1000 | bytes 1000 | tf_op jit(solution)/shard_map/own_part/pallas_call | solution.py:299
  18.4 5.0 %collective-permute-done.2.refs_0_ = bf16[512,256]{1,0:T(8,128)(2,1)S(1)} collective-permute-done((bf16[512,256]{1,0:T(8,128)(2,1)}, bf16[512,256]{1,0:T(8,128)(2,1)S(1)}, u32[]{:S(2)}, u32[]{:S(2)}) %collective-permute-start.2) | collective-permute-done | bytes 262176 | tf_op jit(solution)/shard_map/ppermute | solution.py:34
  23.4 1.5 %receive_keys.1 = (bf16[2,4,256,256]{3,2,1,0:T(8,128)(2,1)S(1)}, bf16[1,256,256]{2,1,0:T(8,128)(2,1)S(1)}) custom-call(s32[1,16]{1,0:T(1,128)S(1)} %get-tuple-element.25.facts_ref, bf16[512,512]{1,0:T(8,128)(2,1)S(1)} %get-tuple-element.34.q_ref, bf16[256,512]{1,0:T(8,128)(2,1)S(1)} %get-tuple-element.35.select_ref, ...), custom_call_target="tpu_custom_call" | custom-call | flops 1000 | bytes 1000 | tf_op jit(solution)/shard_map/receive_keys/pallas_call | solution.py:346
  24.9 3.9 %collective-permute-done.3.refs_1_.refs_0_ = bf16[512,256]{1,0:T(8,128)(2,1)S(1)} collective-permute-done((bf16[512,256]{1,0:T(8,128)(2,1)S(1)}, bf16[512,256]{1,0:T(8,128)(2,1)S(1)}, u32[]{:S(2)}, u32[]{:S(2)}) %collective-permute-start.3) | collective-permute-done | bytes 262176 | tf_op jit(solution)/shard_map/ppermute | solution.py:34
  28.8 0.2 receive_values.1
  29.0 0.8 %collective-permute-start.7 = (bf16[128,256]{1,0:T(8,128)(2,1)S(1)}, bf16[128,256]{1,0:T(8,128)(2,1)S(1)}, u32[]{:S(2)}, u32[]{:S(2)}) collective-permute-start(bf16[128,256]{1,0:T(8,128)(2,1)S(1)} %get-tuple-element.45), channel_id=1, source_target_pairs={{0,2},{1,3},{2,0},{3,1},{4,6},{5,7},{6,4},{7,5},{8,10},{9,11},{10,... | collective-permute-start | bytes 196616 | tf_op jit(solution)/shard_map/ppermute | solution.py:39
  29.8 2.3 %collective-permute-start.8 = (bf16[128,256]{1,0:T(8,128)(2,1)S(1)}, bf16[128,256]{1,0:T(8,128)(2,1)S(1)}, u32[]{:S(2)}, u32[]{:S(2)}) collective-permute-start(bf16[128,256]{1,0:T(8,128)(2,1)S(1)} %get-tuple-element.46), channel_id=1, source_target_pairs={{0,3},{1,2},{2,1},{3,0},{4,7},{5,6},{6,5},{7,4},{8,11},{9,10},{10,... | collective-permute-start | bytes 196616 | tf_op jit(solution)/shard_map/ppermute | solution.py:39
  32.1 0.0 collective-permute-done.4.refs_1_
  32.1 0.4 %collective-permute-start.9 = (bf16[128,256]{1,0:T(8,128)(2,1)S(1)}, bf16[128,256]{1,0:T(8,128)(2,1)S(1)}, u32[]{:S(2)}, u32[]{:S(2)}) collective-permute-start(bf16[128,256]{1,0:T(8,128)(2,1)S(1)} %get-tuple-element.47), channel_id=1, source_target_pairs={{0,1},{1,0},{2,3},{3,2},{4,5},{5,4},{6,7},{7,6},{8,9},{9,8},{10,11... | collective-permute-start | bytes 196616 | tf_op jit(solution)/shard_map/ppermute | solution.py:39
  32.6 1.9 %attend.1 = bf16[512,512]{1,0:T(8,128)(2,1)} custom-call(s32[1,16]{1,0:T(1,128)S(1)} %get-tuple-element.25.facts_ref, f32[512,1024]{1,0:T(8,128)S(1)} %get-tuple-element.32.acc_ref, f32[512,128]{1,0:T(8,128)S(1)} %get-tuple-element.33.live_ref, bf16[2,4,256,256]{3,2,1,0:T(8,128)(2,1)S(1)} %get-tuple-element.37.refs_0_, ...), custom_call_target="tpu_custom_call" | custom-call | flops 10000000000 | bytes 1000 | tf_op jit(solution)/shard_map/attend/pallas_call | solution.py:404
  34.5 0.0 collective-permute-done.5.refs_2_
  34.5 0.0 collective-permute-done.6.refs_3_
  34.5 0.0 collective-permute-done.7.refs_5_
  34.5 0.8 %collective-permute-done.8.refs_6_ = bf16[128,256]{1,0:T(8,128)(2,1)S(1)} collective-permute-done((bf16[128,256]{1,0:T(8,128)(2,1)S(1)}, bf16[128,256]{1,0:T(8,128)(2,1)S(1)}, u32[]{:S(2)}, u32[]{:S(2)}) %collective-permute-start.8) | collective-permute-done | bytes 65568 | tf_op jit(solution)/shard_map/ppermute | solution.py:39
  35.3 1.1 %collective-permute-done.9.refs_7_ = bf16[128,256]{1,0:T(8,128)(2,1)S(1)} collective-permute-done((bf16[128,256]{1,0:T(8,128)(2,1)S(1)}, bf16[128,256]{1,0:T(8,128)(2,1)S(1)}, u32[]{:S(2)}, u32[]{:S(2)}) %collective-permute-start.9) | collective-permute-done | bytes 65568 | tf_op jit(solution)/shard_map/ppermute | solution.py:39
  36.4 1.1 %cache_part.1 = bf16[128,2048]{1,0:T(8,128)(2,1)} custom-call(bf16[128,128]{1,0:T(8,128)(2,1)S(1)} %get-tuple-element.38.kept_ref, bf16[128,256]{1,0:T(8,128)(2,1)S(1)} %get-tuple-element.39.refs_0_, bf16[128,256]{1,0:T(8,128)(2,1)S(1)} %collective-permute-done.4.refs_1_, bf16[128,256]{1,0:T(8,128)(2,1)S(1)} %collective-permute-done.5.refs_2_, ...), custom_call_target="tpu_custom_call" | custom-call | flops 1000 | bytes 1000 | tf_op jit(solution)/shard_map/cache_part/pallas_call | solution.py:429
Async XLA Ops:
  0.6 4.8 %collective-permute-start = (s32[1]{0:T(128)}, s32[1]{0:T(128)}, u32[]{:S(2)}, u32[]{:S(2)}) collective-permute-start(s32[1]{0:T(128)} %param.13), channel_id=1, source_target_pairs={{0,8},{8,0},{16,24},{24,16},{1,9},{9,1},{17,25},{25,17},{2,10},{10... | collective-permute-start | bytes 20 | tf_op jit(solution)/shard_map/ppermute | solution.py:39
  1.1 22.3 %collective-permute-start.2 = (bf16[512,256]{1,0:T(8,128)(2,1)}, bf16[512,256]{1,0:T(8,128)(2,1)S(1)}, u32[]{:S(2)}, u32[]{:S(2)}) collective-permute-start(bf16[512,256]{1,0:T(8,128)(2,1)} %bitcast.8), channel_id=1, source_target_pairs={{0,4},{1,5},{2,6},{3,7},{4,0},{5,1},{6,2},{7,3},{8,12},{9,13},{10,... | collective-permute-start | bytes 786440 | tf_op jit(solution)/shard_map/ppermute | solution.py:34
  8.7 20.1 %collective-permute-start.3 = (bf16[512,256]{1,0:T(8,128)(2,1)S(1)}, bf16[512,256]{1,0:T(8,128)(2,1)S(1)}, u32[]{:S(2)}, u32[]{:S(2)}) collective-permute-start(bf16[512,256]{1,0:T(8,128)(2,1)S(1)} %get-tuple-element.29.v_ref), channel_id=1, source_target_pairs={{0,4},{1,5},{2,6},{3,7},{4,0},{5,1},{6,2},{7,3},{8,12},{9,13},{10,... | collective-permute-start | bytes 786440 | tf_op jit(solution)/shard_map/ppermute | solution.py:34
  9.4 22.8 %collective-permute-start.4 = (bf16[128,256]{1,0:T(8,128)(2,1)S(1)}, bf16[128,256]{1,0:T(8,128)(2,1)S(1)}, u32[]{:S(2)}, u32[]{:S(2)}) collective-permute-start(bf16[128,256]{1,0:T(8,128)(2,1)S(1)} %get-tuple-element.40), channel_id=1, source_target_pairs={{0,2},{1,3},{2,0},{3,1},{4,6},{5,7},{6,4},{7,5},{8,10},{9,11},{10,... | collective-permute-start | bytes 196616 | tf_op jit(solution)/shard_map/ppermute | solution.py:39
  10.9 3.5 %collective-permute-start.1 = (s32[2]{0:T(128)S(1)}, s32[2]{0:T(128)S(1)}, u32[]{:S(2)}, u32[]{:S(2)}) collective-permute-start(s32[2]{0:T(128)S(1)} %get-tuple-element.26.here_ref), channel_id=1, source_target_pairs={{0,16},{8,24},{16,0},{24,8},{1,17},{9,25},{17,1},{25,9},{2,18},{10... | collective-permute-start | bytes 32 | tf_op jit(solution)/shard_map/ppermute | solution.py:39
  12.4 22.0 %collective-permute-start.5 = (bf16[128,256]{1,0:T(8,128)(2,1)S(1)}, bf16[128,256]{1,0:T(8,128)(2,1)S(1)}, u32[]{:S(2)}, u32[]{:S(2)}) collective-permute-start(bf16[128,256]{1,0:T(8,128)(2,1)S(1)} %get-tuple-element.41), channel_id=1, source_target_pairs={{0,3},{1,2},{2,1},{3,0},{4,7},{5,6},{6,5},{7,4},{8,11},{9,10},{10,... | collective-permute-start | bytes 196616 | tf_op jit(solution)/shard_map/ppermute | solution.py:39
  14.5 20.0 %collective-permute-start.6 = (bf16[128,256]{1,0:T(8,128)(2,1)S(1)}, bf16[128,256]{1,0:T(8,128)(2,1)S(1)}, u32[]{:S(2)}, u32[]{:S(2)}) collective-permute-start(bf16[128,256]{1,0:T(8,128)(2,1)S(1)} %get-tuple-element.42), channel_id=1, source_target_pairs={{0,1},{1,0},{2,3},{3,2},{4,5},{5,4},{6,7},{7,6},{8,9},{9,8},{10,11... | collective-permute-start | bytes 196616 | tf_op jit(solution)/shard_map/ppermute | solution.py:39
  29.0 5.5 %collective-permute-start.7 = (bf16[128,256]{1,0:T(8,128)(2,1)S(1)}, bf16[128,256]{1,0:T(8,128)(2,1)S(1)}, u32[]{:S(2)}, u32[]{:S(2)}) collective-permute-start(bf16[128,256]{1,0:T(8,128)(2,1)S(1)} %get-tuple-element.45), channel_id=1, source_target_pairs={{0,2},{1,3},{2,0},{3,1},{4,6},{5,7},{6,4},{7,5},{8,10},{9,11},{10,... | collective-permute-start | bytes 196616 | tf_op jit(solution)/shard_map/ppermute | solution.py:39
  29.8 5.5 %collective-permute-start.8 = (bf16[128,256]{1,0:T(8,128)(2,1)S(1)}, bf16[128,256]{1,0:T(8,128)(2,1)S(1)}, u32[]{:S(2)}, u32[]{:S(2)}) collective-permute-start(bf16[128,256]{1,0:T(8,128)(2,1)S(1)} %get-tuple-element.46), channel_id=1, source_target_pairs={{0,3},{1,2},{2,1},{3,0},{4,7},{5,6},{6,5},{7,4},{8,11},{9,10},{10,... | collective-permute-start | bytes 196616 | tf_op jit(solution)/shard_map/ppermute | solution.py:39
  32.1 4.3 %collective-permute-start.9 = (bf16[128,256]{1,0:T(8,128)(2,1)S(1)}, bf16[128,256]{1,0:T(8,128)(2,1)S(1)}, u32[]{:S(2)}, u32[]{:S(2)}) collective-permute-start(bf16[128,256]{1,0:T(8,128)(2,1)S(1)} %get-tuple-element.47), channel_id=1, source_target_pairs={{0,1},{1,0},{2,3},{3,2},{4,5},{5,4},{6,7},{7,6},{8,9},{9,8},{10,11... | collective-permute-start | bytes 196616 | tf_op jit(solution)/shard_map/ppermute | solution.py:39

commit v2 on v1

--- a/solution.py
+++ b/solution.py
@@ -159,14 +159,16 @@
     slots = table.shape[1]
     residues = decode_rank.shape[1]
     piece = rows // residues
+    first = block_len // slots
     arrays = (keys, values, queries, *tables, table, decode_rank, owner)
     count = len(arrays)
     facts_of = lambda ref: Facts(ref, slots, residues, owner.shape[0])
 
     def body(own_ref, near_ref, *refs):
         inputs, refs = refs[:count], refs[count:]
-        facts_ref, pair_ref, q_ref, kr_ref, v_ref, row_ref, blk_ref, select_ref = refs[:8]
-        e_refs, refs = refs[8:12], refs[12:]
+        facts_ref, pair_ref, q_ref, kr_ref, v_ref, row_ref, blk_ref, select_ref, order_ref = refs[:9]
+        e_refs, refs = refs[9:13], refs[13:]
+        sent_refs, refs = refs[: 2 * slots - 2], refs[2 * slots - 2 :]
         k_ref, map_ref, rank_ref, owner_ref, sems = refs
         targets = (k_ref, v_ref, q_ref, row_ref, blk_ref, map_ref, rank_ref, owner_ref)
         copies = []
@@ -190,6 +192,22 @@
         )
         select_ref[...] = select
         copies[1].wait()
+        for turn in range(1, slots):
+            order = order_matrix(
+                lambda r: rank_ref[0, r],
+                (slot + turn) % slots,
+                head_group,
+                block_len,
+                block_len,
+                residues,
+            )
+            for half in range(2):
+                moved = dot(order, v_ref[columns(half, block_len)]).astype(bf16)
+                sent_refs[2 * turn - 2][columns(half, first)] = moved[:first]
+                sent_refs[2 * turn - 1][columns(half, block_len - first)] = moved[first:]
+        order_ref[...] = order_matrix(
+            lambda r: rank_ref[0, r], slot, head_group, block_len, block_len, residues
+        )
         for kind, source in enumerate((kr_ref, v_ref)):
             chosen = dot(select, source[...]).astype(bf16)
             for m in range(HEAD_DIVISIONS):
@@ -205,8 +223,12 @@
         jax.ShapeDtypeStruct(tables[0].shape, f32),
         jax.ShapeDtypeStruct(tables[1].shape, f32),
         jax.ShapeDtypeStruct((rows // slots, rows), bf16),
+        jax.ShapeDtypeStruct((block_len, block_len), bf16),
     ]
     shapes += [jax.ShapeDtypeStruct((2 * piece, width), bf16) for _ in range(HEAD_DIVISIONS)]
+    for _ in range(1, slots):
+        shapes.append(jax.ShapeDtypeStruct((2 * first, width), bf16))
+        shapes.append(jax.ShapeDtypeStruct((2 * (block_len - first), width), bf16))
     scratch = [pltpu.VMEM(keys.shape, keys.dtype)]
     scratch += [pltpu.SMEM(x.shape, x.dtype) for x in (table, decode_rank, owner)]
     scratch.append(pltpu.SemaphoreType.DMA((count,)))
@@ -218,7 +240,7 @@
         scratch,
         out_specs=[SMEM] * 2 + [VMEM] * (len(shapes) - 2),
     )(own_length, near_length, *in_hbm(arrays))
-    return outs[0], facts_of, outs[1], outs[2:5], outs[5:7], outs[7], outs[8:]
+    return outs[0], facts_of, outs[1], outs[2:5], outs[5:7], outs[7:9], outs[9:13], outs[13:]
 
 
 def own_part(facts_row, facts_of, operands, tables, lens):
@@ -310,72 +332,105 @@
     return outer, first, second
 
 
-def receive_keys(facts_row, facts_of, key_in, query_rot, select, angles):
+def receive_keys(key_in, select, order, angles):
     others = len(key_in)
     rows, width = key_in[0].shape
     block_len = rows // 2
+
+    def body(select_ref, order_ref, angle_ref, *refs):
+        k_refs, refs = refs[:others], refs[others:]
+        p_refs, chosen_ref, kr_ref = refs[:others], refs[others], refs[others + 1]
+        for turn in range(others):
+            for half in range(2):
+                part = columns(half, block_len)
+                there = angle_ref[turn, half, 0], angle_ref[turn, half, 1]
+                for head in range(KV_DEV):
+                    kr_ref[part, columns(head)] = turned(
+                        k_refs[turn][part, columns(head)], there
+                    ).astype(bf16)
+                p_refs[turn][part] = dot(order_ref[...], kr_ref[part]).astype(bf16)
+            chosen_ref[turn] = dot(select_ref[...], kr_ref[...]).astype(bf16)
+
+    shapes = [jax.ShapeDtypeStruct((rows, width), bf16) for _ in range(others)]
+    shapes.append(jax.ShapeDtypeStruct((others, select.shape[0], width), bf16))
+    scratch = [pltpu.VMEM((rows, width), bf16)]
+    outs = call(body, shapes, [VMEM] * (3 + others), "receive_keys", scratch, cost=10**10)(
+        select, order, angles, *key_in
+    )
+    return outs[:others], outs[others]
+
+
+def weigh(facts_row, facts_of, query_rot, key_rot):
+    others = len(key_rot)
+    rows = query_rot.shape[0]
+    block_len = rows // 2
     slots = facts_of(None).slots
 
-    def body(facts_ref, q_ref, select_ref, angle_ref, *refs):
-        k_refs, refs = refs[:others], refs[others:]
-        w_refs, chosen_ref, kr_ref = refs[:others], refs[others], refs[others + 1]
+    def body(facts_ref, q_ref, *refs):
+        k_refs, w_refs = refs[:others], refs[others:]
         facts = facts_of(facts_ref)
         slot = slot_and_head_group()[0]
         for turn in range(1, slots):
-            for half in range(2):
-                part = columns(half, block_len)
-                there = angle_ref[turn - 1, half, 0], angle_ref[turn - 1, half, 1]
-                for head in range(KV_DEV):
-                    kr_ref[part, columns(head)] = turned(
-                        k_refs[turn - 1][part, columns(head)], there
-                    ).astype(bf16)
-            chosen_ref[turn - 1] = dot(select_ref[...], kr_ref[...]).astype(bf16)
             _, *tiles = tiles_of(facts, slot, (slot - turn + slots) % slots)
             for index, (half, other) in enumerate(tiles):
                 for head in range(Q_DEV):
                     key_head = columns(head * KV_DEV // Q_DEV)
                     queries = q_ref[rows_at(half, block_len), columns(head)]
-                    expo = expo_of(dot_t(queries, kr_ref[rows_at(other, block_len), key_head]))
-                    w_refs[turn - 1][index, head] = expo.astype(bf16)
+                    keys = k_refs[turn - 1][rows_at(other, block_len), key_head]
+                    w_refs[turn - 1][index, head] = expo_of(dot_t(queries, keys)).astype(bf16)
 
     shapes = [
         jax.ShapeDtypeStruct((2, Q_DEV, block_len, block_len), bf16) for _ in range(others)
     ]
-    shapes.append(jax.ShapeDtypeStruct((others, select.shape[0], width), bf16))
-    scratch = [pltpu.VMEM((rows, width), bf16)]
-    outs = call(body, shapes, [SMEM] + [VMEM] * (3 + others), "receive_keys", scratch)(
-        facts_row, query_rot, select, angles, *key_in
-    )
-    return outs[:others], outs[others]
-
-
-def receive_values(value_in, select, key_chosen):
-    others = len(value_in)
-    rows, width = value_in[0].shape
-    piece = select.shape[0] // HEAD_DIVISIONS
-
-    def body(select_ref, key_ref, *refs):
+    return call(body, shapes, [SMEM] + [VMEM] * (1 + others), "weigh")(
+        facts_row, query_rot, *key_rot
+    )
+
+
+def late_pieces(heads, key_chosen):
+    others, rows, width = key_chosen.shape
+    piece = rows // HEAD_DIVISIONS
+    run = piece // 2
+    first = heads[0].shape[0] // 2
+
+    def body(key_ref, *refs):
         v_refs, e_refs = refs[:others], refs[others:]
-        for turn in range(others):
-            chosen = dot(select_ref[...], v_refs[turn][...]).astype(bf16)
-            for m in range(HEAD_DIVISIONS):
+        for m in range(HEAD_DIVISIONS):
+            for turn in range(others):
                 e_refs[m][columns(turn, piece)] = key_ref[turn, columns(m, piece)]
-                e_refs[m][columns(others + turn, piece)] = chosen[columns(m, piece)]
+                place = 2 * (others + turn)
+                if run % 16 == 0:
+                    for half in range(2):
+                        start = half * first + m * run
+                        e_refs[m][columns(place + half, run)] = v_refs[turn][start : start + run]
+                    continue
+                lines = [
+                    v_refs[turn][columns(half, first)].astype(f32)[columns(m, run)]
+                    for half in range(2)
+                ]
+                e_refs[m][place * run : (place + 2) * run] = jnp.concatenate(lines, 0).astype(bf16)
 
     shapes = [
         jax.ShapeDtypeStruct((2 * others * piece, width), bf16) for _ in range(HEAD_DIVISIONS)
     ]
-    return call(body, shapes, [VMEM] * (2 + others), "receive_values")(select, key_chosen, *value_in)
-
-
-def attend(facts_row, facts_of, weights, acc, value_in, live):
+    return call(body, shapes, [VMEM] * (1 + others), "late_pieces")(key_chosen, *heads)
+
+
+def attend(facts_row, facts_of, weights, acc, heads, tails, live, mark):
     rows = live.shape[0]
     block_len = rows // 2
     others = len(weights)
     slots = facts_of(None).slots
 
-    def body(facts_ref, acc_ref, live_ref, *refs):
-        w_refs, v_refs, out_ref = refs[:others], refs[others : 2 * others], refs[2 * others]
+    def body(facts_ref, mark_ref, acc_ref, live_ref, *refs):
+        w_refs, h_refs, t_refs = refs[:others], refs[others : 2 * others], refs[2 * others : 3 * others]
+        out_ref, v_scr = refs[3 * others :]
+        for turn in range(others):
+            first, rest = h_refs[turn].shape[0] // 2, t_refs[turn].shape[0] // 2
+            for half in range(2):
+                v_scr[turn, columns(half, block_len)] = jnp.concatenate(
+                    [h_refs[turn][columns(half, first)], t_refs[turn][columns(half, rest)]], axis=0
+                )
         facts = facts_of(facts_ref)
         slot = slot_and_head_group()[0]
         low, high = facts.halves(slot)
@@ -389,7 +444,7 @@
                 either, upper = [
                     dot(
                         w_refs[turn - 1][index, head],
-                        beside_ones(v_refs[turn - 1][rows_at(other, block_len), key_head]),
+                        beside_ones(v_scr[turn - 1, rows_at(other, block_len), key_head]),
                     )
                     for index, (_, other) in enumerate(tiles)
                 ]
@@ -400,9 +455,10 @@
                 out_ref[part, columns(head)] = (total[:, :HEAD_SIZE] * scale).astype(bf16)
 
     shape = jax.ShapeDtypeStruct((rows, Q_DEV * HEAD_SIZE), bf16)
-    specs = [SMEM] + [VMEM] * (2 + 2 * others)
-    return call(body, shape, specs, "attend", cost=10**10)(
-        facts_row, acc, live, *weights, *value_in
+    specs = [SMEM] + [VMEM] * (3 + 3 * others)
+    scratch = [pltpu.VMEM((others, rows, KV_WIDTH), bf16)]
+    return call(body, shape, specs, "attend", scratch)(
+        facts_row, mark, acc, live, *weights, *heads, *tails
     )
 
 
@@ -412,7 +468,8 @@
     width = early[0].shape[1]
 
     def body(kept_ref, *refs):
-        f_refs, s_refs, out_ref = refs[:4], refs[4:8], refs[8]
+        f_refs, s_refs, out_ref, mark_ref = refs[:4], refs[4:8], refs[8], refs[9]
+        mark_ref[...] = jnp.zeros_like(mark_ref)
         head_group = slot_and_head_group()[1]
         later = cache_rows - piece
         for index, m in enumerate(HAND_ORDER):
@@ -425,7 +482,10 @@
                     kept_ref[...], lines
                 ).astype(bf16)
 
-    shape = jax.ShapeDtypeStruct((cache_rows, 2 * HEAD_DIVISIONS * width), bf16)
+    shape = [
+        jax.ShapeDtypeStruct((cache_rows, 2 * HEAD_DIVISIONS * width), bf16),
+        jax.ShapeDtypeStruct((8, HEAD_SIZE), f32),
+    ]
     return call(body, shape, [VMEM] * 9, "cache_part")(kept, *early, *late)
 
 
@@ -435,14 +495,14 @@
     q, k, v = queries[0, 0], keys[0, 0], values[0, 0]
     tables = rotary_tables(block_len, 2 * slots)
 
-    def to_slots(part):
-        return [shifted(part, "blk", HEAD_DIVISIONS * t) for t in range(1, slots)]
+    def to_slots(parts):
+        return [shifted(parts[t - 1], "blk", HEAD_DIVISIONS * t) for t in range(1, slots)]
 
     def hand_on(pieces):
         return [pieces[0]] + [crossed(pieces[m], "blk", m) for m in HAND_ORDER[1:]]
 
-    key_in = to_slots(k)
-    facts_row, facts_of, block, operands, tables, select, early = prepare(
+    key_in = to_slots([k] * (slots - 1))
+    facts_row, facts_of, block, operands, tables, (select, order), early, sent = prepare(
         q,
         k,
         v,
@@ -453,7 +513,9 @@
         lengths,
         crossed(lengths, "req", 1),
     )
-    value_in = to_slots(operands[2])
+    heads = to_slots(sent[0::2])
+    tails, key_in = lax.optimization_barrier((sent[1::2], key_in))
+    tails = to_slots(tails)
     early = hand_on(early)
     span, groups = 2, lax.axis_size("req")
     while 2 * span < groups:
@@ -465,10 +527,11 @@
         span = 2 * span
     lens = (block, crossed(block, "req", span))
     query_rot, acc, kept, live, angles = own_part(facts_row, facts_of, operands, tables, lens)
-    weights, chosen = receive_keys(facts_row, facts_of, key_in, query_rot, select, angles)
-    late = hand_on(receive_values(value_in, select, chosen))
-    attended = attend(facts_row, facts_of, weights, acc, value_in, live)
-    cache = cache_part(early, late, kept)
+    key_rot, chosen = receive_keys(key_in, select, order, angles)
+    late = hand_on(late_pieces(heads, chosen))
+    weights = weigh(facts_row, facts_of, query_rot, key_rot)
+    cache, mark = cache_part(early, late, kept)
+    attended = attend(facts_row, facts_of, weights, acc, heads, tails, live, mark)
     return (attended[None, None], cache[None])
 
 

time: 37.6 us -> 35.8 us (0.952)
  waiting for transfers between devices: 11.5 us -> 9.4 us
    ppermute x2 -> x3, waiting for transfers between devices: 8.95 us -> 5.27 us  [shifted(): lax.ppermute(shard, axis, [(i, (i + by) % peers) for i in range(peers)])]
    ppermute x8, waiting for transfers between devices: 2.56 us -> 4.13 us  [crossed(): return lax.ppermute(shard, axis, [(i, i ^ by) for i in range(peers)])]
    ppermute x2 -> x3, starting transfers between devices: 4.37 us -> 4.44 us  [shifted(): lax.ppermute(shard, axis, [(i, (i + by) % peers) for i in range(peers)])]
    pallas_call x3 -> x4, Pallas kernels: 3.58 us -> 3.6 us  [the longest x1 1.89 us: attend(): call(body, shape, specs, 'attend', scratch)]
  transfers between devices with their start and end apart: 10 -> 11, of which waited for: 5 -> 6; matrix products, arithmetic and copies ran while one was open for 0% -> 0% of each run, Pallas kernels for 24% -> 24%
where the time goes in v2:
time: 35.8 us; the launch traced here: 35.7 us
  starting transfers between devices  14.5 us (41%)
  Pallas kernels  10.4 us (29%)
  waiting for transfers between devices  9.4 us (26%)
  between operations  1.34 us (4%)
    ppermute x8, starting transfers between devices, crossed(): return lax.ppermute(shard, axis, [(i, i ^ by) for i in range(peers)])  10.1 us
    ppermute x3, waiting for transfers between devices, shifted(): lax.ppermute(shard, axis, [(i, (i + by) % peers) for i in range(peers)])  5.27 us
    ppermute x3, starting transfers between devices, shifted(): lax.ppermute(shard, axis, [(i, (i + by) % peers) for i in range(peers)])  4.44 us
    ppermute x8, waiting for transfers between devices, crossed(): return lax.ppermute(shard, axis, [(i, i ^ by) for i in range(peers)])  4.13 us
    pallas_call x1, Pallas kernels, prepare(): call(body, shapes, [SMEM] * 2 + [HBM] * count, 'prepare', scratch, out_sp...  3.34 us
    pallas_call x1, Pallas kernels, own_part(): call(body, shapes, [SMEM] * 3 + [VMEM] * 5, 'own_part')  2.35 us
    pallas_call x1, Pallas kernels, attend(): call(body, shape, specs, 'attend', scratch)  1.89 us
    pallas_call x1, Pallas kernels, weigh(): call(body, shapes, [SMEM] + [VMEM] * (1 + others), 'weigh')  1.27 us
  transfers between devices with their start and end apart: 11, of which 6 were waited for; matrix products, arithmetic and copies ran while one was open for 0% of the time, Pallas kernels for 24%

profile of v2, /device:TPU:0, one launch (start us, length us, event | category | flops | bytes accessed | tf_op | source)
XLA Modules:
  0.0 35.7 jit_solution(3089273670599287868)
XLA Ops:
  0.6 4.1 %collective-permute-start.5 = (bf16[512,256]{1,0:T(8,128)(2,1)}, bf16[512,256]{1,0:T(8,128)(2,1)S(1)}, u32[]{:S(2)}, u32[]{:S(2)}) collective-permute-start(bf16[512,256]{1,0:T(8,128)(2,1)} %bitcast.8), channel_id=1, source_target_pairs={{0,4},{1,5},{2,6},{3,7},{4,0},{5,1},{6,2},{7,3},{8,12},{9,13},{10,... | collective-permute-start | bytes 786440 | tf_op jit(solution)/shard_map/ppermute | solution.py:34
  4.7 0.0 collective-permute-start
  5.4 0.6 %collective-permute-done.near_ref = s32[1]{0:T(128)} collective-permute-done((s32[1]{0:T(128)}, s32[1]{0:T(128)}, u32[]{:S(2)}, u32[]{:S(2)}) %collective-permute-start) | collective-permute-done | bytes 36 | tf_op jit(solution)/shard_map/ppermute | solution.py:39
  6.0 3.3 %prepare.1 = (s32[1,16]{1,0:T(1,128)S(1)}, s32[2]{0:T(128)S(1)}, bf16[512,512]{1,0:T(8,128)(2,1)S(1)}, bf16[512,256]{1,0:T(8,128)(2,1)S(1)}, bf16[512,256]{1,0:T...) custom-call(s32[1]{0:T(128)S(6)} %copy.11.own_ref, ...), custom_call_target="tpu_custom_call" | custom-call | flops 1000 | bytes 1000 | tf_op jit(solution)/shard_map/prepare/pallas_call | solution.py:235
  9.3 1.6 %collective-permute-start.1 = (s32[2]{0:T(128)S(1)}, s32[2]{0:T(128)S(1)}, u32[]{:S(2)}, u32[]{:S(2)}) collective-permute-start(s32[2]{0:T(128)S(1)} %get-tuple-element.33.here_ref), channel_id=1, source_target_pairs={{0,16},{8,24},{16,0},{24,8},{1,17},{9,25},{17,1},{25,9},{2,18},{10... | collective-permute-start | bytes 32 | tf_op jit(solution)/shard_map/ppermute | solution.py:39
  10.9 0.3 collective-permute-start.6
  11.2 1.6 %collective-permute-start.2 = (bf16[128,256]{1,0:T(8,128)(2,1)S(1)}, bf16[128,256]{1,0:T(8,128)(2,1)S(1)}, u32[]{:S(2)}, u32[]{:S(2)}) collective-permute-start(bf16[128,256]{1,0:T(8,128)(2,1)S(1)} %get-tuple-element.41), channel_id=1, source_target_pairs={{0,2},{1,3},{2,0},{3,1},{4,6},{5,7},{6,4},{7,5},{8,10},{9,11},{10,... | collective-permute-start | bytes 196616 | tf_op jit(solution)/shard_map/ppermute | solution.py:39
  12.8 1.4 %collective-permute-start.3 = (bf16[128,256]{1,0:T(8,128)(2,1)S(1)}, bf16[128,256]{1,0:T(8,128)(2,1)S(1)}, u32[]{:S(2)}, u32[]{:S(2)}) collective-permute-start(bf16[128,256]{1,0:T(8,128)(2,1)S(1)} %get-tuple-element.42), channel_id=1, source_target_pairs={{0,3},{1,2},{2,1},{3,0},{4,7},{5,6},{6,5},{7,4},{8,11},{9,10},{10,... | collective-permute-start | bytes 196616 | tf_op jit(solution)/shard_map/ppermute | solution.py:39
  14.2 0.0 collective-permute-done.1.there_ref
  14.2 0.5 %collective-permute-start.4 = (bf16[128,256]{1,0:T(8,128)(2,1)S(1)}, bf16[128,256]{1,0:T(8,128)(2,1)S(1)}, u32[]{:S(2)}, u32[]{:S(2)}) collective-permute-start(bf16[128,256]{1,0:T(8,128)(2,1)S(1)} %get-tuple-element.43), channel_id=1, source_target_pairs={{0,1},{1,0},{2,3},{3,2},{4,5},{5,4},{6,7},{7,6},{8,9},{9,8},{10,11... | collective-permute-start | bytes 196616 | tf_op jit(solution)/shard_map/ppermute | solution.py:39
  14.7 2.4 %own_part.1 = (bf16[512,512]{1,0:T(8,128)(2,1)S(1)}, f32[512,1024]{1,0:T(8,128)S(1)}, bf16[128,128]{1,0:T(8,128)(2,1)S(1)}, f32[512,128]{1,0:T(8,128)S(1)}, f32[1,2,2,256,128]{4,3,2,1,0:T(8,128)S(1)}) custom-call(s32[1,16]{1,0:T(1,128)S(1)} %get-tuple-element.32.facts_ref, s32[2]{0:T(128)S(1)} %get-tuple-element.33.here_ref, ...), custom_call_target="tpu_custom_call" | custom-call | flops 1000 | bytes 1000 | tf_op jit(solution)/shard_map/own_part/pallas_call | solution.py:321
  17.1 3.5 %collective-permute-done.5.refs_0_ = bf16[512,256]{1,0:T(8,128)(2,1)S(1)} collective-permute-done((bf16[512,256]{1,0:T(8,128)(2,1)}, bf16[512,256]{1,0:T(8,128)(2,1)S(1)}, u32[]{:S(2)}, u32[]{:S(2)}) %collective-permute-start.5) | collective-permute-done | bytes 262176 | tf_op jit(solution)/shard_map/ppermute | solution.py:34
  20.5 0.0 collective-permute-start.10
  20.5 0.4 %receive_keys.1 = (bf16[512,256]{1,0:T(8,128)(2,1)S(1)}, bf16[1,256,256]{2,1,0:T(8,128)(2,1)S(1)}) custom-call(bf16[256,512]{1,0:T(8,128)(2,1)S(1)} %get-tuple-element.44.select_ref, bf16[256,256]{1,0:T(8,128)(2,1)S(1)} %get-tuple-element.45.order_ref, f32[1,2,2,256,128]{4,3,2,1,0:T(8,128)S(1)} %get-tuple-element.46.angle_ref, ...), custom_call_target="tpu_custom_call" | custom-call | flops 10000000000 | bytes 1000 | tf_op jit(solution)/shard_map/receive_keys/pallas_call | solution.py:357
  21.0 1.8 %collective-permute-done.6.refs_0_.refs_1_ = bf16[256,256]{1,0:T(8,128)(2,1)S(1)} collective-permute-done((bf16[256,256]{1,0:T(8,128)(2,1)S(1)}, bf16[256,256]{1,0:T(8,128)(2,1)S(1)}, u32[]{:S(2)}, u32[]{:S(2)}) %collective-permute-start.6) | collective-permute-done | bytes 131104 | tf_op jit(solution)/shard_map/ppermute | solution.py:34
  22.8 3.5 %collective-permute-start.7 = (bf16[128,256]{1,0:T(8,128)(2,1)S(1)}, bf16[128,256]{1,0:T(8,128)(2,1)S(1)}, u32[]{:S(2)}, u32[]{:S(2)}) collective-permute-start(bf16[128,256]{1,0:T(8,128)(2,1)S(1)} %get-tuple-element.52), channel_id=1, source_target_pairs={{0,2},{1,3},{2,0},{3,1},{4,6},{5,7},{6,4},{7,5},{8,10},{9,11},{10,... | collective-permute-start | bytes 196616 | tf_op jit(solution)/shard_map/ppermute | solution.py:39
  26.3 0.0 collective-permute-done.2.refs_1_
  26.3 1.0 %collective-permute-start.8 = (bf16[128,256]{1,0:T(8,128)(2,1)S(1)}, bf16[128,256]{1,0:T(8,128)(2,1)S(1)}, u32[]{:S(2)}, u32[]{:S(2)}) collective-permute-start(bf16[128,256]{1,0:T(8,128)(2,1)S(1)} %get-tuple-element.53), channel_id=1, source_target_pairs={{0,3},{1,2},{2,1},{3,0},{4,7},{5,6},{6,5},{7,4},{8,11},{9,10},{10,... | collective-permute-start | bytes 196616 | tf_op jit(solution)/shard_map/ppermute | solution.py:39
  27.3 0.0 collective-permute-done.3.refs_2_
  27.3 0.5 %collective-permute-start.9 = (bf16[128,256]{1,0:T(8,128)(2,1)S(1)}, bf16[128,256]{1,0:T(8,128)(2,1)S(1)}, u32[]{:S(2)}, u32[]{:S(2)}) collective-permute-start(bf16[128,256]{1,0:T(8,128)(2,1)S(1)} %get-tuple-element.54), channel_id=1, source_target_pairs={{0,1},{1,0},{2,3},{3,2},{4,5},{5,4},{6,7},{7,6},{8,9},{9,8},{10,11... | collective-permute-start | bytes 196616 | tf_op jit(solution)/shard_map/ppermute | solution.py:39
  27.8 1.3 %weigh.1.refs_0_ = bf16[2,4,256,256]{3,2,1,0:T(8,128)(2,1)S(1)} custom-call(s32[1,16]{1,0:T(1,128)S(1)} %get-tuple-element.32.facts_ref, bf16[512,512]{1,0:T(8,128)(2,1)S(1)} %get-tuple-element.58.q_ref, bf16[512,256]{1,0:T(8,128)(2,1)S(1)} %get-tuple-element.59.refs_0_), custom_call_target="tpu_custom_call" | custom-call | flops 1000 | bytes 1000 | tf_op jit(solution)/shard_map/weigh/pallas_call | solution.py:385
  29.1 0.0 collective-permute-done.4.refs_3_
  29.1 0.7 %collective-permute-done.7.refs_5_ = bf16[128,256]{1,0:T(8,128)(2,1)S(1)} collective-permute-done((bf16[128,256]{1,0:T(8,128)(2,1)S(1)}, bf16[128,256]{1,0:T(8,128)(2,1)S(1)}, u32[]{:S(2)}, u32[]{:S(2)}) %collective-permute-start.7) | collective-permute-done | bytes 65568 | tf_op jit(solution)/shard_map/ppermute | solution.py:39
  29.8 2.2 %collective-permute-done.8.refs_6_ = bf16[128,256]{1,0:T(8,128)(2,1)S(1)} collective-permute-done((bf16[128,256]{1,0:T(8,128)(2,1)S(1)}, bf16[128,256]{1,0:T(8,128)(2,1)S(1)}, u32[]{:S(2)}, u32[]{:S(2)}) %collective-permute-start.8) | collective-permute-done | bytes 65568 | tf_op jit(solution)/shard_map/ppermute | solution.py:39
  32.1 0.6 %collective-permute-done.9.refs_7_ = bf16[128,256]{1,0:T(8,128)(2,1)S(1)} collective-permute-done((bf16[128,256]{1,0:T(8,128)(2,1)S(1)}, bf16[128,256]{1,0:T(8,128)(2,1)S(1)}, u32[]{:S(2)}, u32[]{:S(2)}) %collective-permute-start.9) | collective-permute-done | bytes 65568 | tf_op jit(solution)/shard_map/ppermute | solution.py:39
  32.7 1.1 %cache_part.1 = (bf16[128,2048]{1,0:T(8,128)(2,1)}, f32[8,128]{1,0:T(8,128)S(1)}) custom-call(bf16[128,128]{1,0:T(8,128)(2,1)S(1)} %get-tuple-element.39.kept_ref, bf16[128,256]{1,0:T(8,128)(2,1)S(1)} %get-tuple-element.40.refs_0_, bf16[128,256]{1,0:T(8,128)(2,1)S(1)} %collective-permute-done.2.refs_1_, bf16[128,256]{1,0:T(8,128)(2,1)S(1)} %collective-permute-done.3.refs_2_, ...), custom_call_target="tpu_custom_call" | custom-call | flops 1000 | bytes 1000 | tf_op jit(solution)/shard_map/cache_part/pallas_call | solution.py:489
  33.8 0.0 collective-permute-done.10.refs_2_
  33.8 1.9 %attend.1 = bf16[512,512]{1,0:T(8,128)(2,1)} custom-call(s32[1,16]{1,0:T(1,128)S(1)} %get-tuple-element.32.facts_ref, f32[8,128]{1,0:T(8,128)S(1)} %get-tuple-element.55.mark_ref, f32[512,1024]{1,0:T(8,128)S(1)} %get-tuple-element.56.acc_ref, f32[512,128]{1,0:T(8,128)S(1)} %get-tuple-element.57.live_ref, bf16[2,4,256,256]{3,2,1,0:T(8,128)(2,1)S(1)} %weigh.1.refs_0_, ...), custom_call_target="tpu_custom_call" | custom-call | flops 1000 | bytes 1000 | tf_op jit(solution)/shard_map/attend/pallas_call | solution.py:460
  (1 shorter events, 0.0 us)
Async XLA Ops:
  0.6 19.9 %collective-permute-start.5 = (bf16[512,256]{1,0:T(8,128)(2,1)}, bf16[512,256]{1,0:T(8,128)(2,1)S(1)}, u32[]{:S(2)}, u32[]{:S(2)}) collective-permute-start(bf16[512,256]{1,0:T(8,128)(2,1)} %bitcast.8), channel_id=1, source_target_pairs={{0,4},{1,5},{2,6},{3,7},{4,0},{5,1},{6,2},{7,3},{8,12},{9,13},{10,... | collective-permute-start | bytes 786440 | tf_op jit(solution)/shard_map/ppermute | solution.py:34
  4.7 1.2 %collective-permute-start = (s32[1]{0:T(128)}, s32[1]{0:T(128)}, u32[]{:S(2)}, u32[]{:S(2)}) collective-permute-start(s32[1]{0:T(128)} %param.13), channel_id=1, source_target_pairs={{0,8},{8,0},{16,24},{24,16},{1,9},{9,1},{17,25},{25,17},{2,10},{10... | collective-permute-start | bytes 20 | tf_op jit(solution)/shard_map/ppermute | solution.py:39
  9.3 4.9 %collective-permute-start.1 = (s32[2]{0:T(128)S(1)}, s32[2]{0:T(128)S(1)}, u32[]{:S(2)}, u32[]{:S(2)}) collective-permute-start(s32[2]{0:T(128)S(1)} %get-tuple-element.33.here_ref), channel_id=1, source_target_pairs={{0,16},{8,24},{16,0},{24,8},{1,17},{9,25},{17,1},{25,9},{2,18},{10... | collective-permute-start | bytes 32 | tf_op jit(solution)/shard_map/ppermute | solution.py:39
  10.9 11.9 %collective-permute-start.6 = (bf16[256,256]{1,0:T(8,128)(2,1)S(1)}, bf16[256,256]{1,0:T(8,128)(2,1)S(1)}, u32[]{:S(2)}, u32[]{:S(2)}) collective-permute-start(bf16[256,256]{1,0:T(8,128)(2,1)S(1)} %get-tuple-element.50), channel_id=1, source_target_pairs={{0,4},{1,5},{2,6},{3,7},{4,0},{5,1},{6,2},{7,3},{8,12},{9,13},{10,... | collective-permute-start | bytes 393224 | tf_op jit(solution)/shard_map/ppermute | solution.py:34
  11.2 15.0 %collective-permute-start.2 = (bf16[128,256]{1,0:T(8,128)(2,1)S(1)}, bf16[128,256]{1,0:T(8,128)(2,1)S(1)}, u32[]{:S(2)}, u32[]{:S(2)}) collective-permute-start(bf16[128,256]{1,0:T(8,128)(2,1)S(1)} %get-tuple-element.41), channel_id=1, source_target_pairs={{0,2},{1,3},{2,0},{3,1},{4,6},{5,7},{6,4},{7,5},{8,10},{9,11},{10,... | collective-permute-start | bytes 196616 | tf_op jit(solution)/shard_map/ppermute | solution.py:39
  12.8 14.5 %collective-permute-start.3 = (bf16[128,256]{1,0:T(8,128)(2,1)S(1)}, bf16[128,256]{1,0:T(8,128)(2,1)S(1)}, u32[]{:S(2)}, u32[]{:S(2)}) collective-permute-start(bf16[128,256]{1,0:T(8,128)(2,1)S(1)} %get-tuple-element.42), channel_id=1, source_target_pairs={{0,3},{1,2},{2,1},{3,0},{4,7},{5,6},{6,5},{7,4},{8,11},{9,10},{10,... | collective-permute-start | bytes 196616 | tf_op jit(solution)/shard_map/ppermute | solution.py:39
  14.2 14.9 %collective-permute-start.4 = (bf16[128,256]{1,0:T(8,128)(2,1)S(1)}, bf16[128,256]{1,0:T(8,128)(2,1)S(1)}, u32[]{:S(2)}, u32[]{:S(2)}) collective-permute-start(bf16[128,256]{1,0:T(8,128)(2,1)S(1)} %get-tuple-element.43), channel_id=1, source_target_pairs={{0,1},{1,0},{2,3},{3,2},{4,5},{5,4},{6,7},{7,6},{8,9},{9,8},{10,11... | collective-permute-start | bytes 196616 | tf_op jit(solution)/shard_map/ppermute | solution.py:39
  20.5 13.2 %collective-permute-start.10 = (bf16[256,256]{1,0:T(8,128)(2,1)S(1)}, bf16[256,256]{1,0:T(8,128)(2,1)S(1)}, u32[]{:S(2)}, u32[]{:S(2)}) collective-permute-start(bf16[256,256]{1,0:T(8,128)(2,1)S(1)} %get-tuple-element.60), channel_id=1, source_target_pairs={{0,4},{1,5},{2,6},{3,7},{4,0},{5,1},{6,2},{7,3},{8,12},{9,13},{10,... | collective-permute-start | bytes 393224 | tf_op jit(solution)/shard_map/ppermute | solution.py:34
  22.8 7.1 %collective-permute-start.7 = (bf16[128,256]{1,0:T(8,128)(2,1)S(1)}, bf16[128,256]{1,0:T(8,128)(2,1)S(1)}, u32[]{:S(2)}, u32[]{:S(2)}) collective-permute-start(bf16[128,256]{1,0:T(8,128)(2,1)S(1)} %get-tuple-element.52), channel_id=1, source_target_pairs={{0,2},{1,3},{2,0},{3,1},{4,6},{5,7},{6,4},{7,5},{8,10},{9,11},{10,... | collective-permute-start | bytes 196616 | tf_op jit(solution)/shard_map/ppermute | solution.py:39
  26.3 5.8 %collective-permute-start.8 = (bf16[128,256]{1,0:T(8,128)(2,1)S(1)}, bf16[128,256]{1,0:T(8,128)(2,1)S(1)}, u32[]{:S(2)}, u32[]{:S(2)}) collective-permute-start(bf16[128,256]{1,0:T(8,128)(2,1)S(1)} %get-tuple-element.53), channel_id=1, source_target_pairs={{0,3},{1,2},{2,1},{3,0},{4,7},{5,6},{6,5},{7,4},{8,11},{9,10},{10,... | collective-permute-start | bytes 196616 | tf_op jit(solution)/shard_map/ppermute | solution.py:39
  27.3 5.4 %collective-permute-start.9 = (bf16[128,256]{1,0:T(8,128)(2,1)S(1)}, bf16[128,256]{1,0:T(8,128)(2,1)S(1)}, u32[]{:S(2)}, u32[]{:S(2)}) collective-permute-start(bf16[128,256]{1,0:T(8,128)(2,1)S(1)} %get-tuple-element.54), channel_id=1, source_target_pairs={{0,1},{1,0},{2,3},{3,2},{4,5},{5,4},{6,7},{7,6},{8,9},{9,8},{10,11... | collective-permute-start | bytes 196616 | tf_op jit(solution)/shard_map/ppermute | solution.py:39

commit v3 on v2

--- a/solution.py
+++ b/solution.py
@@ -360,14 +360,17 @@
     return outs[:others], outs[others]
 
 
-def weigh(facts_row, facts_of, query_rot, key_rot):
+def weigh(facts_row, facts_of, query_rot, key_rot, payload):
     others = len(key_rot)
     rows = query_rot.shape[0]
     block_len = rows // 2
     slots = facts_of(None).slots
 
     def body(facts_ref, q_ref, *refs):
-        k_refs, w_refs = refs[:others], refs[others:]
+        k_refs, pay_refs, refs = refs[:others], refs[others : 2 * others], refs[2 * others :]
+        w_refs, out_refs = refs[:others], refs[others:]
+        for pay_ref, out_ref in zip(pay_refs, out_refs):
+            out_ref[...] = pay_ref[...]
         facts = facts_of(facts_ref)
         slot = slot_and_head_group()[0]
         for turn in range(1, slots):
@@ -382,9 +385,11 @@
     shapes = [
         jax.ShapeDtypeStruct((2, Q_DEV, block_len, block_len), bf16) for _ in range(others)
     ]
-    return call(body, shapes, [SMEM] + [VMEM] * (1 + others), "weigh")(
-        facts_row, query_rot, *key_rot
-    )
+    shapes += [jax.ShapeDtypeStruct(x.shape, bf16) for x in payload]
+    outs = call(body, shapes, [SMEM] + [VMEM] * (1 + 2 * others), "weigh")(
+        facts_row, query_rot, *key_rot, *payload
+    )
+    return outs[:others], outs[others:]
 
 
 def late_pieces(heads, key_chosen):
@@ -514,8 +519,6 @@
         crossed(lengths, "req", 1),
     )
     heads = to_slots(sent[0::2])
-    tails, key_in = lax.optimization_barrier((sent[1::2], key_in))
-    tails = to_slots(tails)
     early = hand_on(early)
     span, groups = 2, lax.axis_size("req")
     while 2 * span < groups:
@@ -528,8 +531,9 @@
     lens = (block, crossed(block, "req", span))
     query_rot, acc, kept, live, angles = own_part(facts_row, facts_of, operands, tables, lens)
     key_rot, chosen = receive_keys(key_in, select, order, angles)
+    weights, tails = weigh(facts_row, facts_of, query_rot, key_rot, sent[1::2])
+    tails = to_slots(tails)
     late = hand_on(late_pieces(heads, chosen))
-    weights = weigh(facts_row, facts_of, query_rot, key_rot)
     cache, mark = cache_part(early, late, kept)
     attended = attend(facts_row, facts_of, weights, acc, heads, tails, live, mark)
     return (attended[None, None], cache[None])

time: 35.8 us -> 36.1 us (level)
  starting transfers between devices: 14.5 us -> 15.6 us
  waiting for transfers between devices: 9.4 us -> 8.63 us
    ppermute x3, waiting for transfers between devices: 5.27 us -> 3.81 us  [shifted(): lax.ppermute(shard, axis, [(i, (i + by) % peers) for i in range(peers)])]
    ppermute x8, starting transfers between devices: 10.1 us -> 11.1 us  [crossed(): return lax.ppermute(shard, axis, [(i, i ^ by) for i in range(peers)])]
    ppermute x8, waiting for transfers between devices: 4.13 us -> 4.82 us  [crossed(): return lax.ppermute(shard, axis, [(i, i ^ by) for i in range(peers)])]
  transfers between devices with their start and end apart: 11 -> 11, of which waited for: 6 -> 5; matrix products, arithmetic and copies ran while one was open for 0% -> 0% of each run, Pallas kernels for 24% -> 24%
where the time goes in v3:
time: 36.1 us; the launch traced here: 36 us
  starting transfers between devices  15.6 us (43%)
  Pallas kernels  10.4 us (29%)
  waiting for transfers between devices  8.63 us (24%)
  between operations  1.34 us (4%)
    ppermute x8, starting transfers between devices, crossed(): return lax.ppermute(shard, axis, [(i, i ^ by) for i in range(peers)])  11.1 us
    ppermute x8, waiting for transfers between devices, crossed(): return lax.ppermute(shard, axis, [(i, i ^ by) for i in range(peers)])  4.82 us
    ppermute x3, starting transfers between devices, shifted(): lax.ppermute(shard, axis, [(i, (i + by) % peers) for i in range(peers)])  4.51 us
    ppermute x3, waiting for transfers between devices, shifted(): lax.ppermute(shard, axis, [(i, (i + by) % peers) for i in range(peers)])  3.81 us
    pallas_call x1, Pallas kernels, prepare(): call(body, shapes, [SMEM] * 2 + [HBM] * count, 'prepare', scratch, out_sp...  3.36 us
    pallas_call x1, Pallas kernels, own_part(): call(body, shapes, [SMEM] * 3 + [VMEM] * 5, 'own_part')  2.35 us
    pallas_call x1, Pallas kernels, attend(): call(body, shape, specs, 'attend', scratch)  1.88 us
    pallas_call x1, Pallas kernels, weigh(): call(body, shapes, [SMEM] + [VMEM] * (1 + 2 * others), 'weigh')  1.28 us
  transfers between devices with their start and end apart: 11, of which 5 were waited for; matrix products, arithmetic and copies ran while one was open for 0% of the time, Pallas kernels for 24%

profile of v3, /device:TPU:0, one launch (start us, length us, event | category | flops | bytes accessed | tf_op | source)
XLA Modules:
  0.0 36.0 jit_solution(10685390910064999320)
XLA Ops:
  0.6 4.1 %collective-permute-start.5 = (bf16[512,256]{1,0:T(8,128)(2,1)}, bf16[512,256]{1,0:T(8,128)(2,1)S(1)}, u32[]{:S(2)}, u32[]{:S(2)}) collective-permute-start(bf16[512,256]{1,0:T(8,128)(2,1)} %bitcast.8), channel_id=1, source_target_pairs={{0,4},{1,5},{2,6},{3,7},{4,0},{5,1},{6,2},{7,3},{8,12},{9,13},{10,... | collective-permute-start | bytes 786440 | tf_op jit(solution)/shard_map/ppermute | solution.py:34
  4.7 0.0 collective-permute-start
  5.4 0.7 %collective-permute-done.near_ref = s32[1]{0:T(128)} collective-permute-done((s32[1]{0:T(128)}, s32[1]{0:T(128)}, u32[]{:S(2)}, u32[]{:S(2)}) %collective-permute-start) | collective-permute-done | bytes 36 | tf_op jit(solution)/shard_map/ppermute | solution.py:39
  6.1 3.4 %prepare.1 = (s32[1,16]{1,0:T(1,128)S(1)}, s32[2]{0:T(128)S(1)}, bf16[512,512]{1,0:T(8,128)(2,1)S(1)}, bf16[512,256]{1,0:T(8,128)(2,1)S(1)}, bf16[512,256]{1,0:T...) custom-call(s32[1]{0:T(128)S(6)} %copy.11.own_ref, ...), custom_call_target="tpu_custom_call" | custom-call | flops 1000 | bytes 1000 | tf_op jit(solution)/shard_map/prepare/pallas_call | solution.py:235
  9.5 1.6 %collective-permute-start.1 = (s32[2]{0:T(128)S(1)}, s32[2]{0:T(128)S(1)}, u32[]{:S(2)}, u32[]{:S(2)}) collective-permute-start(s32[2]{0:T(128)S(1)} %get-tuple-element.33.here_ref), channel_id=1, source_target_pairs={{0,16},{8,24},{16,0},{24,8},{1,17},{9,25},{17,1},{25,9},{2,18},{10... | collective-permute-start | bytes 32 | tf_op jit(solution)/shard_map/ppermute | solution.py:39
  11.0 0.3 collective-permute-start.6
  11.4 1.6 %collective-permute-start.2 = (bf16[128,256]{1,0:T(8,128)(2,1)S(1)}, bf16[128,256]{1,0:T(8,128)(2,1)S(1)}, u32[]{:S(2)}, u32[]{:S(2)}) collective-permute-start(bf16[128,256]{1,0:T(8,128)(2,1)S(1)} %get-tuple-element.41), channel_id=1, source_target_pairs={{0,2},{1,3},{2,0},{3,1},{4,6},{5,7},{6,4},{7,5},{8,10},{9,11},{10,... | collective-permute-start | bytes 196616 | tf_op jit(solution)/shard_map/ppermute | solution.py:39
  13.0 1.4 %collective-permute-start.3 = (bf16[128,256]{1,0:T(8,128)(2,1)S(1)}, bf16[128,256]{1,0:T(8,128)(2,1)S(1)}, u32[]{:S(2)}, u32[]{:S(2)}) collective-permute-start(bf16[128,256]{1,0:T(8,128)(2,1)S(1)} %get-tuple-element.42), channel_id=1, source_target_pairs={{0,3},{1,2},{2,1},{3,0},{4,7},{5,6},{6,5},{7,4},{8,11},{9,10},{10,... | collective-permute-start | bytes 196616 | tf_op jit(solution)/shard_map/ppermute | solution.py:39
  14.4 0.0 collective-permute-done.1.there_ref
  14.4 2.4 %own_part.1 = (bf16[512,512]{1,0:T(8,128)(2,1)S(1)}, f32[512,1024]{1,0:T(8,128)S(1)}, bf16[128,128]{1,0:T(8,128)(2,1)S(1)}, f32[512,128]{1,0:T(8,128)S(1)}, f32[1,2,2,256,128]{4,3,2,1,0:T(8,128)S(1)}) custom-call(s32[1,16]{1,0:T(1,128)S(1)} %get-tuple-element.32.facts_ref, s32[2]{0:T(128)S(1)} %get-tuple-element.33.here_ref, ...), custom_call_target="tpu_custom_call" | custom-call | flops 1000 | bytes 1000 | tf_op jit(solution)/shard_map/own_part/pallas_call | solution.py:321
  16.7 3.8 %collective-permute-done.5.refs_0_ = bf16[512,256]{1,0:T(8,128)(2,1)S(1)} collective-permute-done((bf16[512,256]{1,0:T(8,128)(2,1)}, bf16[512,256]{1,0:T(8,128)(2,1)S(1)}, u32[]{:S(2)}, u32[]{:S(2)}) %collective-permute-start.5) | collective-permute-done | bytes 262176 | tf_op jit(solution)/shard_map/ppermute | solution.py:34
  20.5 0.4 %receive_keys.1 = (bf16[512,256]{1,0:T(8,128)(2,1)S(1)}, bf16[1,256,256]{2,1,0:T(8,128)(2,1)S(1)}) custom-call(bf16[256,512]{1,0:T(8,128)(2,1)S(1)} %get-tuple-element.44.select_ref, bf16[256,256]{1,0:T(8,128)(2,1)S(1)} %get-tuple-element.45.order_ref, f32[1,2,2,256,128]{4,3,2,1,0:T(8,128)S(1)} %get-tuple-element.46.angle_ref, ...), custom_call_target="tpu_custom_call" | custom-call | flops 10000000000 | bytes 1000 | tf_op jit(solution)/shard_map/receive_keys/pallas_call | solution.py:357
  21.0 1.3 %weigh.1 = (bf16[2,4,256,256]{3,2,1,0:T(8,128)(2,1)S(1)}, bf16[256,256]{1,0:T(8,128)(2,1)S(1)}) custom-call(s32[1,16]{1,0:T(1,128)S(1)} %get-tuple-element.32.facts_ref, bf16[512,512]{1,0:T(8,128)(2,1)S(1)} %get-tuple-element.56.q_ref, bf16[512,256]{1,0:T(8,128)(2,1)S(1)} %get-tuple-element.57.refs_0_, bf16[256,256]{1,0:T(8,128)(2,1)S(1)} %get-tuple-element.58.refs_1_), custom_call_target="tpu_custom_call" | custom-call | flops 1000 | bytes 1000 | tf_op jit(solution)/shard_map/weigh/pallas_call | solution.py:389
  22.3 0.1 collective-permute-start.10
  22.3 1.9 %collective-permute-start.4 = (bf16[128,256]{1,0:T(8,128)(2,1)S(1)}, bf16[128,256]{1,0:T(8,128)(2,1)S(1)}, u32[]{:S(2)}, u32[]{:S(2)}) collective-permute-start(bf16[128,256]{1,0:T(8,128)(2,1)S(1)} %get-tuple-element.43), channel_id=1, source_target_pairs={{0,1},{1,0},{2,3},{3,2},{4,5},{5,4},{6,7},{7,6},{8,9},{9,8},{10,11... | collective-permute-start | bytes 196616 | tf_op jit(solution)/shard_map/ppermute | solution.py:39
  24.3 0.0 collective-permute-done.6.refs_0_.refs_1_
  24.3 3.1 %collective-permute-start.7 = (bf16[128,256]{1,0:T(8,128)(2,1)S(1)}, bf16[128,256]{1,0:T(8,128)(2,1)S(1)}, u32[]{:S(2)}, u32[]{:S(2)}) collective-permute-start(bf16[128,256]{1,0:T(8,128)(2,1)S(1)} %get-tuple-element.50), channel_id=1, source_target_pairs={{0,2},{1,3},{2,0},{3,1},{4,6},{5,7},{6,4},{7,5},{8,10},{9,11},{10,... | collective-permute-start | bytes 196616 | tf_op jit(solution)/shard_map/ppermute | solution.py:39
  27.4 0.0 collective-permute-done.2.refs_1_
  27.4 0.0 collective-permute-start.8
  27.4 0.0 collective-permute-done.3.refs_2_
  27.4 1.5 %collective-permute-start.9 = (bf16[128,256]{1,0:T(8,128)(2,1)S(1)}, bf16[128,256]{1,0:T(8,128)(2,1)S(1)}, u32[]{:S(2)}, u32[]{:S(2)}) collective-permute-start(bf16[128,256]{1,0:T(8,128)(2,1)S(1)} %get-tuple-element.52), channel_id=1, source_target_pairs={{0,1},{1,0},{2,3},{3,2},{4,5},{5,4},{6,7},{7,6},{8,9},{9,8},{10,11... | collective-permute-start | bytes 196616 | tf_op jit(solution)/shard_map/ppermute | solution.py:39
  28.9 0.0 collective-permute-done.4.refs_3_
  28.9 2.6 %collective-permute-done.7.refs_5_ = bf16[128,256]{1,0:T(8,128)(2,1)S(1)} collective-permute-done((bf16[128,256]{1,0:T(8,128)(2,1)S(1)}, bf16[128,256]{1,0:T(8,128)(2,1)S(1)}, u32[]{:S(2)}, u32[]{:S(2)}) %collective-permute-start.7) | collective-permute-done | bytes 65568 | tf_op jit(solution)/shard_map/ppermute | solution.py:39
  31.5 1.1 %collective-permute-done.8.refs_6_ = bf16[128,256]{1,0:T(8,128)(2,1)S(1)} collective-permute-done((bf16[128,256]{1,0:T(8,128)(2,1)S(1)}, bf16[128,256]{1,0:T(8,128)(2,1)S(1)}, u32[]{:S(2)}, u32[]{:S(2)}) %collective-permute-start.8) | collective-permute-done | bytes 65568 | tf_op jit(solution)/shard_map/ppermute | solution.py:39
  32.6 0.4 %collective-permute-done.9.refs_7_ = bf16[128,256]{1,0:T(8,128)(2,1)S(1)} collective-permute-done((bf16[128,256]{1,0:T(8,128)(2,1)S(1)}, bf16[128,256]{1,0:T(8,128)(2,1)S(1)}, u32[]{:S(2)}, u32[]{:S(2)}) %collective-permute-start.9) | collective-permute-done | bytes 65568 | tf_op jit(solution)/shard_map/ppermute | solution.py:39
  33.0 1.1 %cache_part.1 = (bf16[128,2048]{1,0:T(8,128)(2,1)}, f32[8,128]{1,0:T(8,128)S(1)}) custom-call(bf16[128,128]{1,0:T(8,128)(2,1)S(1)} %get-tuple-element.39.kept_ref, bf16[128,256]{1,0:T(8,128)(2,1)S(1)} %get-tuple-element.40.refs_0_, bf16[128,256]{1,0:T(8,128)(2,1)S(1)} %collective-permute-done.2.refs_1_, bf16[128,256]{1,0:T(8,128)(2,1)S(1)} %collective-permute-done.3.refs_2_, ...), custom_call_target="tpu_custom_call" | custom-call | flops 1000 | bytes 1000 | tf_op jit(solution)/shard_map/cache_part/pallas_call | solution.py:494
  34.1 0.0 collective-permute-done.10.refs_2_
  34.1 1.9 %attend.1 = bf16[512,512]{1,0:T(8,128)(2,1)} custom-call(s32[1,16]{1,0:T(1,128)S(1)} %get-tuple-element.32.facts_ref, f32[8,128]{1,0:T(8,128)S(1)} %get-tuple-element.53.mark_ref, f32[512,1024]{1,0:T(8,128)S(1)} %get-tuple-element.54.acc_ref, f32[512,128]{1,0:T(8,128)S(1)} %get-tuple-element.55.live_ref, ...), custom_call_target="tpu_custom_call" | custom-call | flops 1000 | bytes 1000 | tf_op jit(solution)/shard_map/attend/pallas_call | solution.py:465
  (1 shorter events, 0.0 us)
Async XLA Ops:
  0.6 19.9 %collective-permute-start.5 = (bf16[512,256]{1,0:T(8,128)(2,1)}, bf16[512,256]{1,0:T(8,128)(2,1)S(1)}, u32[]{:S(2)}, u32[]{:S(2)}) collective-permute-start(bf16[512,256]{1,0:T(8,128)(2,1)} %bitcast.8), channel_id=1, source_target_pairs={{0,4},{1,5},{2,6},{3,7},{4,0},{5,1},{6,2},{7,3},{8,12},{9,13},{10,... | collective-permute-start | bytes 786440 | tf_op jit(solution)/shard_map/ppermute | solution.py:34
  4.7 1.4 %collective-permute-start = (s32[1]{0:T(128)}, s32[1]{0:T(128)}, u32[]{:S(2)}, u32[]{:S(2)}) collective-permute-start(s32[1]{0:T(128)} %param.13), channel_id=1, source_target_pairs={{0,8},{8,0},{16,24},{24,16},{1,9},{9,1},{17,25},{25,17},{2,10},{10... | collective-permute-start | bytes 20 | tf_op jit(solution)/shard_map/ppermute | solution.py:39
  9.5 4.9 %collective-permute-start.1 = (s32[2]{0:T(128)S(1)}, s32[2]{0:T(128)S(1)}, u32[]{:S(2)}, u32[]{:S(2)}) collective-permute-start(s32[2]{0:T(128)S(1)} %get-tuple-element.33.here_ref), channel_id=1, source_target_pairs={{0,16},{8,24},{16,0},{24,8},{1,17},{9,25},{17,1},{25,9},{2,18},{10... | collective-permute-start | bytes 32 | tf_op jit(solution)/shard_map/ppermute | solution.py:39
  11.0 13.2 %collective-permute-start.6 = (bf16[256,256]{1,0:T(8,128)(2,1)S(1)}, bf16[256,256]{1,0:T(8,128)(2,1)S(1)}, u32[]{:S(2)}, u32[]{:S(2)}) collective-permute-start(bf16[256,256]{1,0:T(8,128)(2,1)S(1)} %get-tuple-element.48), channel_id=1, source_target_pairs={{0,4},{1,5},{2,6},{3,7},{4,0},{5,1},{6,2},{7,3},{8,12},{9,13},{10,... | collective-permute-start | bytes 393224 | tf_op jit(solution)/shard_map/ppermute | solution.py:34
  11.4 16.0 %collective-permute-start.2 = (bf16[128,256]{1,0:T(8,128)(2,1)S(1)}, bf16[128,256]{1,0:T(8,128)(2,1)S(1)}, u32[]{:S(2)}, u32[]{:S(2)}) collective-permute-start(bf16[128,256]{1,0:T(8,128)(2,1)S(1)} %get-tuple-element.41), channel_id=1, source_target_pairs={{0,2},{1,3},{2,0},{3,1},{4,6},{5,7},{6,4},{7,5},{8,10},{9,11},{10,... | collective-permute-start | bytes 196616 | tf_op jit(solution)/shard_map/ppermute | solution.py:39
  13.0 14.4 %collective-permute-start.3 = (bf16[128,256]{1,0:T(8,128)(2,1)S(1)}, bf16[128,256]{1,0:T(8,128)(2,1)S(1)}, u32[]{:S(2)}, u32[]{:S(2)}) collective-permute-start(bf16[128,256]{1,0:T(8,128)(2,1)S(1)} %get-tuple-element.42), channel_id=1, source_target_pairs={{0,3},{1,2},{2,1},{3,0},{4,7},{5,6},{6,5},{7,4},{8,11},{9,10},{10,... | collective-permute-start | bytes 196616 | tf_op jit(solution)/shard_map/ppermute | solution.py:39
  22.3 11.8 %collective-permute-start.10 = (bf16[256,256]{1,0:T(8,128)(2,1)S(1)}, bf16[256,256]{1,0:T(8,128)(2,1)S(1)}, u32[]{:S(2)}, u32[]{:S(2)}) collective-permute-start(bf16[256,256]{1,0:T(8,128)(2,1)S(1)} %get-tuple-element.60), channel_id=1, source_target_pairs={{0,4},{1,5},{2,6},{3,7},{4,0},{5,1},{6,2},{7,3},{8,12},{9,13},{10,... | collective-permute-start | bytes 393224 | tf_op jit(solution)/shard_map/ppermute | solution.py:34
  22.3 6.6 %collective-permute-start.4 = (bf16[128,256]{1,0:T(8,128)(2,1)S(1)}, bf16[128,256]{1,0:T(8,128)(2,1)S(1)}, u32[]{:S(2)}, u32[]{:S(2)}) collective-permute-start(bf16[128,256]{1,0:T(8,128)(2,1)S(1)} %get-tuple-element.43), channel_id=1, source_target_pairs={{0,1},{1,0},{2,3},{3,2},{4,5},{5,4},{6,7},{7,6},{8,9},{9,8},{10,11... | collective-permute-start | bytes 196616 | tf_op jit(solution)/shard_map/ppermute | solution.py:39
  24.3 7.2 %collective-permute-start.7 = (bf16[128,256]{1,0:T(8,128)(2,1)S(1)}, bf16[128,256]{1,0:T(8,128)(2,1)S(1)}, u32[]{:S(2)}, u32[]{:S(2)}) collective-permute-start(bf16[128,256]{1,0:T(8,128)(2,1)S(1)} %get-tuple-element.50), channel_id=1, source_target_pairs={{0,2},{1,3},{2,0},{3,1},{4,6},{5,7},{6,4},{7,5},{8,10},{9,11},{10,... | collective-permute-start | bytes 196616 | tf_op jit(solution)/shard_map/ppermute | solution.py:39
  27.4 5.2 %collective-permute-start.8 = (bf16[128,256]{1,0:T(8,128)(2,1)S(1)}, bf16[128,256]{1,0:T(8,128)(2,1)S(1)}, u32[]{:S(2)}, u32[]{:S(2)}) collective-permute-start(bf16[128,256]{1,0:T(8,128)(2,1)S(1)} %get-tuple-element.51), channel_id=1, source_target_pairs={{0,3},{1,2},{2,1},{3,0},{4,7},{5,6},{6,5},{7,4},{8,11},{9,10},{10,... | collective-permute-start | bytes 196616 | tf_op jit(solution)/shard_map/ppermute | solution.py:39
  27.4 5.6 %collective-permute-start.9 = (bf16[128,256]{1,0:T(8,128)(2,1)S(1)}, bf16[128,256]{1,0:T(8,128)(2,1)S(1)}, u32[]{:S(2)}, u32[]{:S(2)}) collective-permute-start(bf16[128,256]{1,0:T(8,128)(2,1)S(1)} %get-tuple-element.52), channel_id=1, source_target_pairs={{0,1},{1,0},{2,3},{3,2},{4,5},{5,4},{6,7},{7,6},{8,9},{9,8},{10,11... | collective-permute-start | bytes 196616 | tf_op jit(solution)/shard_map/ppermute | solution.py:39

commit v4 on v3

--- a/solution.py
+++ b/solution.py
@@ -360,13 +360,13 @@
     return outs[:others], outs[others]
 
 
-def weigh(facts_row, facts_of, query_rot, key_rot, payload):
+def weigh(facts_row, facts_of, query_rot, key_rot, payload, after):
     others = len(key_rot)
     rows = query_rot.shape[0]
     block_len = rows // 2
     slots = facts_of(None).slots
 
-    def body(facts_ref, q_ref, *refs):
+    def body(facts_ref, _, q_ref, *refs):
         k_refs, pay_refs, refs = refs[:others], refs[others : 2 * others], refs[2 * others :]
         w_refs, out_refs = refs[:others], refs[others:]
         for pay_ref, out_ref in zip(pay_refs, out_refs):
@@ -386,8 +386,8 @@
         jax.ShapeDtypeStruct((2, Q_DEV, block_len, block_len), bf16) for _ in range(others)
     ]
     shapes += [jax.ShapeDtypeStruct(x.shape, bf16) for x in payload]
-    outs = call(body, shapes, [SMEM] + [VMEM] * (1 + 2 * others), "weigh")(
-        facts_row, query_rot, *key_rot, *payload
+    outs = call(body, shapes, [SMEM] + [VMEM] * (2 + 2 * others), "weigh")(
+        facts_row, after, query_rot, *key_rot, *payload
     )
     return outs[:others], outs[others:]
 
@@ -531,7 +531,9 @@
     lens = (block, crossed(block, "req", span))
     query_rot, acc, kept, live, angles = own_part(facts_row, facts_of, operands, tables, lens)
     key_rot, chosen = receive_keys(key_in, select, order, angles)
-    weights, tails = weigh(facts_row, facts_of, query_rot, key_rot, sent[1::2])
+    weights, tails = weigh(
+        facts_row, facts_of, query_rot, key_rot, sent[1::2], early[-1]
+    )
     tails = to_slots(tails)
     late = hand_on(late_pieces(heads, chosen))
     cache, mark = cache_part(early, late, kept)

time: 36.1 us -> 36.9 us (1.022)
  starting transfers between devices: 15.6 us -> 17.1 us
  waiting for transfers between devices: 8.63 us -> 7.91 us
    ppermute x8, starting transfers between devices: 11.1 us -> 12.6 us  [crossed(): return lax.ppermute(shard, axis, [(i, i ^ by) for i in range(peers)])]
    ppermute x8, waiting for transfers between devices: 4.82 us -> 4.24 us  [crossed(): return lax.ppermute(shard, axis, [(i, i ^ by) for i in range(peers)])]
  transfers between devices with their start and end apart: 11 -> 11, of which waited for: 5 -> 5; matrix products, arithmetic and copies ran while one was open for 0% -> 0% of each run, Pallas kernels for 24% -> 23%
where the time goes in v4:
time: 36.9 us; the launch traced here: 36.8 us
  starting transfers between devices  17.1 us (46%)
  Pallas kernels  10.4 us (28%)
  waiting for transfers between devices  7.91 us (21%)
  between operations  1.35 us (4%)
    ppermute x8, starting transfers between devices, crossed(): return lax.ppermute(shard, axis, [(i, i ^ by) for i in range(peers)])  12.6 us
    ppermute x3, starting transfers between devices, shifted(): lax.ppermute(shard, axis, [(i, (i + by) % peers) for i in range(peers)])  4.51 us
    ppermute x8, waiting for transfers between devices, crossed(): return lax.ppermute(shard, axis, [(i, i ^ by) for i in range(peers)])  4.24 us
    ppermute x3, waiting for transfers between devices, shifted(): lax.ppermute(shard, axis, [(i, (i + by) % peers) for i in range(peers)])  3.68 us
    pallas_call x1, Pallas kernels, prepare(): call(body, shapes, [SMEM] * 2 + [HBM] * count, 'prepare', scratch, out_sp...  3.36 us
    pallas_call x1, Pallas kernels, own_part(): call(body, shapes, [SMEM] * 3 + [VMEM] * 5, 'own_part')  2.38 us
    pallas_call x1, Pallas kernels, attend(): call(body, shape, specs, 'attend', scratch)  1.88 us
    pallas_call x1, Pallas kernels, weigh(): call(body, shapes, [SMEM] + [VMEM] * (2 + 2 * others), 'weigh')  1.28 us
  transfers between devices with their start and end apart: 11, of which 5 were waited for; matrix products, arithmetic and copies ran while one was open for 0% of the time, Pallas kernels for 23%

profile of v4, /device:TPU:0, one launch (start us, length us, event | category | flops | bytes accessed | tf_op | source)
XLA Modules:
  0.0 36.8 jit_solution(8374845542739184892)
XLA Ops:
  0.6 4.1 %collective-permute-start.5 = (bf16[512,256]{1,0:T(8,128)(2,1)}, bf16[512,256]{1,0:T(8,128)(2,1)S(1)}, u32[]{:S(2)}, u32[]{:S(2)}) collective-permute-start(bf16[512,256]{1,0:T(8,128)(2,1)} %bitcast.8), channel_id=1, source_target_pairs={{0,4},{1,5},{2,6},{3,7},{4,0},{5,1},{6,2},{7,3},{8,12},{9,13},{10,... | collective-permute-start | bytes 786440 | tf_op jit(solution)/shard_map/ppermute | solution.py:34
  4.7 0.0 collective-permute-start
  5.4 0.7 %collective-permute-done.near_ref = s32[1]{0:T(128)} collective-permute-done((s32[1]{0:T(128)}, s32[1]{0:T(128)}, u32[]{:S(2)}, u32[]{:S(2)}) %collective-permute-start) | collective-permute-done | bytes 36 | tf_op jit(solution)/shard_map/ppermute | solution.py:39
  6.1 3.4 %prepare.1 = (s32[1,16]{1,0:T(1,128)S(1)}, s32[2]{0:T(128)S(1)}, bf16[512,512]{1,0:T(8,128)(2,1)S(1)}, bf16[512,256]{1,0:T(8,128)(2,1)S(1)}, bf16[512,256]{1,0:T...) custom-call(s32[1]{0:T(128)S(6)} %copy.11.own_ref, ...), custom_call_target="tpu_custom_call" | custom-call | flops 1000 | bytes 1000 | tf_op jit(solution)/shard_map/prepare/pallas_call | solution.py:235
  9.5 1.6 %collective-permute-start.1 = (s32[2]{0:T(128)S(1)}, s32[2]{0:T(128)S(1)}, u32[]{:S(2)}, u32[]{:S(2)}) collective-permute-start(s32[2]{0:T(128)S(1)} %get-tuple-element.33.here_ref), channel_id=1, source_target_pairs={{0,16},{8,24},{16,0},{24,8},{1,17},{9,25},{17,1},{25,9},{2,18},{10... | collective-permute-start | bytes 32 | tf_op jit(solution)/shard_map/ppermute | solution.py:39
  11.1 1.5 %collective-permute-start.4 = (bf16[128,256]{1,0:T(8,128)(2,1)S(1)}, bf16[128,256]{1,0:T(8,128)(2,1)S(1)}, u32[]{:S(2)}, u32[]{:S(2)}) collective-permute-start(bf16[128,256]{1,0:T(8,128)(2,1)S(1)} %get-tuple-element.43), channel_id=1, source_target_pairs={{0,1},{1,0},{2,3},{3,2},{4,5},{5,4},{6,7},{7,6},{8,9},{9,8},{10,11... | collective-permute-start | bytes 196616 | tf_op jit(solution)/shard_map/ppermute | solution.py:39
  12.6 0.3 collective-permute-start.6
  12.9 1.6 %collective-permute-start.2 = (bf16[128,256]{1,0:T(8,128)(2,1)S(1)}, bf16[128,256]{1,0:T(8,128)(2,1)S(1)}, u32[]{:S(2)}, u32[]{:S(2)}) collective-permute-start(bf16[128,256]{1,0:T(8,128)(2,1)S(1)} %get-tuple-element.41), channel_id=1, source_target_pairs={{0,2},{1,3},{2,0},{3,1},{4,6},{5,7},{6,4},{7,5},{8,10},{9,11},{10,... | collective-permute-start | bytes 196616 | tf_op jit(solution)/shard_map/ppermute | solution.py:39
  14.5 0.0 collective-permute-done.1.there_ref
  14.5 2.4 %own_part.1 = (bf16[512,512]{1,0:T(8,128)(2,1)S(1)}, f32[512,1024]{1,0:T(8,128)S(1)}, bf16[128,128]{1,0:T(8,128)(2,1)S(1)}, f32[512,128]{1,0:T(8,128)S(1)}, f32[1,2,2,256,128]{4,3,2,1,0:T(8,128)S(1)}) custom-call(s32[1,16]{1,0:T(1,128)S(1)} %get-tuple-element.32.facts_ref, s32[2]{0:T(128)S(1)} %get-tuple-element.33.here_ref, ...), custom_call_target="tpu_custom_call" | custom-call | flops 1000 | bytes 1000 | tf_op jit(solution)/shard_map/own_part/pallas_call | solution.py:321
  16.9 3.7 %collective-permute-done.5.refs_0_ = bf16[512,256]{1,0:T(8,128)(2,1)S(1)} collective-permute-done((bf16[512,256]{1,0:T(8,128)(2,1)}, bf16[512,256]{1,0:T(8,128)(2,1)S(1)}, u32[]{:S(2)}, u32[]{:S(2)}) %collective-permute-start.5) | collective-permute-done | bytes 262176 | tf_op jit(solution)/shard_map/ppermute | solution.py:34
  20.5 0.4 %receive_keys.1 = (bf16[512,256]{1,0:T(8,128)(2,1)S(1)}, bf16[1,256,256]{2,1,0:T(8,128)(2,1)S(1)}) custom-call(bf16[256,512]{1,0:T(8,128)(2,1)S(1)} %get-tuple-element.44.select_ref, bf16[256,256]{1,0:T(8,128)(2,1)S(1)} %get-tuple-element.45.order_ref, f32[1,2,2,256,128]{4,3,2,1,0:T(8,128)S(1)} %get-tuple-element.46.angle_ref, ...), custom_call_target="tpu_custom_call" | custom-call | flops 10000000000 | bytes 1000 | tf_op jit(solution)/shard_map/receive_keys/pallas_call | solution.py:357
  21.0 0.0 collective-permute-done.4.refs_3_._
  21.0 1.3 %weigh.1 = (bf16[2,4,256,256]{3,2,1,0:T(8,128)(2,1)S(1)}, bf16[256,256]{1,0:T(8,128)(2,1)S(1)}) custom-call(s32[1,16]{1,0:T(1,128)S(1)} %get-tuple-element.32.facts_ref, bf16[128,256]{1,0:T(8,128)(2,1)S(1)} %collective-permute-done.4.refs_3_._, bf16[512,512]{1,0:T(8,128)(2,1)S(1)} %get-tuple-element.56.q_ref, ...), custom_call_target="tpu_custom_call" | custom-call | flops 1000 | bytes 1000 | tf_op jit(solution)/shard_map/weigh/pallas_call | solution.py:389
  22.3 0.1 collective-permute-start.10
  22.4 4.4 %collective-permute-start.3 = (bf16[128,256]{1,0:T(8,128)(2,1)S(1)}, bf16[128,256]{1,0:T(8,128)(2,1)S(1)}, u32[]{:S(2)}, u32[]{:S(2)}) collective-permute-start(bf16[128,256]{1,0:T(8,128)(2,1)S(1)} %get-tuple-element.42), channel_id=1, source_target_pairs={{0,3},{1,2},{2,1},{3,0},{4,7},{5,6},{6,5},{7,4},{8,11},{9,10},{10,... | collective-permute-start | bytes 196616 | tf_op jit(solution)/shard_map/ppermute | solution.py:39
  26.7 0.0 collective-permute-done.6.refs_0_.refs_1_
  26.7 0.1 collective-permute-start.7
  26.8 2.0 %collective-permute-start.8 = (bf16[128,256]{1,0:T(8,128)(2,1)S(1)}, bf16[128,256]{1,0:T(8,128)(2,1)S(1)}, u32[]{:S(2)}, u32[]{:S(2)}) collective-permute-start(bf16[128,256]{1,0:T(8,128)(2,1)S(1)} %get-tuple-element.51), channel_id=1, source_target_pairs={{0,3},{1,2},{2,1},{3,0},{4,7},{5,6},{6,5},{7,4},{8,11},{9,10},{10,... | collective-permute-start | bytes 196616 | tf_op jit(solution)/shard_map/ppermute | solution.py:39
  28.8 0.0 collective-permute-done.2.refs_1_
  28.8 1.5 %collective-permute-start.9 = (bf16[128,256]{1,0:T(8,128)(2,1)S(1)}, bf16[128,256]{1,0:T(8,128)(2,1)S(1)}, u32[]{:S(2)}, u32[]{:S(2)}) collective-permute-start(bf16[128,256]{1,0:T(8,128)(2,1)S(1)} %get-tuple-element.52), channel_id=1, source_target_pairs={{0,1},{1,0},{2,3},{3,2},{4,5},{5,4},{6,7},{7,6},{8,9},{9,8},{10,11... | collective-permute-start | bytes 196616 | tf_op jit(solution)/shard_map/ppermute | solution.py:39
  30.3 0.0 collective-permute-done.3.refs_2_
  30.3 1.5 %collective-permute-done.7.refs_5_ = bf16[128,256]{1,0:T(8,128)(2,1)S(1)} collective-permute-done((bf16[128,256]{1,0:T(8,128)(2,1)S(1)}, bf16[128,256]{1,0:T(8,128)(2,1)S(1)}, u32[]{:S(2)}, u32[]{:S(2)}) %collective-permute-start.7) | collective-permute-done | bytes 65568 | tf_op jit(solution)/shard_map/ppermute | solution.py:39
  31.8 1.4 %collective-permute-done.8.refs_6_ = bf16[128,256]{1,0:T(8,128)(2,1)S(1)} collective-permute-done((bf16[128,256]{1,0:T(8,128)(2,1)S(1)}, bf16[128,256]{1,0:T(8,128)(2,1)S(1)}, u32[]{:S(2)}, u32[]{:S(2)}) %collective-permute-start.8) | collective-permute-done | bytes 65568 | tf_op jit(solution)/shard_map/ppermute | solution.py:39
  33.3 0.5 %collective-permute-done.9.refs_7_ = bf16[128,256]{1,0:T(8,128)(2,1)S(1)} collective-permute-done((bf16[128,256]{1,0:T(8,128)(2,1)S(1)}, bf16[128,256]{1,0:T(8,128)(2,1)S(1)}, u32[]{:S(2)}, u32[]{:S(2)}) %collective-permute-start.9) | collective-permute-done | bytes 65568 | tf_op jit(solution)/shard_map/ppermute | solution.py:39
  33.8 1.1 %cache_part.1 = (bf16[128,2048]{1,0:T(8,128)(2,1)}, f32[8,128]{1,0:T(8,128)S(1)}) custom-call(bf16[128,128]{1,0:T(8,128)(2,1)S(1)} %get-tuple-element.39.kept_ref, bf16[128,256]{1,0:T(8,128)(2,1)S(1)} %get-tuple-element.40.refs_0_, bf16[128,256]{1,0:T(8,128)(2,1)S(1)} %collective-permute-done.2.refs_1_, bf16[128,256]{1,0:T(8,128)(2,1)S(1)} %collective-permute-done.3.refs_2_, ...), custom_call_target="tpu_custom_call" | custom-call | flops 1000 | bytes 1000 | tf_op jit(solution)/shard_map/cache_part/pallas_call | solution.py:494
  34.9 0.0 collective-permute-done.10.refs_2_
  34.9 1.9 %attend.1 = bf16[512,512]{1,0:T(8,128)(2,1)} custom-call(s32[1,16]{1,0:T(1,128)S(1)} %get-tuple-element.32.facts_ref, f32[8,128]{1,0:T(8,128)S(1)} %get-tuple-element.53.mark_ref, f32[512,1024]{1,0:T(8,128)S(1)} %get-tuple-element.54.acc_ref, f32[512,128]{1,0:T(8,128)S(1)} %get-tuple-element.55.live_ref, ...), custom_call_target="tpu_custom_call" | custom-call | flops 1000 | bytes 1000 | tf_op jit(solution)/shard_map/attend/pallas_call | solution.py:465
  (1 shorter events, 0.0 us)
Async XLA Ops:
  0.6 19.9 %collective-permute-start.5 = (bf16[512,256]{1,0:T(8,128)(2,1)}, bf16[512,256]{1,0:T(8,128)(2,1)S(1)}, u32[]{:S(2)}, u32[]{:S(2)}) collective-permute-start(bf16[512,256]{1,0:T(8,128)(2,1)} %bitcast.8), channel_id=1, source_target_pairs={{0,4},{1,5},{2,6},{3,7},{4,0},{5,1},{6,2},{7,3},{8,12},{9,13},{10,... | collective-permute-start | bytes 786440 | tf_op jit(solution)/shard_map/ppermute | solution.py:34
  4.7 1.4 %collective-permute-start = (s32[1]{0:T(128)}, s32[1]{0:T(128)}, u32[]{:S(2)}, u32[]{:S(2)}) collective-permute-start(s32[1]{0:T(128)} %param.13), channel_id=1, source_target_pairs={{0,8},{8,0},{16,24},{24,16},{1,9},{9,1},{17,25},{25,17},{2,10},{10... | collective-permute-start | bytes 20 | tf_op jit(solution)/shard_map/ppermute | solution.py:39
  9.5 5.0 %collective-permute-start.1 = (s32[2]{0:T(128)S(1)}, s32[2]{0:T(128)S(1)}, u32[]{:S(2)}, u32[]{:S(2)}) collective-permute-start(s32[2]{0:T(128)S(1)} %get-tuple-element.33.here_ref), channel_id=1, source_target_pairs={{0,16},{8,24},{16,0},{24,8},{1,17},{9,25},{17,1},{25,9},{2,18},{10... | collective-permute-start | bytes 32 | tf_op jit(solution)/shard_map/ppermute | solution.py:39
  11.1 9.9 %collective-permute-start.4 = (bf16[128,256]{1,0:T(8,128)(2,1)S(1)}, bf16[128,256]{1,0:T(8,128)(2,1)S(1)}, u32[]{:S(2)}, u32[]{:S(2)}) collective-permute-start(bf16[128,256]{1,0:T(8,128)(2,1)S(1)} %get-tuple-element.43), channel_id=1, source_target_pairs={{0,1},{1,0},{2,3},{3,2},{4,5},{5,4},{6,7},{7,6},{8,9},{9,8},{10,11... | collective-permute-start | bytes 196616 | tf_op jit(solution)/shard_map/ppermute | solution.py:39
  12.6 14.2 %collective-permute-start.6 = (bf16[256,256]{1,0:T(8,128)(2,1)S(1)}, bf16[256,256]{1,0:T(8,128)(2,1)S(1)}, u32[]{:S(2)}, u32[]{:S(2)}) collective-permute-start(bf16[256,256]{1,0:T(8,128)(2,1)S(1)} %get-tuple-element.48), channel_id=1, source_target_pairs={{0,4},{1,5},{2,6},{3,7},{4,0},{5,1},{6,2},{7,3},{8,12},{9,13},{10,... | collective-permute-start | bytes 393224 | tf_op jit(solution)/shard_map/ppermute | solution.py:34
  12.9 15.9 %collective-permute-start.2 = (bf16[128,256]{1,0:T(8,128)(2,1)S(1)}, bf16[128,256]{1,0:T(8,128)(2,1)S(1)}, u32[]{:S(2)}, u32[]{:S(2)}) collective-permute-start(bf16[128,256]{1,0:T(8,128)(2,1)S(1)} %get-tuple-element.41), channel_id=1, source_target_pairs={{0,2},{1,3},{2,0},{3,1},{4,6},{5,7},{6,4},{7,5},{8,10},{9,11},{10,... | collective-permute-start | bytes 196616 | tf_op jit(solution)/shard_map/ppermute | solution.py:39
  22.3 12.6 %collective-permute-start.10 = (bf16[256,256]{1,0:T(8,128)(2,1)S(1)}, bf16[256,256]{1,0:T(8,128)(2,1)S(1)}, u32[]{:S(2)}, u32[]{:S(2)}) collective-permute-start(bf16[256,256]{1,0:T(8,128)(2,1)S(1)} %get-tuple-element.60), channel_id=1, source_target_pairs={{0,4},{1,5},{2,6},{3,7},{4,0},{5,1},{6,2},{7,3},{8,12},{9,13},{10,... | collective-permute-start | bytes 393224 | tf_op jit(solution)/shard_map/ppermute | solution.py:34
  22.4 8.0 %collective-permute-start.3 = (bf16[128,256]{1,0:T(8,128)(2,1)S(1)}, bf16[128,256]{1,0:T(8,128)(2,1)S(1)}, u32[]{:S(2)}, u32[]{:S(2)}) collective-permute-start(bf16[128,256]{1,0:T(8,128)(2,1)S(1)} %get-tuple-element.42), channel_id=1, source_target_pairs={{0,3},{1,2},{2,1},{3,0},{4,7},{5,6},{6,5},{7,4},{8,11},{9,10},{10,... | collective-permute-start | bytes 196616 | tf_op jit(solution)/shard_map/ppermute | solution.py:39
  26.7 5.1 %collective-permute-start.7 = (bf16[128,256]{1,0:T(8,128)(2,1)S(1)}, bf16[128,256]{1,0:T(8,128)(2,1)S(1)}, u32[]{:S(2)}, u32[]{:S(2)}) collective-permute-start(bf16[128,256]{1,0:T(8,128)(2,1)S(1)} %get-tuple-element.50), channel_id=1, source_target_pairs={{0,2},{1,3},{2,0},{3,1},{4,6},{5,7},{6,4},{7,5},{8,10},{9,11},{10,... | collective-permute-start | bytes 196616 | tf_op jit(solution)/shard_map/ppermute | solution.py:39
  26.8 6.4 %collective-permute-start.8 = (bf16[128,256]{1,0:T(8,128)(2,1)S(1)}, bf16[128,256]{1,0:T(8,128)(2,1)S(1)}, u32[]{:S(2)}, u32[]{:S(2)}) collective-permute-start(bf16[128,256]{1,0:T(8,128)(2,1)S(1)} %get-tuple-element.51), channel_id=1, source_target_pairs={{0,3},{1,2},{2,1},{3,0},{4,7},{5,6},{6,5},{7,4},{8,11},{9,10},{10,... | collective-permute-start | bytes 196616 | tf_op jit(solution)/shard_map/ppermute | solution.py:39
  28.8 5.0 %collective-permute-start.9 = (bf16[128,256]{1,0:T(8,128)(2,1)S(1)}, bf16[128,256]{1,0:T(8,128)(2,1)S(1)}, u32[]{:S(2)}, u32[]{:S(2)}) collective-permute-start(bf16[128,256]{1,0:T(8,128)(2,1)S(1)} %get-tuple-element.52), channel_id=1, source_target_pairs={{0,1},{1,0},{2,3},{3,2},{4,5},{5,4},{6,7},{7,6},{8,9},{9,8},{10,11... | collective-permute-start | bytes 196616 | tf_op jit(solution)/shard_map/ppermute | solution.py:39

commit v5 on v2

--- a/solution.py
+++ b/solution.py
@@ -387,14 +387,14 @@
     )
 
 
-def late_pieces(heads, key_chosen):
+def late_pieces(heads, key_chosen, after):
     others, rows, width = key_chosen.shape
     piece = rows // HEAD_DIVISIONS
     run = piece // 2
     first = heads[0].shape[0] // 2
 
     def body(key_ref, *refs):
-        v_refs, e_refs = refs[:others], refs[others:]
+        v_refs, e_refs = refs[:others], refs[others + len(after) :]
         for m in range(HEAD_DIVISIONS):
             for turn in range(others):
                 e_refs[m][columns(turn, piece)] = key_ref[turn, columns(m, piece)]
@@ -413,18 +413,21 @@
     shapes = [
         jax.ShapeDtypeStruct((2 * others * piece, width), bf16) for _ in range(HEAD_DIVISIONS)
     ]
-    return call(body, shapes, [VMEM] * (1 + others), "late_pieces")(key_chosen, *heads)
-
-
-def attend(facts_row, facts_of, weights, acc, heads, tails, live, mark):
+    return call(body, shapes, [VMEM] * (1 + others + len(after)), "late_pieces")(
+        key_chosen, *heads, *after
+    )
+
+
+def attend(facts_row, facts_of, weights, acc, heads, tails, live):
     rows = live.shape[0]
     block_len = rows // 2
     others = len(weights)
     slots = facts_of(None).slots
 
-    def body(facts_ref, mark_ref, acc_ref, live_ref, *refs):
+    def body(facts_ref, acc_ref, live_ref, *refs):
         w_refs, h_refs, t_refs = refs[:others], refs[others : 2 * others], refs[2 * others : 3 * others]
-        out_ref, v_scr = refs[3 * others :]
+        out_ref, mark_ref, v_scr = refs[3 * others :]
+        mark_ref[...] = jnp.zeros_like(mark_ref)
         for turn in range(others):
             first, rest = h_refs[turn].shape[0] // 2, t_refs[turn].shape[0] // 2
             for half in range(2):
@@ -454,22 +457,24 @@
                 scale = live_ref[part] / total[:, HEAD_SIZE:]
                 out_ref[part, columns(head)] = (total[:, :HEAD_SIZE] * scale).astype(bf16)
 
-    shape = jax.ShapeDtypeStruct((rows, Q_DEV * HEAD_SIZE), bf16)
-    specs = [SMEM] + [VMEM] * (3 + 3 * others)
+    shape = [
+        jax.ShapeDtypeStruct((rows, Q_DEV * HEAD_SIZE), bf16),
+        jax.ShapeDtypeStruct((8, HEAD_SIZE), f32),
+    ]
+    specs = [SMEM] + [VMEM] * (2 + 3 * others)
     scratch = [pltpu.VMEM((others, rows, KV_WIDTH), bf16)]
     return call(body, shape, specs, "attend", scratch)(
-        facts_row, mark, acc, live, *weights, *heads, *tails
-    )
-
-
-def cache_part(early, late, kept):
+        facts_row, acc, live, *weights, *heads, *tails
+    )
+
+
+def cache_part(early, late, kept, mark):
     cache_rows = kept.shape[0]
     piece = early[0].shape[0] // 2
     width = early[0].shape[1]
 
     def body(kept_ref, *refs):
-        f_refs, s_refs, out_ref, mark_ref = refs[:4], refs[4:8], refs[8], refs[9]
-        mark_ref[...] = jnp.zeros_like(mark_ref)
+        f_refs, s_refs, out_ref = refs[:4], refs[4:8], refs[9]
         head_group = slot_and_head_group()[1]
         later = cache_rows - piece
         for index, m in enumerate(HAND_ORDER):
@@ -482,11 +487,8 @@
                     kept_ref[...], lines
                 ).astype(bf16)
 
-    shape = [
-        jax.ShapeDtypeStruct((cache_rows, 2 * HEAD_DIVISIONS * width), bf16),
-        jax.ShapeDtypeStruct((8, HEAD_SIZE), f32),
-    ]
-    return call(body, shape, [VMEM] * 9, "cache_part")(kept, *early, *late)
+    shape = jax.ShapeDtypeStruct((cache_rows, 2 * HEAD_DIVISIONS * width), bf16)
+    return call(body, shape, [VMEM] * 10, "cache_part")(kept, *early, *late, mark)
 
 
 def on_device(queries, keys, values, block_map, lengths, group_of_prompt, decode_rank):
@@ -528,10 +530,10 @@
     lens = (block, crossed(block, "req", span))
     query_rot, acc, kept, live, angles = own_part(facts_row, facts_of, operands, tables, lens)
     key_rot, chosen = receive_keys(key_in, select, order, angles)
-    late = hand_on(late_pieces(heads, chosen))
+    late = hand_on(late_pieces(heads, chosen, early[1:]))
     weights = weigh(facts_row, facts_of, query_rot, key_rot)
-    cache, mark = cache_part(early, late, kept)
-    attended = attend(facts_row, facts_of, weights, acc, heads, tails, live, mark)
+    attended, mark = attend(facts_row, facts_of, weights, acc, heads, tails, live)
+    cache = cache_part(early, late, kept, mark)
     return (attended[None, None], cache[None])
 
 

time: 35.8 us -> 34.2 us (0.955)
  waiting for transfers between devices: 9.4 us -> 7.81 us
    ppermute x8, waiting for transfers between devices: 4.13 us -> 2.58 us  [crossed(): return lax.ppermute(shard, axis, [(i, i ^ by) for i in range(peers)])]
  transfers between devices with their start and end apart: 11 -> 11, of which waited for: 6 -> 4; matrix products, arithmetic and copies ran while one was open for 0% -> 0% of each run, Pallas kernels for 24% -> 27%
where the time goes in v5:
time: 34.2 us; the launch traced here: 34 us
  starting transfers between devices  14.5 us (42%)
  Pallas kernels  10.4 us (30%)
  waiting for transfers between devices  7.81 us (23%)
  between operations  1.36 us (4%)
    ppermute x8, starting transfers between devices, crossed(): return lax.ppermute(shard, axis, [(i, i ^ by) for i in range(peers)])  10 us
    ppermute x3, waiting for transfers between devices, shifted(): lax.ppermute(shard, axis, [(i, (i + by) % peers) for i in range(peers)])  5.23 us
    ppermute x3, starting transfers between devices, shifted(): lax.ppermute(shard, axis, [(i, (i + by) % peers) for i in range(peers)])  4.44 us
    pallas_call x1, Pallas kernels, prepare(): call(body, shapes, [SMEM] * 2 + [HBM] * count, 'prepare', scratch, out_sp...  3.33 us
    ppermute x8, waiting for transfers between devices, crossed(): return lax.ppermute(shard, axis, [(i, i ^ by) for i in range(peers)])  2.58 us
    pallas_call x1, Pallas kernels, own_part(): call(body, shapes, [SMEM] * 3 + [VMEM] * 5, 'own_part')  2.36 us
    pallas_call x1, Pallas kernels, attend(): call(body, shape, specs, 'attend', scratch)  1.88 us
    pallas_call x1, Pallas kernels, weigh(): call(body, shapes, [SMEM] + [VMEM] * (1 + others), 'weigh')  1.27 us
  transfers between devices with their start and end apart: 11, of which 4 were waited for; matrix products, arithmetic and copies ran while one was open for 0% of the time, Pallas kernels for 27%

profile of v5, /device:TPU:0, one launch (start us, length us, event | category | flops | bytes accessed | tf_op | source)
XLA Modules:
  0.0 34.0 jit_solution(1580441487679576402)
XLA Ops:
  0.6 4.1 %collective-permute-start.2 = (bf16[512,256]{1,0:T(8,128)(2,1)}, bf16[512,256]{1,0:T(8,128)(2,1)S(1)}, u32[]{:S(2)}, u32[]{:S(2)}) collective-permute-start(bf16[512,256]{1,0:T(8,128)(2,1)} %bitcast.8), channel_id=1, source_target_pairs={{0,4},{1,5},{2,6},{3,7},{4,0},{5,1},{6,2},{7,3},{8,12},{9,13},{10,... | collective-permute-start | bytes 786440 | tf_op jit(solution)/shard_map/ppermute | solution.py:34
  4.7 0.0 collective-permute-start
  5.4 0.6 %collective-permute-done.near_ref = s32[1]{0:T(128)} collective-permute-done((s32[1]{0:T(128)}, s32[1]{0:T(128)}, u32[]{:S(2)}, u32[]{:S(2)}) %collective-permute-start) | collective-permute-done | bytes 36 | tf_op jit(solution)/shard_map/ppermute | solution.py:39
  6.0 3.3 %prepare.1 = (s32[1,16]{1,0:T(1,128)S(1)}, s32[2]{0:T(128)S(1)}, bf16[512,512]{1,0:T(8,128)(2,1)S(1)}, bf16[512,256]{1,0:T(8,128)(2,1)S(1)}, bf16[512,256]{1,0:T...) custom-call(s32[1]{0:T(128)S(6)} %copy.11.own_ref, ...), custom_call_target="tpu_custom_call" | custom-call | flops 1000 | bytes 1000 | tf_op jit(solution)/shard_map/prepare/pallas_call | solution.py:235
  9.3 1.6 %collective-permute-start.1 = (s32[2]{0:T(128)S(1)}, s32[2]{0:T(128)S(1)}, u32[]{:S(2)}, u32[]{:S(2)}) collective-permute-start(s32[2]{0:T(128)S(1)} %get-tuple-element.33.here_ref), channel_id=1, source_target_pairs={{0,16},{8,24},{16,0},{24,8},{1,17},{9,25},{17,1},{25,9},{2,18},{10... | collective-permute-start | bytes 32 | tf_op jit(solution)/shard_map/ppermute | solution.py:39
  10.9 0.3 collective-permute-start.3
  11.2 1.6 %collective-permute-start.5 = (bf16[128,256]{1,0:T(8,128)(2,1)S(1)}, bf16[128,256]{1,0:T(8,128)(2,1)S(1)}, u32[]{:S(2)}, u32[]{:S(2)}) collective-permute-start(bf16[128,256]{1,0:T(8,128)(2,1)S(1)} %get-tuple-element.53), channel_id=1, source_target_pairs={{0,2},{1,3},{2,0},{3,1},{4,6},{5,7},{6,4},{7,5},{8,10},{9,11},{10,... | collective-permute-start | bytes 196616 | tf_op jit(solution)/shard_map/ppermute | solution.py:39
  12.8 1.4 %collective-permute-start.6 = (bf16[128,256]{1,0:T(8,128)(2,1)S(1)}, bf16[128,256]{1,0:T(8,128)(2,1)S(1)}, u32[]{:S(2)}, u32[]{:S(2)}) collective-permute-start(bf16[128,256]{1,0:T(8,128)(2,1)S(1)} %get-tuple-element.54), channel_id=1, source_target_pairs={{0,3},{1,2},{2,1},{3,0},{4,7},{5,6},{6,5},{7,4},{8,11},{9,10},{10,... | collective-permute-start | bytes 196616 | tf_op jit(solution)/shard_map/ppermute | solution.py:39
  14.2 0.0 collective-permute-done.1.there_ref
  14.2 0.5 %collective-permute-start.7 = (bf16[128,256]{1,0:T(8,128)(2,1)S(1)}, bf16[128,256]{1,0:T(8,128)(2,1)S(1)}, u32[]{:S(2)}, u32[]{:S(2)}) collective-permute-start(bf16[128,256]{1,0:T(8,128)(2,1)S(1)} %get-tuple-element.55), channel_id=1, source_target_pairs={{0,1},{1,0},{2,3},{3,2},{4,5},{5,4},{6,7},{7,6},{8,9},{9,8},{10,11... | collective-permute-start | bytes 196616 | tf_op jit(solution)/shard_map/ppermute | solution.py:39
  14.7 2.4 %own_part.1 = (bf16[512,512]{1,0:T(8,128)(2,1)S(1)}, f32[512,1024]{1,0:T(8,128)S(1)}, bf16[128,128]{1,0:T(8,128)(2,1)S(1)}, f32[512,128]{1,0:T(8,128)S(1)}, f32[1,2,2,256,128]{4,3,2,1,0:T(8,128)S(1)}) custom-call(s32[1,16]{1,0:T(1,128)S(1)} %get-tuple-element.32.facts_ref, s32[2]{0:T(128)S(1)} %get-tuple-element.33.here_ref, ...), custom_call_target="tpu_custom_call" | custom-call | flops 1000 | bytes 1000 | tf_op jit(solution)/shard_map/own_part/pallas_call | solution.py:321
  17.1 3.5 %collective-permute-done.2.refs_0_ = bf16[512,256]{1,0:T(8,128)(2,1)S(1)} collective-permute-done((bf16[512,256]{1,0:T(8,128)(2,1)}, bf16[512,256]{1,0:T(8,128)(2,1)S(1)}, u32[]{:S(2)}, u32[]{:S(2)}) %collective-permute-start.2) | collective-permute-done | bytes 262176 | tf_op jit(solution)/shard_map/ppermute | solution.py:34
  20.5 0.0 collective-permute-start.4
  20.5 0.4 %receive_keys.1 = (bf16[512,256]{1,0:T(8,128)(2,1)S(1)}, bf16[1,256,256]{2,1,0:T(8,128)(2,1)S(1)}) custom-call(bf16[256,512]{1,0:T(8,128)(2,1)S(1)} %get-tuple-element.42.select_ref, bf16[256,256]{1,0:T(8,128)(2,1)S(1)} %get-tuple-element.43.order_ref, f32[1,2,2,256,128]{4,3,2,1,0:T(8,128)S(1)} %get-tuple-element.44.angle_ref, ...), custom_call_target="tpu_custom_call" | custom-call | flops 10000000000 | bytes 1000 | tf_op jit(solution)/shard_map/receive_keys/pallas_call | solution.py:357
  21.0 0.0 collective-permute-done.5.refs_1_
  21.0 0.0 collective-permute-done.6.refs_2_
  21.0 0.0 collective-permute-done.7.refs_3_
  21.0 1.8 %collective-permute-done.3.refs_1_.refs_0_ = bf16[256,256]{1,0:T(8,128)(2,1)S(1)} collective-permute-done((bf16[256,256]{1,0:T(8,128)(2,1)S(1)}, bf16[256,256]{1,0:T(8,128)(2,1)S(1)}, u32[]{:S(2)}, u32[]{:S(2)}) %collective-permute-start.3) | collective-permute-done | bytes 131104 | tf_op jit(solution)/shard_map/ppermute | solution.py:34
  22.8 2.2 %collective-permute-start.10 = (bf16[128,256]{1,0:T(8,128)(2,1)S(1)}, bf16[128,256]{1,0:T(8,128)(2,1)S(1)}, u32[]{:S(2)}, u32[]{:S(2)}) collective-permute-start(bf16[128,256]{1,0:T(8,128)(2,1)S(1)} %get-tuple-element.60), channel_id=1, source_target_pairs={{0,1},{1,0},{2,3},{3,2},{4,5},{5,4},{6,7},{7,6},{8,9},{9,8},{10,11... | collective-permute-start | bytes 196616 | tf_op jit(solution)/shard_map/ppermute | solution.py:39
  25.0 2.8 %collective-permute-start.8 = (bf16[128,256]{1,0:T(8,128)(2,1)S(1)}, bf16[128,256]{1,0:T(8,128)(2,1)S(1)}, u32[]{:S(2)}, u32[]{:S(2)}) collective-permute-start(bf16[128,256]{1,0:T(8,128)(2,1)S(1)} %get-tuple-element.58), channel_id=1, source_target_pairs={{0,2},{1,3},{2,0},{3,1},{4,6},{5,7},{6,4},{7,5},{8,10},{9,11},{10,... | collective-permute-start | bytes 196616 | tf_op jit(solution)/shard_map/ppermute | solution.py:39
  27.8 0.0 collective-permute-start.9
  27.8 1.3 %weigh.1.refs_0_ = bf16[2,4,256,256]{3,2,1,0:T(8,128)(2,1)S(1)} custom-call(s32[1,16]{1,0:T(1,128)S(1)} %get-tuple-element.32.facts_ref, bf16[512,512]{1,0:T(8,128)(2,1)S(1)} %get-tuple-element.41.q_ref, bf16[512,256]{1,0:T(8,128)(2,1)S(1)} %get-tuple-element.47.refs_0_), custom_call_target="tpu_custom_call" | custom-call | flops 1000 | bytes 1000 | tf_op jit(solution)/shard_map/weigh/pallas_call | solution.py:385
  29.0 0.0 collective-permute-done.4.refs_2_
  29.1 1.9 %attend.1 = (bf16[512,512]{1,0:T(8,128)(2,1)}, f32[8,128]{1,0:T(8,128)S(1)}) custom-call(s32[1,16]{1,0:T(1,128)S(1)} %get-tuple-element.32.facts_ref, f32[512,1024]{1,0:T(8,128)S(1)} %get-tuple-element.39.acc_ref, f32[512,128]{1,0:T(8,128)S(1)} %get-tuple-element.40.live_ref, bf16[2,4,256,256]{3,2,1,0:T(8,128)(2,1)S(1)} %weigh.1.refs_0_, ...), custom_call_target="tpu_custom_call" | custom-call | flops 1000 | bytes 1000 | tf_op jit(solution)/shard_map/attend/pallas_call | solution.py:466
  30.9 0.0 collective-permute-done.10.refs_7_
  30.9 0.0 collective-permute-done.8.refs_5_
  30.9 2.0 %collective-permute-done.9.refs_6_ = bf16[128,256]{1,0:T(8,128)(2,1)S(1)} collective-permute-done((bf16[128,256]{1,0:T(8,128)(2,1)S(1)}, bf16[128,256]{1,0:T(8,128)(2,1)S(1)}, u32[]{:S(2)}, u32[]{:S(2)}) %collective-permute-start.9) | collective-permute-done | bytes 65568 | tf_op jit(solution)/shard_map/ppermute | solution.py:39
  32.9 1.1 %cache_part.1 = bf16[128,2048]{1,0:T(8,128)(2,1)} custom-call(bf16[128,128]{1,0:T(8,128)(2,1)S(1)} %get-tuple-element.51.kept_ref, bf16[128,256]{1,0:T(8,128)(2,1)S(1)} %get-tuple-element.52.refs_0_, bf16[128,256]{1,0:T(8,128)(2,1)S(1)} %collective-permute-done.5.refs_1_, bf16[128,256]{1,0:T(8,128)(2,1)S(1)} %collective-permute-done.6.refs_2_, ...), custom_call_target="tpu_custom_call" | custom-call | flops 1000 | bytes 1000 | tf_op jit(solution)/shard_map/cache_part/pallas_call | solution.py:491
  (1 shorter events, 0.0 us)
Async XLA Ops:
  0.6 19.9 %collective-permute-start.2 = (bf16[512,256]{1,0:T(8,128)(2,1)}, bf16[512,256]{1,0:T(8,128)(2,1)S(1)}, u32[]{:S(2)}, u32[]{:S(2)}) collective-permute-start(bf16[512,256]{1,0:T(8,128)(2,1)} %bitcast.8), channel_id=1, source_target_pairs={{0,4},{1,5},{2,6},{3,7},{4,0},{5,1},{6,2},{7,3},{8,12},{9,13},{10,... | collective-permute-start | bytes 786440 | tf_op jit(solution)/shard_map/ppermute | solution.py:34
  4.7 1.2 %collective-permute-start = (s32[1]{0:T(128)}, s32[1]{0:T(128)}, u32[]{:S(2)}, u32[]{:S(2)}) collective-permute-start(s32[1]{0:T(128)} %param.13), channel_id=1, source_target_pairs={{0,8},{8,0},{16,24},{24,16},{1,9},{9,1},{17,25},{25,17},{2,10},{10... | collective-permute-start | bytes 20 | tf_op jit(solution)/shard_map/ppermute | solution.py:39
  9.3 4.9 %collective-permute-start.1 = (s32[2]{0:T(128)S(1)}, s32[2]{0:T(128)S(1)}, u32[]{:S(2)}, u32[]{:S(2)}) collective-permute-start(s32[2]{0:T(128)S(1)} %get-tuple-element.33.here_ref), channel_id=1, source_target_pairs={{0,16},{8,24},{16,0},{24,8},{1,17},{9,25},{17,1},{25,9},{2,18},{10... | collective-permute-start | bytes 32 | tf_op jit(solution)/shard_map/ppermute | solution.py:39
  10.9 11.9 %collective-permute-start.3 = (bf16[256,256]{1,0:T(8,128)(2,1)S(1)}, bf16[256,256]{1,0:T(8,128)(2,1)S(1)}, u32[]{:S(2)}, u32[]{:S(2)}) collective-permute-start(bf16[256,256]{1,0:T(8,128)(2,1)S(1)} %get-tuple-element.48), channel_id=1, source_target_pairs={{0,4},{1,5},{2,6},{3,7},{4,0},{5,1},{6,2},{7,3},{8,12},{9,13},{10,... | collective-permute-start | bytes 393224 | tf_op jit(solution)/shard_map/ppermute | solution.py:34
  11.2 9.8 %collective-permute-start.5 = (bf16[128,256]{1,0:T(8,128)(2,1)S(1)}, bf16[128,256]{1,0:T(8,128)(2,1)S(1)}, u32[]{:S(2)}, u32[]{:S(2)}) collective-permute-start(bf16[128,256]{1,0:T(8,128)(2,1)S(1)} %get-tuple-element.53), channel_id=1, source_target_pairs={{0,2},{1,3},{2,0},{3,1},{4,6},{5,7},{6,4},{7,5},{8,10},{9,11},{10,... | collective-permute-start | bytes 196616 | tf_op jit(solution)/shard_map/ppermute | solution.py:39
  12.8 8.2 %collective-permute-start.6 = (bf16[128,256]{1,0:T(8,128)(2,1)S(1)}, bf16[128,256]{1,0:T(8,128)(2,1)S(1)}, u32[]{:S(2)}, u32[]{:S(2)}) collective-permute-start(bf16[128,256]{1,0:T(8,128)(2,1)S(1)} %get-tuple-element.54), channel_id=1, source_target_pairs={{0,3},{1,2},{2,1},{3,0},{4,7},{5,6},{6,5},{7,4},{8,11},{9,10},{10,... | collective-permute-start | bytes 196616 | tf_op jit(solution)/shard_map/ppermute | solution.py:39
  14.2 6.8 %collective-permute-start.7 = (bf16[128,256]{1,0:T(8,128)(2,1)S(1)}, bf16[128,256]{1,0:T(8,128)(2,1)S(1)}, u32[]{:S(2)}, u32[]{:S(2)}) collective-permute-start(bf16[128,256]{1,0:T(8,128)(2,1)S(1)} %get-tuple-element.55), channel_id=1, source_target_pairs={{0,1},{1,0},{2,3},{3,2},{4,5},{5,4},{6,7},{7,6},{8,9},{9,8},{10,11... | collective-permute-start | bytes 196616 | tf_op jit(solution)/shard_map/ppermute | solution.py:39
  20.5 8.5 %collective-permute-start.4 = (bf16[256,256]{1,0:T(8,128)(2,1)S(1)}, bf16[256,256]{1,0:T(8,128)(2,1)S(1)}, u32[]{:S(2)}, u32[]{:S(2)}) collective-permute-start(bf16[256,256]{1,0:T(8,128)(2,1)S(1)} %get-tuple-element.49), channel_id=1, source_target_pairs={{0,4},{1,5},{2,6},{3,7},{4,0},{5,1},{6,2},{7,3},{8,12},{9,13},{10,... | collective-permute-start | bytes 393224 | tf_op jit(solution)/shard_map/ppermute | solution.py:34
  22.8 8.2 %collective-permute-start.10 = (bf16[128,256]{1,0:T(8,128)(2,1)S(1)}, bf16[128,256]{1,0:T(8,128)(2,1)S(1)}, u32[]{:S(2)}, u32[]{:S(2)}) collective-permute-start(bf16[128,256]{1,0:T(8,128)(2,1)S(1)} %get-tuple-element.60), channel_id=1, source_target_pairs={{0,1},{1,0},{2,3},{3,2},{4,5},{5,4},{6,7},{7,6},{8,9},{9,8},{10,11... | collective-permute-start | bytes 196616 | tf_op jit(solution)/shard_map/ppermute | solution.py:39
  25.0 6.0 %collective-permute-start.8 = (bf16[128,256]{1,0:T(8,128)(2,1)S(1)}, bf16[128,256]{1,0:T(8,128)(2,1)S(1)}, u32[]{:S(2)}, u32[]{:S(2)}) collective-permute-start(bf16[128,256]{1,0:T(8,128)(2,1)S(1)} %get-tuple-element.58), channel_id=1, source_target_pairs={{0,2},{1,3},{2,0},{3,1},{4,6},{5,7},{6,4},{7,5},{8,10},{9,11},{10,... | collective-permute-start | bytes 196616 | tf_op jit(solution)/shard_map/ppermute | solution.py:39
  27.8 5.2 %collective-permute-start.9 = (bf16[128,256]{1,0:T(8,128)(2,1)S(1)}, bf16[128,256]{1,0:T(8,128)(2,1)S(1)}, u32[]{:S(2)}, u32[]{:S(2)}) collective-permute-start(bf16[128,256]{1,0:T(8,128)(2,1)S(1)} %get-tuple-element.59), channel_id=1, source_target_pairs={{0,3},{1,2},{2,1},{3,0},{4,7},{5,6},{6,5},{7,4},{8,11},{9,10},{10,... | collective-permute-start | bytes 196616 | tf_op jit(solution)/shard_map/ppermute | solution.py:39

commit v6 on v5

--- a/solution.py
+++ b/solution.py
@@ -360,14 +360,17 @@
     return outs[:others], outs[others]
 
 
-def weigh(facts_row, facts_of, query_rot, key_rot):
+def weigh(facts_row, facts_of, query_rot, key_rot, payload):
     others = len(key_rot)
     rows = query_rot.shape[0]
     block_len = rows // 2
     slots = facts_of(None).slots
 
     def body(facts_ref, q_ref, *refs):
-        k_refs, w_refs = refs[:others], refs[others:]
+        k_refs, pay_refs, refs = refs[:others], refs[others : 2 * others], refs[2 * others :]
+        w_refs, out_refs = refs[:others], refs[others:]
+        for pay_ref, out_ref in zip(pay_refs, out_refs):
+            out_ref[...] = pay_ref[...]
         facts = facts_of(facts_ref)
         slot = slot_and_head_group()[0]
         for turn in range(1, slots):
@@ -382,9 +385,11 @@
     shapes = [
         jax.ShapeDtypeStruct((2, Q_DEV, block_len, block_len), bf16) for _ in range(others)
     ]
-    return call(body, shapes, [SMEM] + [VMEM] * (1 + others), "weigh")(
-        facts_row, query_rot, *key_rot
-    )
+    shapes += [jax.ShapeDtypeStruct(x.shape, bf16) for x in payload]
+    outs = call(body, shapes, [SMEM] + [VMEM] * (1 + 2 * others), "weigh")(
+        facts_row, query_rot, *key_rot, *payload
+    )
+    return outs[:others], outs[others:]
 
 
 def late_pieces(heads, key_chosen, after):
@@ -516,8 +521,6 @@
         crossed(lengths, "req", 1),
     )
     heads = to_slots(sent[0::2])
-    tails, key_in = lax.optimization_barrier((sent[1::2], key_in))
-    tails = to_slots(tails)
     early = hand_on(early)
     span, groups = 2, lax.axis_size("req")
     while 2 * span < groups:
@@ -530,8 +533,9 @@
     lens = (block, crossed(block, "req", span))
     query_rot, acc, kept, live, angles = own_part(facts_row, facts_of, operands, tables, lens)
     key_rot, chosen = receive_keys(key_in, select, order, angles)
+    weights, tails = weigh(facts_row, facts_of, query_rot, key_rot, sent[1::2])
+    tails = to_slots(tails)
     late = hand_on(late_pieces(heads, chosen, early[1:]))
-    weights = weigh(facts_row, facts_of, query_rot, key_rot)
     attended, mark = attend(facts_row, facts_of, weights, acc, heads, tails, live)
     cache = cache_part(early, late, kept, mark)
     return (attended[None, None], cache[None])

time: 34.2 us -> 33.8 us (0.988)
    ppermute x8, waiting for transfers between devices: 2.58 us -> 1.2 us  [crossed(): return lax.ppermute(shard, axis, [(i, i ^ by) for i in range(peers)])]
    ppermute x3, waiting for transfers between devices: 5.23 us -> 6.29 us  [shifted(): lax.ppermute(shard, axis, [(i, (i + by) % peers) for i in range(peers)])]
  transfers between devices with their start and end apart: 11 -> 11, of which waited for: 4 -> 5; matrix products, arithmetic and copies ran while one was open for 0% -> 0% of each run, Pallas kernels for 27% -> 28%
where the time goes in v6:
time: 33.8 us; the launch traced here: 33.6 us
  starting transfers between devices  14.4 us (43%)
  Pallas kernels  10.4 us (31%)
  waiting for transfers between devices  7.49 us (22%)
  between operations  1.36 us (4%)
    ppermute x8, starting transfers between devices, crossed(): return lax.ppermute(shard, axis, [(i, i ^ by) for i in range(peers)])  9.89 us
    ppermute x3, waiting for transfers between devices, shifted(): lax.ppermute(shard, axis, [(i, (i + by) % peers) for i in range(peers)])  6.29 us
    ppermute x3, starting transfers between devices, shifted(): lax.ppermute(shard, axis, [(i, (i + by) % peers) for i in range(peers)])  4.51 us
    pallas_call x1, Pallas kernels, prepare(): call(body, shapes, [SMEM] * 2 + [HBM] * count, 'prepare', scratch, out_sp...  3.36 us
    pallas_call x1, Pallas kernels, own_part(): call(body, shapes, [SMEM] * 3 + [VMEM] * 5, 'own_part')  2.36 us
    pallas_call x1, Pallas kernels, attend(): call(body, shape, specs, 'attend', scratch)  1.88 us
    pallas_call x1, Pallas kernels, weigh(): call(body, shapes, [SMEM] + [VMEM] * (1 + 2 * others), 'weigh')  1.28 us
    ppermute x8, waiting for transfers between devices, crossed(): return lax.ppermute(shard, axis, [(i, i ^ by) for i in range(peers)])  1.2 us
  transfers between devices with their start and end apart: 11, of which 5 were waited for; matrix products, arithmetic and copies ran while one was open for 0% of the time, Pallas kernels for 28%

profile of v6, /device:TPU:0, one launch (start us, length us, event | category | flops | bytes accessed | tf_op | source)
XLA Modules:
  0.0 33.6 jit_solution(9970619073542996719)
XLA Ops:
  0.6 4.1 %collective-permute-start.2 = (bf16[512,256]{1,0:T(8,128)(2,1)}, bf16[512,256]{1,0:T(8,128)(2,1)S(1)}, u32[]{:S(2)}, u32[]{:S(2)}) collective-permute-start(bf16[512,256]{1,0:T(8,128)(2,1)} %bitcast.8), channel_id=1, source_target_pairs={{0,4},{1,5},{2,6},{3,7},{4,0},{5,1},{6,2},{7,3},{8,12},{9,13},{10,... | collective-permute-start | bytes 786440 | tf_op jit(solution)/shard_map/ppermute | solution.py:34
  4.7 0.0 collective-permute-start
  5.4 0.7 %collective-permute-done.near_ref = s32[1]{0:T(128)} collective-permute-done((s32[1]{0:T(128)}, s32[1]{0:T(128)}, u32[]{:S(2)}, u32[]{:S(2)}) %collective-permute-start) | collective-permute-done | bytes 36 | tf_op jit(solution)/shard_map/ppermute | solution.py:39
  6.1 3.4 %prepare.1 = (s32[1,16]{1,0:T(1,128)S(1)}, s32[2]{0:T(128)S(1)}, bf16[512,512]{1,0:T(8,128)(2,1)S(1)}, bf16[512,256]{1,0:T(8,128)(2,1)S(1)}, bf16[512,256]{1,0:T...) custom-call(s32[1]{0:T(128)S(6)} %copy.11.own_ref, ...), custom_call_target="tpu_custom_call" | custom-call | flops 1000 | bytes 1000 | tf_op jit(solution)/shard_map/prepare/pallas_call | solution.py:235
  9.5 1.6 %collective-permute-start.1 = (s32[2]{0:T(128)S(1)}, s32[2]{0:T(128)S(1)}, u32[]{:S(2)}, u32[]{:S(2)}) collective-permute-start(s32[2]{0:T(128)S(1)} %get-tuple-element.33.here_ref), channel_id=1, source_target_pairs={{0,16},{8,24},{16,0},{24,8},{1,17},{9,25},{17,1},{25,9},{2,18},{10... | collective-permute-start | bytes 32 | tf_op jit(solution)/shard_map/ppermute | solution.py:39
  11.0 0.3 collective-permute-start.3
  11.4 1.6 %collective-permute-start.5 = (bf16[128,256]{1,0:T(8,128)(2,1)S(1)}, bf16[128,256]{1,0:T(8,128)(2,1)S(1)}, u32[]{:S(2)}, u32[]{:S(2)}) collective-permute-start(bf16[128,256]{1,0:T(8,128)(2,1)S(1)} %get-tuple-element.53), channel_id=1, source_target_pairs={{0,2},{1,3},{2,0},{3,1},{4,6},{5,7},{6,4},{7,5},{8,10},{9,11},{10,... | collective-permute-start | bytes 196616 | tf_op jit(solution)/shard_map/ppermute | solution.py:39
  13.0 1.4 %collective-permute-start.6 = (bf16[128,256]{1,0:T(8,128)(2,1)S(1)}, bf16[128,256]{1,0:T(8,128)(2,1)S(1)}, u32[]{:S(2)}, u32[]{:S(2)}) collective-permute-start(bf16[128,256]{1,0:T(8,128)(2,1)S(1)} %get-tuple-element.54), channel_id=1, source_target_pairs={{0,3},{1,2},{2,1},{3,0},{4,7},{5,6},{6,5},{7,4},{8,11},{9,10},{10,... | collective-permute-start | bytes 196616 | tf_op jit(solution)/shard_map/ppermute | solution.py:39
  14.4 0.0 collective-permute-done.1.there_ref
  14.4 0.5 %collective-permute-start.7 = (bf16[128,256]{1,0:T(8,128)(2,1)S(1)}, bf16[128,256]{1,0:T(8,128)(2,1)S(1)}, u32[]{:S(2)}, u32[]{:S(2)}) collective-permute-start(bf16[128,256]{1,0:T(8,128)(2,1)S(1)} %get-tuple-element.55), channel_id=1, source_target_pairs={{0,1},{1,0},{2,3},{3,2},{4,5},{5,4},{6,7},{7,6},{8,9},{9,8},{10,11... | collective-permute-start | bytes 196616 | tf_op jit(solution)/shard_map/ppermute | solution.py:39
  14.9 2.4 %own_part.1 = (bf16[512,512]{1,0:T(8,128)(2,1)S(1)}, f32[512,1024]{1,0:T(8,128)S(1)}, bf16[128,128]{1,0:T(8,128)(2,1)S(1)}, f32[512,128]{1,0:T(8,128)S(1)}, f32[1,2,2,256,128]{4,3,2,1,0:T(8,128)S(1)}) custom-call(s32[1,16]{1,0:T(1,128)S(1)} %get-tuple-element.32.facts_ref, s32[2]{0:T(128)S(1)} %get-tuple-element.33.here_ref, ...), custom_call_target="tpu_custom_call" | custom-call | flops 1000 | bytes 1000 | tf_op jit(solution)/shard_map/own_part/pallas_call | solution.py:321
  17.2 3.3 %collective-permute-done.2.refs_0_ = bf16[512,256]{1,0:T(8,128)(2,1)S(1)} collective-permute-done((bf16[512,256]{1,0:T(8,128)(2,1)}, bf16[512,256]{1,0:T(8,128)(2,1)S(1)}, u32[]{:S(2)}, u32[]{:S(2)}) %collective-permute-start.2) | collective-permute-done | bytes 262176 | tf_op jit(solution)/shard_map/ppermute | solution.py:34
  20.5 0.4 %receive_keys.1 = (bf16[512,256]{1,0:T(8,128)(2,1)S(1)}, bf16[1,256,256]{2,1,0:T(8,128)(2,1)S(1)}) custom-call(bf16[256,512]{1,0:T(8,128)(2,1)S(1)} %get-tuple-element.42.select_ref, bf16[256,256]{1,0:T(8,128)(2,1)S(1)} %get-tuple-element.43.order_ref, f32[1,2,2,256,128]{4,3,2,1,0:T(8,128)S(1)} %get-tuple-element.44.angle_ref, ...), custom_call_target="tpu_custom_call" | custom-call | flops 10000000000 | bytes 1000 | tf_op jit(solution)/shard_map/receive_keys/pallas_call | solution.py:357
  21.0 1.3 %weigh.1 = (bf16[2,4,256,256]{3,2,1,0:T(8,128)(2,1)S(1)}, bf16[256,256]{1,0:T(8,128)(2,1)S(1)}) custom-call(s32[1,16]{1,0:T(1,128)S(1)} %get-tuple-element.32.facts_ref, bf16[512,512]{1,0:T(8,128)(2,1)S(1)} %get-tuple-element.41.q_ref, bf16[512,256]{1,0:T(8,128)(2,1)S(1)} %get-tuple-element.45.refs_0_, bf16[256,256]{1,0:T(8,128)(2,1)S(1)} %get-tuple-element.46.refs_1_), custom_call_target="tpu_custom_call" | custom-call | flops 1000 | bytes 1000 | tf_op jit(solution)/shard_map/weigh/pallas_call | solution.py:389
  22.3 0.1 collective-permute-start.4
  22.3 0.0 collective-permute-done.5.refs_1_
  22.3 0.0 collective-permute-done.6.refs_2_
  22.4 0.0 collective-permute-done.7.refs_3_
  22.4 0.2 collective-permute-done.3.refs_1_.refs_0_
  22.5 1.8 %collective-permute-start.10 = (bf16[128,256]{1,0:T(8,128)(2,1)S(1)}, bf16[128,256]{1,0:T(8,128)(2,1)S(1)}, u32[]{:S(2)}, u32[]{:S(2)}) collective-permute-start(bf16[128,256]{1,0:T(8,128)(2,1)S(1)} %get-tuple-element.60), channel_id=1, source_target_pairs={{0,1},{1,0},{2,3},{3,2},{4,5},{5,4},{6,7},{7,6},{8,9},{9,8},{10,11... | collective-permute-start | bytes 196616 | tf_op jit(solution)/shard_map/ppermute | solution.py:39
  24.3 3.0 %collective-permute-start.8 = (bf16[128,256]{1,0:T(8,128)(2,1)S(1)}, bf16[128,256]{1,0:T(8,128)(2,1)S(1)}, u32[]{:S(2)}, u32[]{:S(2)}) collective-permute-start(bf16[128,256]{1,0:T(8,128)(2,1)S(1)} %get-tuple-element.58), channel_id=1, source_target_pairs={{0,2},{1,3},{2,0},{3,1},{4,6},{5,7},{6,4},{7,5},{8,10},{9,11},{10,... | collective-permute-start | bytes 196616 | tf_op jit(solution)/shard_map/ppermute | solution.py:39
  27.4 0.0 collective-permute-start.9
  27.4 2.8 %collective-permute-done.4.refs_2_ = bf16[256,256]{1,0:T(8,128)(2,1)S(1)} collective-permute-done((bf16[256,256]{1,0:T(8,128)(2,1)S(1)}, bf16[256,256]{1,0:T(8,128)(2,1)S(1)}, u32[]{:S(2)}, u32[]{:S(2)}) %collective-permute-start.4) | collective-permute-done | bytes 131104 | tf_op jit(solution)/shard_map/ppermute | solution.py:34
  30.2 1.9 %attend.1 = (bf16[512,512]{1,0:T(8,128)(2,1)}, f32[8,128]{1,0:T(8,128)S(1)}) custom-call(s32[1,16]{1,0:T(1,128)S(1)} %get-tuple-element.32.facts_ref, f32[512,1024]{1,0:T(8,128)S(1)} %get-tuple-element.39.acc_ref, f32[512,128]{1,0:T(8,128)S(1)} %get-tuple-element.40.live_ref, bf16[2,4,256,256]{3,2,1,0:T(8,128)(2,1)S(1)} %get-tuple-element.47.refs_0_, ...), custom_call_target="tpu_custom_call" | custom-call | flops 1000 | bytes 1000 | tf_op jit(solution)/shard_map/attend/pallas_call | solution.py:471
  32.1 0.0 collective-permute-done.10.refs_7_
  32.1 0.0 collective-permute-done.8.refs_5_
  32.1 0.5 %collective-permute-done.9.refs_6_ = bf16[128,256]{1,0:T(8,128)(2,1)S(1)} collective-permute-done((bf16[128,256]{1,0:T(8,128)(2,1)S(1)}, bf16[128,256]{1,0:T(8,128)(2,1)S(1)}, u32[]{:S(2)}, u32[]{:S(2)}) %collective-permute-start.9) | collective-permute-done | bytes 65568 | tf_op jit(solution)/shard_map/ppermute | solution.py:39
  32.6 1.1 %cache_part.1 = bf16[128,2048]{1,0:T(8,128)(2,1)} custom-call(bf16[128,128]{1,0:T(8,128)(2,1)S(1)} %get-tuple-element.51.kept_ref, bf16[128,256]{1,0:T(8,128)(2,1)S(1)} %get-tuple-element.52.refs_0_, bf16[128,256]{1,0:T(8,128)(2,1)S(1)} %collective-permute-done.5.refs_1_, bf16[128,256]{1,0:T(8,128)(2,1)S(1)} %collective-permute-done.6.refs_2_, ...), custom_call_target="tpu_custom_call" | custom-call | flops 1000 | bytes 1000 | tf_op jit(solution)/shard_map/cache_part/pallas_call | solution.py:496
  (1 shorter events, 0.0 us)
Async XLA Ops:
  0.6 19.9 %collective-permute-start.2 = (bf16[512,256]{1,0:T(8,128)(2,1)}, bf16[512,256]{1,0:T(8,128)(2,1)S(1)}, u32[]{:S(2)}, u32[]{:S(2)}) collective-permute-start(bf16[512,256]{1,0:T(8,128)(2,1)} %bitcast.8), channel_id=1, source_target_pairs={{0,4},{1,5},{2,6},{3,7},{4,0},{5,1},{6,2},{7,3},{8,12},{9,13},{10,... | collective-permute-start | bytes 786440 | tf_op jit(solution)/shard_map/ppermute | solution.py:34
  4.7 1.4 %collective-permute-start = (s32[1]{0:T(128)}, s32[1]{0:T(128)}, u32[]{:S(2)}, u32[]{:S(2)}) collective-permute-start(s32[1]{0:T(128)} %param.13), channel_id=1, source_target_pairs={{0,8},{8,0},{16,24},{24,16},{1,9},{9,1},{17,25},{25,17},{2,10},{10... | collective-permute-start | bytes 20 | tf_op jit(solution)/shard_map/ppermute | solution.py:39
  9.5 4.9 %collective-permute-start.1 = (s32[2]{0:T(128)S(1)}, s32[2]{0:T(128)S(1)}, u32[]{:S(2)}, u32[]{:S(2)}) collective-permute-start(s32[2]{0:T(128)S(1)} %get-tuple-element.33.here_ref), channel_id=1, source_target_pairs={{0,16},{8,24},{16,0},{24,8},{1,17},{9,25},{17,1},{25,9},{2,18},{10... | collective-permute-start | bytes 32 | tf_op jit(solution)/shard_map/ppermute | solution.py:39
  11.0 11.5 %collective-permute-start.3 = (bf16[256,256]{1,0:T(8,128)(2,1)S(1)}, bf16[256,256]{1,0:T(8,128)(2,1)S(1)}, u32[]{:S(2)}, u32[]{:S(2)}) collective-permute-start(bf16[256,256]{1,0:T(8,128)(2,1)S(1)} %get-tuple-element.48), channel_id=1, source_target_pairs={{0,4},{1,5},{2,6},{3,7},{4,0},{5,1},{6,2},{7,3},{8,12},{9,13},{10,... | collective-permute-start | bytes 393224 | tf_op jit(solution)/shard_map/ppermute | solution.py:34
  11.4 11.0 %collective-permute-start.5 = (bf16[128,256]{1,0:T(8,128)(2,1)S(1)}, bf16[128,256]{1,0:T(8,128)(2,1)S(1)}, u32[]{:S(2)}, u32[]{:S(2)}) collective-permute-start(bf16[128,256]{1,0:T(8,128)(2,1)S(1)} %get-tuple-element.53), channel_id=1, source_target_pairs={{0,2},{1,3},{2,0},{3,1},{4,6},{5,7},{6,4},{7,5},{8,10},{9,11},{10,... | collective-permute-start | bytes 196616 | tf_op jit(solution)/shard_map/ppermute | solution.py:39
  13.0 9.4 %collective-permute-start.6 = (bf16[128,256]{1,0:T(8,128)(2,1)S(1)}, bf16[128,256]{1,0:T(8,128)(2,1)S(1)}, u32[]{:S(2)}, u32[]{:S(2)}) collective-permute-start(bf16[128,256]{1,0:T(8,128)(2,1)S(1)} %get-tuple-element.54), channel_id=1, source_target_pairs={{0,3},{1,2},{2,1},{3,0},{4,7},{5,6},{6,5},{7,4},{8,11},{9,10},{10,... | collective-permute-start | bytes 196616 | tf_op jit(solution)/shard_map/ppermute | solution.py:39
  14.4 8.0 %collective-permute-start.7 = (bf16[128,256]{1,0:T(8,128)(2,1)S(1)}, bf16[128,256]{1,0:T(8,128)(2,1)S(1)}, u32[]{:S(2)}, u32[]{:S(2)}) collective-permute-start(bf16[128,256]{1,0:T(8,128)(2,1)S(1)} %get-tuple-element.55), channel_id=1, source_target_pairs={{0,1},{1,0},{2,3},{3,2},{4,5},{5,4},{6,7},{7,6},{8,9},{9,8},{10,11... | collective-permute-start | bytes 196616 | tf_op jit(solution)/shard_map/ppermute | solution.py:39
  22.3 8.0 %collective-permute-start.4 = (bf16[256,256]{1,0:T(8,128)(2,1)S(1)}, bf16[256,256]{1,0:T(8,128)(2,1)S(1)}, u32[]{:S(2)}, u32[]{:S(2)}) collective-permute-start(bf16[256,256]{1,0:T(8,128)(2,1)S(1)} %get-tuple-element.49), channel_id=1, source_target_pairs={{0,4},{1,5},{2,6},{3,7},{4,0},{5,1},{6,2},{7,3},{8,12},{9,13},{10,... | collective-permute-start | bytes 393224 | tf_op jit(solution)/shard_map/ppermute | solution.py:34
  22.5 9.6 %collective-permute-start.10 = (bf16[128,256]{1,0:T(8,128)(2,1)S(1)}, bf16[128,256]{1,0:T(8,128)(2,1)S(1)}, u32[]{:S(2)}, u32[]{:S(2)}) collective-permute-start(bf16[128,256]{1,0:T(8,128)(2,1)S(1)} %get-tuple-element.60), channel_id=1, source_target_pairs={{0,1},{1,0},{2,3},{3,2},{4,5},{5,4},{6,7},{7,6},{8,9},{9,8},{10,11... | collective-permute-start | bytes 196616 | tf_op jit(solution)/shard_map/ppermute | solution.py:39
  24.3 7.8 %collective-permute-start.8 = (bf16[128,256]{1,0:T(8,128)(2,1)S(1)}, bf16[128,256]{1,0:T(8,128)(2,1)S(1)}, u32[]{:S(2)}, u32[]{:S(2)}) collective-permute-start(bf16[128,256]{1,0:T(8,128)(2,1)S(1)} %get-tuple-element.58), channel_id=1, source_target_pairs={{0,2},{1,3},{2,0},{3,1},{4,6},{5,7},{6,4},{7,5},{8,10},{9,11},{10,... | collective-permute-start | bytes 196616 | tf_op jit(solution)/shard_map/ppermute | solution.py:39
  27.4 5.2 %collective-permute-start.9 = (bf16[128,256]{1,0:T(8,128)(2,1)S(1)}, bf16[128,256]{1,0:T(8,128)(2,1)S(1)}, u32[]{:S(2)}, u32[]{:S(2)}) collective-permute-start(bf16[128,256]{1,0:T(8,128)(2,1)S(1)} %get-tuple-element.59), channel_id=1, source_target_pairs={{0,3},{1,2},{2,1},{3,0},{4,7},{5,6},{6,5},{7,4},{8,11},{9,10},{10,... | collective-permute-start | bytes 196616 | tf_op jit(solution)/shard_map/ppermute | solution.py:39

commit v7 on v6

--- a/solution.py
+++ b/solution.py
@@ -153,33 +153,30 @@
     return member // HEAD_DIVISIONS, member % HEAD_DIVISIONS
 
 
-def prepare(queries, keys, values, table, decode_rank, owner, tables, own_length, near_length):
+def prepare(keys, values, table, decode_rank, owner, tables):
     rows, width = keys.shape
     block_len = rows // 2
     slots = table.shape[1]
     residues = decode_rank.shape[1]
     piece = rows // residues
     first = block_len // slots
-    arrays = (keys, values, queries, *tables, table, decode_rank, owner)
+    arrays = (keys, values, *tables, table, decode_rank, owner)
     count = len(arrays)
     facts_of = lambda ref: Facts(ref, slots, residues, owner.shape[0])
 
-    def body(own_ref, near_ref, *refs):
+    def body(*refs):
         inputs, refs = refs[:count], refs[count:]
-        facts_ref, pair_ref, q_ref, kr_ref, v_ref, row_ref, blk_ref, select_ref, order_ref = refs[:9]
-        e_refs, refs = refs[9:13], refs[13:]
+        facts_ref, kr_ref, v_ref, row_ref, blk_ref, select_ref, order_ref = refs[:7]
+        e_refs, refs = refs[7:11], refs[11:]
         sent_refs, refs = refs[: 2 * slots - 2], refs[2 * slots - 2 :]
         k_ref, map_ref, rank_ref, owner_ref, sems = refs
-        targets = (k_ref, v_ref, q_ref, row_ref, blk_ref, map_ref, rank_ref, owner_ref)
+        targets = (k_ref, v_ref, row_ref, blk_ref, map_ref, rank_ref, owner_ref)
         copies = []
         for index in range(count):
             copies.append(pltpu.make_async_copy(inputs[index], targets[index], sems.at[index]))
             copies[-1].start()
         slot, head_group = slot_and_head_group()
-        odd = lax.axis_index("req") % 2 == 1
-        pair_ref[0] = jnp.where(odd, near_ref[0], own_ref[0])
-        pair_ref[1] = jnp.where(odd, own_ref[0], near_ref[0])
-        for index in (0, 3, 4, 5, 6, 7):
+        for index in (0, 2, 3, 4, 5, 6):
             copies[index].wait()
         facts_of(facts_ref).store(map_ref, rank_ref, owner_ref)
         for half in range(2):
@@ -212,12 +209,9 @@
             chosen = dot(select, source[...]).astype(bf16)
             for m in range(HEAD_DIVISIONS):
                 e_refs[m][columns(kind, piece)] = chosen[columns(m, piece)]
-        copies[2].wait()
 
     shapes = [
         jax.ShapeDtypeStruct((1, facts_of(None).size), jnp.int32),
-        jax.ShapeDtypeStruct((2,), jnp.int32),
-        jax.ShapeDtypeStruct(queries.shape, bf16),
         jax.ShapeDtypeStruct(keys.shape, bf16),
         jax.ShapeDtypeStruct(values.shape, bf16),
         jax.ShapeDtypeStruct(tables[0].shape, f32),
@@ -235,16 +229,25 @@
     outs = call(
         body,
         shapes,
-        [SMEM] * 2 + [HBM] * count,
+        [HBM] * count,
         "prepare",
         scratch,
-        out_specs=[SMEM] * 2 + [VMEM] * (len(shapes) - 2),
-    )(own_length, near_length, *in_hbm(arrays))
-    return outs[0], facts_of, outs[1], outs[2:5], outs[5:7], outs[7:9], outs[9:13], outs[13:]
-
-
-def own_part(facts_row, facts_of, operands, tables, lens):
-    queries = operands[0]
+        out_specs=[SMEM] + [VMEM] * (len(shapes) - 1),
+    )(*in_hbm(arrays))
+    return outs[0], facts_of, outs[1:3], outs[3:5], outs[5:7], outs[7:11], outs[11:]
+
+
+def pair_up(own_length, near_length):
+    def body(own_ref, near_ref, pair_ref):
+        odd = lax.axis_index("req") % 2 == 1
+        pair_ref[0] = jnp.where(odd, near_ref[0], own_ref[0])
+        pair_ref[1] = jnp.where(odd, own_ref[0], near_ref[0])
+
+    shape = jax.ShapeDtypeStruct((2,), jnp.int32)
+    return call(body, shape, [SMEM] * 2, "pair_up", out_specs=SMEM)(own_length, near_length)
+
+
+def own_part(facts_row, facts_of, queries, operands, tables, lens):
     rows = queries.shape[0]
     block_len = rows // 2
     sizes = facts_of(None)
@@ -252,11 +255,14 @@
     run = block_len // residues
     cache_rows = 2 * slots * run
 
-    def body(facts_ref, here_ref, there_ref, q_ref, kr_ref, v_ref, row_ref, blk_ref, *refs):
-        qr_ref, acc_ref, kept_ref, live_ref, angle_ref = refs
+    def body(facts_ref, here_ref, there_ref, q_hbm, kr_ref, v_ref, row_ref, blk_ref, *refs):
+        qr_ref, acc_ref, kept_ref, live_ref, angle_ref, q_ref, sem = refs
+        copy = pltpu.make_async_copy(q_hbm, q_ref, sem.at[0])
+        copy.start()
         facts = facts_of(facts_ref)
         slot = slot_and_head_group()[0]
         group = lax.axis_index("req")
+        copy.wait()
         for half in range(2):
             part = columns(half, block_len)
             angles = block_angles(row_ref, blk_ref, facts.block(slot, half))
@@ -318,8 +324,10 @@
         jax.ShapeDtypeStruct((rows, HEAD_SIZE), f32),
         jax.ShapeDtypeStruct((slots - 1, 2, 2, block_len, HEAD_SIZE), f32),
     ]
-    return call(body, shapes, [SMEM] * 3 + [VMEM] * 5, "own_part")(
-        facts_row, *lens, *operands, *tables
+    scratch = [pltpu.VMEM(queries.shape, bf16), pltpu.SemaphoreType.DMA((1,))]
+    specs = [SMEM] * 3 + [HBM] + [VMEM] * 4
+    return call(body, shapes, specs, "own_part", scratch)(
+        facts_row, *lens, *in_hbm([queries]), *operands, *tables
     )
 
 
@@ -509,19 +517,12 @@
         return [pieces[0]] + [crossed(pieces[m], "blk", m) for m in HAND_ORDER[1:]]
 
     key_in = to_slots([k] * (slots - 1))
-    facts_row, facts_of, block, operands, tables, (select, order), early, sent = prepare(
-        q,
-        k,
-        v,
-        block_map,
-        decode_rank,
-        group_of_prompt,
-        tables,
-        lengths,
-        crossed(lengths, "req", 1),
+    facts_row, facts_of, operands, tables, (select, order), early, sent = prepare(
+        k, v, block_map, decode_rank, group_of_prompt, tables
     )
     heads = to_slots(sent[0::2])
     early = hand_on(early)
+    block = pair_up(lengths, crossed(lengths, "req", 1))
     span, groups = 2, lax.axis_size("req")
     while 2 * span < groups:
         other = crossed(block, "req", span)
@@ -531,7 +532,7 @@
         )
         span = 2 * span
     lens = (block, crossed(block, "req", span))
-    query_rot, acc, kept, live, angles = own_part(facts_row, facts_of, operands, tables, lens)
+    query_rot, acc, kept, live, angles = own_part(facts_row, facts_of, q, operands, tables, lens)
     key_rot, chosen = receive_keys(key_in, select, order, angles)
     weights, tails = weigh(facts_row, facts_of, query_rot, key_rot, sent[1::2])
     tails = to_slots(tails)

time: 33.8 us -> 33.8 us (level)
  waiting for transfers between devices: 7.49 us -> 5.97 us
  Pallas kernels: 10.4 us -> 11.5 us
  starting transfers between devices: 14.4 us -> 14.8 us
    ppermute x3, waiting for transfers between devices: 6.29 us -> 3.47 us  [shifted(): lax.ppermute(shard, axis, [(i, (i + by) % peers) for i in range(peers)])]
    ppermute x3, starting transfers between devices: 4.51 us -> 6.16 us  [shifted(): lax.ppermute(shard, axis, [(i, (i + by) % peers) for i in range(peers)])]
    ppermute x8, waiting for transfers between devices: 1.2 us -> 2.5 us  [crossed(): return lax.ppermute(shard, axis, [(i, i ^ by) for i in range(peers)])]
    ppermute x8, starting transfers between devices: 9.89 us -> 8.6 us  [crossed(): return lax.ppermute(shard, axis, [(i, i ^ by) for i in range(peers)])]
    pallas_call x2 -> x3, Pallas kernels: 5.71 us -> 6.8 us  [the longest x1 3.43 us: own_part(): call(body, shapes, specs, 'own_part', scratch)]
  transfers between devices with their start and end apart: 11 -> 11, of which waited for: 5 -> 4; matrix products, arithmetic and copies ran while one was open for 0% -> 0% of each run, Pallas kernels for 28% -> 31%
where the time goes in v7:
time: 33.8 us; the launch traced here: 33.6 us
  starting transfers between devices  14.8 us (44%)
  Pallas kernels  11.5 us (34%)
  waiting for transfers between devices  5.97 us (18%)
  between operations  1.36 us (4%)
    ppermute x8, starting transfers between devices, crossed(): return lax.ppermute(shard, axis, [(i, i ^ by) for i in range(peers)])  8.6 us
    ppermute x3, starting transfers between devices, shifted(): lax.ppermute(shard, axis, [(i, (i + by) % peers) for i in range(peers)])  6.16 us
    ppermute x3, waiting for transfers between devices, shifted(): lax.ppermute(shard, axis, [(i, (i + by) % peers) for i in range(peers)])  3.47 us
    pallas_call x1, Pallas kernels, own_part(): call(body, shapes, specs, 'own_part', scratch)  3.43 us
    ppermute x8, waiting for transfers between devices, crossed(): return lax.ppermute(shard, axis, [(i, i ^ by) for i in range(peers)])  2.5 us
    pallas_call x1, Pallas kernels, prepare(): call(body, shapes, [HBM] * count, 'prepare', scratch, out_specs=[SMEM] +...  2.14 us
    pallas_call x1, Pallas kernels, attend(): call(body, shape, specs, 'attend', scratch)  1.88 us
    pallas_call x1, Pallas kernels, weigh(): call(body, shapes, [SMEM] + [VMEM] * (1 + 2 * others), 'weigh')  1.28 us
  transfers between devices with their start and end apart: 11, of which 4 were waited for; matrix products, arithmetic and copies ran while one was open for 0% of the time, Pallas kernels for 31%

profile of v7, /device:TPU:0, one launch (start us, length us, event | category | flops | bytes accessed | tf_op | source)
XLA Modules:
  0.0 33.6 jit_solution(5084440772060293433)
XLA Ops:
  0.6 4.1 %collective-permute-start.2 = (bf16[512,256]{1,0:T(8,128)(2,1)}, bf16[512,256]{1,0:T(8,128)(2,1)S(1)}, u32[]{:S(2)}, u32[]{:S(2)}) collective-permute-start(bf16[512,256]{1,0:T(8,128)(2,1)} %bitcast.8), channel_id=1, source_target_pairs={{0,4},{1,5},{2,6},{3,7},{4,0},{5,1},{6,2},{7,3},{8,12},{9,13},{10,... | collective-permute-start | bytes 786440 | tf_op jit(solution)/shard_map/ppermute | solution.py:34
  4.7 0.0 collective-permute-start
  4.7 2.1 %prepare.1 = (s32[1,16]{1,0:T(1,128)S(1)}, bf16[512,256]{1,0:T(8,128)(2,1)S(1)}, bf16[512,256]{1,0:T(8,128)(2,1)S(1)}, f32[2,256,128]{2,1,0:T(8,128)S(1)}, f32[2...) custom-call(bf16[512,256]{1,0:T(8,128)(2,1)} %bitcast.9, ...), custom_call_target="tpu_custom_call" | custom-call | flops 1000 | bytes 1000 | tf_op jit(solution)/shard_map/prepare/pallas_call | solution.py:229
  6.9 0.2 collective-permute-start.3
  7.0 1.8 %collective-permute-start.5 = (bf16[128,256]{1,0:T(8,128)(2,1)S(1)}, bf16[128,256]{1,0:T(8,128)(2,1)S(1)}, u32[]{:S(2)}, u32[]{:S(2)}) collective-permute-start(bf16[128,256]{1,0:T(8,128)(2,1)S(1)} %get-tuple-element.49), channel_id=1, source_target_pairs={{0,2},{1,3},{2,0},{3,1},{4,6},{5,7},{6,4},{7,5},{8,10},{9,11},{10,... | collective-permute-start | bytes 196616 | tf_op jit(solution)/shard_map/ppermute | solution.py:39
  8.9 1.4 %collective-permute-start.6 = (bf16[128,256]{1,0:T(8,128)(2,1)S(1)}, bf16[128,256]{1,0:T(8,128)(2,1)S(1)}, u32[]{:S(2)}, u32[]{:S(2)}) collective-permute-start(bf16[128,256]{1,0:T(8,128)(2,1)S(1)} %get-tuple-element.50), channel_id=1, source_target_pairs={{0,3},{1,2},{2,1},{3,0},{4,7},{5,6},{6,5},{7,4},{8,11},{9,10},{10,... | collective-permute-start | bytes 196616 | tf_op jit(solution)/shard_map/ppermute | solution.py:39
  10.9 0.0 collective-permute-done.near_ref
  10.9 1.2 %pair_up.1.here_ref = s32[2]{0:T(128)S(1)} custom-call(s32[1]{0:T(128)S(6)} %copy.11.own_ref, s32[1]{0:T(128)} %collective-permute-done.near_ref), custom_call_target="tpu_custom_call" | custom-call | flops 1000 | bytes 1000 | tf_op jit(solution)/shard_map/pair_up/pallas_call | solution.py:247
  12.2 1.6 %collective-permute-start.1 = (s32[2]{0:T(128)S(1)}, s32[2]{0:T(128)S(1)}, u32[]{:S(2)}, u32[]{:S(2)}) collective-permute-start(s32[2]{0:T(128)S(1)} %pair_up.1.here_ref), channel_id=1, source_target_pairs={{0,16},{8,24},{16,0},{24,8},{1,17},{9,25},{17,1},{25,9},{2,18},{10... | collective-permute-start | bytes 32 | tf_op jit(solution)/shard_map/ppermute | solution.py:39
  13.7 2.0 %collective-permute-done.1.there_ref = s32[2]{0:T(128)S(1)} collective-permute-done((s32[2]{0:T(128)S(1)}, s32[2]{0:T(128)S(1)}, u32[]{:S(2)}, u32[]{:S(2)}) %collective-permute-start.1) | collective-permute-done | bytes 40 | tf_op jit(solution)/shard_map/ppermute | solution.py:39
  15.8 0.3 collective-permute-start.7
  16.1 3.4 %own_part.1 = (bf16[512,512]{1,0:T(8,128)(2,1)S(1)}, f32[512,1024]{1,0:T(8,128)S(1)}, bf16[128,128]{1,0:T(8,128)(2,1)S(1)}, f32[512,128]{1,0:T(8,128)S(1)}, f32[1,2,2,256,128]{4,3,2,1,0:T(8,128)S(1)}) custom-call(s32[1,16]{1,0:T(1,128)S(1)} %get-tuple-element.30.facts_ref, s32[2]{0:T(128)S(1)} %pair_up.1.here_ref, s32[2]{0:T(128)S(1)} %collective-permute-done.1.there_ref, ...), custom_call_target="tpu_custom_call" | custom-call | flops 1000 | bytes 1000 | tf_op jit(solution)/shard_map/own_part/pallas_call | solution.py:329
  19.5 1.0 %collective-permute-done.2.refs_0_ = bf16[512,256]{1,0:T(8,128)(2,1)S(1)} collective-permute-done((bf16[512,256]{1,0:T(8,128)(2,1)}, bf16[512,256]{1,0:T(8,128)(2,1)S(1)}, u32[]{:S(2)}, u32[]{:S(2)}) %collective-permute-start.2) | collective-permute-done | bytes 262176 | tf_op jit(solution)/shard_map/ppermute | solution.py:34
  20.5 0.4 %receive_keys.1 = (bf16[512,256]{1,0:T(8,128)(2,1)S(1)}, bf16[1,256,256]{2,1,0:T(8,128)(2,1)S(1)}) custom-call(bf16[256,512]{1,0:T(8,128)(2,1)S(1)} %get-tuple-element.38.select_ref, bf16[256,256]{1,0:T(8,128)(2,1)S(1)} %get-tuple-element.39.order_ref, f32[1,2,2,256,128]{4,3,2,1,0:T(8,128)S(1)} %get-tuple-element.40.angle_ref, ...), custom_call_target="tpu_custom_call" | custom-call | flops 10000000000 | bytes 1000 | tf_op jit(solution)/shard_map/receive_keys/pallas_call | solution.py:365
  20.9 1.3 %weigh.1 = (bf16[2,4,256,256]{3,2,1,0:T(8,128)(2,1)S(1)}, bf16[256,256]{1,0:T(8,128)(2,1)S(1)}) custom-call(s32[1,16]{1,0:T(1,128)S(1)} %get-tuple-element.30.facts_ref, bf16[512,512]{1,0:T(8,128)(2,1)S(1)} %get-tuple-element.37.q_ref, bf16[512,256]{1,0:T(8,128)(2,1)S(1)} %get-tuple-element.41.refs_0_, bf16[256,256]{1,0:T(8,128)(2,1)S(1)} %get-tuple-element.42.refs_1_), custom_call_target="tpu_custom_call" | custom-call | flops 1000 | bytes 1000 | tf_op jit(solution)/shard_map/weigh/pallas_call | solution.py:397
  22.2 1.9 %collective-permute-start.4 = (bf16[256,256]{1,0:T(8,128)(2,1)S(1)}, bf16[256,256]{1,0:T(8,128)(2,1)S(1)}, u32[]{:S(2)}, u32[]{:S(2)}) collective-permute-start(bf16[256,256]{1,0:T(8,128)(2,1)S(1)} %get-tuple-element.45), channel_id=1, source_target_pairs={{0,4},{1,5},{2,6},{3,7},{4,0},{5,1},{6,2},{7,3},{8,12},{9,13},{10,... | collective-permute-start | bytes 393224 | tf_op jit(solution)/shard_map/ppermute | solution.py:34
  24.1 0.0 collective-permute-done.5.refs_1_
  24.1 0.0 collective-permute-done.6.refs_2_
  24.1 0.0 collective-permute-done.7.refs_3_
  24.1 0.0 collective-permute-done.3.refs_1_.refs_0_
  24.2 1.6 %collective-permute-start.10 = (bf16[128,256]{1,0:T(8,128)(2,1)S(1)}, bf16[128,256]{1,0:T(8,128)(2,1)S(1)}, u32[]{:S(2)}, u32[]{:S(2)}) collective-permute-start(bf16[128,256]{1,0:T(8,128)(2,1)S(1)} %get-tuple-element.56), channel_id=1, source_target_pairs={{0,1},{1,0},{2,3},{3,2},{4,5},{5,4},{6,7},{7,6},{8,9},{9,8},{10,11... | collective-permute-start | bytes 196616 | tf_op jit(solution)/shard_map/ppermute | solution.py:39
  25.8 1.6 %collective-permute-start.8 = (bf16[128,256]{1,0:T(8,128)(2,1)S(1)}, bf16[128,256]{1,0:T(8,128)(2,1)S(1)}, u32[]{:S(2)}, u32[]{:S(2)}) collective-permute-start(bf16[128,256]{1,0:T(8,128)(2,1)S(1)} %get-tuple-element.54), channel_id=1, source_target_pairs={{0,2},{1,3},{2,0},{3,1},{4,6},{5,7},{6,4},{7,5},{8,10},{9,11},{10,... | collective-permute-start | bytes 196616 | tf_op jit(solution)/shard_map/ppermute | solution.py:39
  27.3 0.4 %collective-permute-start.9 = (bf16[128,256]{1,0:T(8,128)(2,1)S(1)}, bf16[128,256]{1,0:T(8,128)(2,1)S(1)}, u32[]{:S(2)}, u32[]{:S(2)}) collective-permute-start(bf16[128,256]{1,0:T(8,128)(2,1)S(1)} %get-tuple-element.55), channel_id=1, source_target_pairs={{0,3},{1,2},{2,1},{3,0},{4,7},{5,6},{6,5},{7,4},{8,11},{9,10},{10,... | collective-permute-start | bytes 196616 | tf_op jit(solution)/shard_map/ppermute | solution.py:39
  27.7 2.5 %collective-permute-done.4.refs_2_ = bf16[256,256]{1,0:T(8,128)(2,1)S(1)} collective-permute-done((bf16[256,256]{1,0:T(8,128)(2,1)S(1)}, bf16[256,256]{1,0:T(8,128)(2,1)S(1)}, u32[]{:S(2)}, u32[]{:S(2)}) %collective-permute-start.4) | collective-permute-done | bytes 131104 | tf_op jit(solution)/shard_map/ppermute | solution.py:34
  30.2 1.9 %attend.1 = (bf16[512,512]{1,0:T(8,128)(2,1)}, f32[8,128]{1,0:T(8,128)S(1)}) custom-call(s32[1,16]{1,0:T(1,128)S(1)} %get-tuple-element.30.facts_ref, f32[512,1024]{1,0:T(8,128)S(1)} %get-tuple-element.35.acc_ref, f32[512,128]{1,0:T(8,128)S(1)} %get-tuple-element.36.live_ref, bf16[2,4,256,256]{3,2,1,0:T(8,128)(2,1)S(1)} %get-tuple-element.43.refs_0_, ...), custom_call_target="tpu_custom_call" | custom-call | flops 1000 | bytes 1000 | tf_op jit(solution)/shard_map/attend/pallas_call | solution.py:479
  32.1 0.0 collective-permute-done.10.refs_7_
  32.1 0.0 collective-permute-done.8.refs_5_
  32.1 0.4 %collective-permute-done.9.refs_6_ = bf16[128,256]{1,0:T(8,128)(2,1)S(1)} collective-permute-done((bf16[128,256]{1,0:T(8,128)(2,1)S(1)}, bf16[128,256]{1,0:T(8,128)(2,1)S(1)}, u32[]{:S(2)}, u32[]{:S(2)}) %collective-permute-start.9) | collective-permute-done | bytes 65568 | tf_op jit(solution)/shard_map/ppermute | solution.py:39
  32.5 1.1 %cache_part.1 = bf16[128,2048]{1,0:T(8,128)(2,1)} custom-call(bf16[128,128]{1,0:T(8,128)(2,1)S(1)} %get-tuple-element.47.kept_ref, bf16[128,256]{1,0:T(8,128)(2,1)S(1)} %get-tuple-element.48.refs_0_, bf16[128,256]{1,0:T(8,128)(2,1)S(1)} %collective-permute-done.5.refs_1_, bf16[128,256]{1,0:T(8,128)(2,1)S(1)} %collective-permute-done.6.refs_2_, ...), custom_call_target="tpu_custom_call" | custom-call | flops 1000 | bytes 1000 | tf_op jit(solution)/shard_map/cache_part/pallas_call | solution.py:504
  (1 shorter events, 0.0 us)
Async XLA Ops:
  0.6 19.9 %collective-permute-start.2 = (bf16[512,256]{1,0:T(8,128)(2,1)}, bf16[512,256]{1,0:T(8,128)(2,1)S(1)}, u32[]{:S(2)}, u32[]{:S(2)}) collective-permute-start(bf16[512,256]{1,0:T(8,128)(2,1)} %bitcast.8), channel_id=1, source_target_pairs={{0,4},{1,5},{2,6},{3,7},{4,0},{5,1},{6,2},{7,3},{8,12},{9,13},{10,... | collective-permute-start | bytes 786440 | tf_op jit(solution)/shard_map/ppermute | solution.py:34
  4.7 6.2 %collective-permute-start = (s32[1]{0:T(128)}, s32[1]{0:T(128)}, u32[]{:S(2)}, u32[]{:S(2)}) collective-permute-start(s32[1]{0:T(128)} %param.13), channel_id=1, source_target_pairs={{0,8},{8,0},{16,24},{24,16},{1,9},{9,1},{17,25},{25,17},{2,10},{10... | collective-permute-start | bytes 20 | tf_op jit(solution)/shard_map/ppermute | solution.py:39
  6.9 17.3 %collective-permute-start.3 = (bf16[256,256]{1,0:T(8,128)(2,1)S(1)}, bf16[256,256]{1,0:T(8,128)(2,1)S(1)}, u32[]{:S(2)}, u32[]{:S(2)}) collective-permute-start(bf16[256,256]{1,0:T(8,128)(2,1)S(1)} %get-tuple-element.44), channel_id=1, source_target_pairs={{0,4},{1,5},{2,6},{3,7},{4,0},{5,1},{6,2},{7,3},{8,12},{9,13},{10,... | collective-permute-start | bytes 393224 | tf_op jit(solution)/shard_map/ppermute | solution.py:34
  7.0 17.1 %collective-permute-start.5 = (bf16[128,256]{1,0:T(8,128)(2,1)S(1)}, bf16[128,256]{1,0:T(8,128)(2,1)S(1)}, u32[]{:S(2)}, u32[]{:S(2)}) collective-permute-start(bf16[128,256]{1,0:T(8,128)(2,1)S(1)} %get-tuple-element.49), channel_id=1, source_target_pairs={{0,2},{1,3},{2,0},{3,1},{4,6},{5,7},{6,4},{7,5},{8,10},{9,11},{10,... | collective-permute-start | bytes 196616 | tf_op jit(solution)/shard_map/ppermute | solution.py:39
  8.9 15.3 %collective-permute-start.6 = (bf16[128,256]{1,0:T(8,128)(2,1)S(1)}, bf16[128,256]{1,0:T(8,128)(2,1)S(1)}, u32[]{:S(2)}, u32[]{:S(2)}) collective-permute-start(bf16[128,256]{1,0:T(8,128)(2,1)S(1)} %get-tuple-element.50), channel_id=1, source_target_pairs={{0,3},{1,2},{2,1},{3,0},{4,7},{5,6},{6,5},{7,4},{8,11},{9,10},{10,... | collective-permute-start | bytes 196616 | tf_op jit(solution)/shard_map/ppermute | solution.py:39
  12.2 3.6 %collective-permute-start.1 = (s32[2]{0:T(128)S(1)}, s32[2]{0:T(128)S(1)}, u32[]{:S(2)}, u32[]{:S(2)}) collective-permute-start(s32[2]{0:T(128)S(1)} %pair_up.1.here_ref), channel_id=1, source_target_pairs={{0,16},{8,24},{16,0},{24,8},{1,17},{9,25},{17,1},{25,9},{2,18},{10... | collective-permute-start | bytes 32 | tf_op jit(solution)/shard_map/ppermute | solution.py:39
  15.8 8.3 %collective-permute-start.7 = (bf16[128,256]{1,0:T(8,128)(2,1)S(1)}, bf16[128,256]{1,0:T(8,128)(2,1)S(1)}, u32[]{:S(2)}, u32[]{:S(2)}) collective-permute-start(bf16[128,256]{1,0:T(8,128)(2,1)S(1)} %get-tuple-element.51), channel_id=1, source_target_pairs={{0,1},{1,0},{2,3},{3,2},{4,5},{5,4},{6,7},{7,6},{8,9},{9,8},{10,11... | collective-permute-start | bytes 196616 | tf_op jit(solution)/shard_map/ppermute | solution.py:39
  22.2 8.0 %collective-permute-start.4 = (bf16[256,256]{1,0:T(8,128)(2,1)S(1)}, bf16[256,256]{1,0:T(8,128)(2,1)S(1)}, u32[]{:S(2)}, u32[]{:S(2)}) collective-permute-start(bf16[256,256]{1,0:T(8,128)(2,1)S(1)} %get-tuple-element.45), channel_id=1, source_target_pairs={{0,4},{1,5},{2,6},{3,7},{4,0},{5,1},{6,2},{7,3},{8,12},{9,13},{10,... | collective-permute-start | bytes 393224 | tf_op jit(solution)/shard_map/ppermute | solution.py:34
  24.2 7.9 %collective-permute-start.10 = (bf16[128,256]{1,0:T(8,128)(2,1)S(1)}, bf16[128,256]{1,0:T(8,128)(2,1)S(1)}, u32[]{:S(2)}, u32[]{:S(2)}) collective-permute-start(bf16[128,256]{1,0:T(8,128)(2,1)S(1)} %get-tuple-element.56), channel_id=1, source_target_pairs={{0,1},{1,0},{2,3},{3,2},{4,5},{5,4},{6,7},{7,6},{8,9},{9,8},{10,11... | collective-permute-start | bytes 196616 | tf_op jit(solution)/shard_map/ppermute | solution.py:39
  25.8 6.3 %collective-permute-start.8 = (bf16[128,256]{1,0:T(8,128)(2,1)S(1)}, bf16[128,256]{1,0:T(8,128)(2,1)S(1)}, u32[]{:S(2)}, u32[]{:S(2)}) collective-permute-start(bf16[128,256]{1,0:T(8,128)(2,1)S(1)} %get-tuple-element.54), channel_id=1, source_target_pairs={{0,2},{1,3},{2,0},{3,1},{4,6},{5,7},{6,4},{7,5},{8,10},{9,11},{10,... | collective-permute-start | bytes 196616 | tf_op jit(solution)/shard_map/ppermute | solution.py:39
  27.3 5.2 %collective-permute-start.9 = (bf16[128,256]{1,0:T(8,128)(2,1)S(1)}, bf16[128,256]{1,0:T(8,128)(2,1)S(1)}, u32[]{:S(2)}, u32[]{:S(2)}) collective-permute-start(bf16[128,256]{1,0:T(8,128)(2,1)S(1)} %get-tuple-element.55), channel_id=1, source_target_pairs={{0,3},{1,2},{2,1},{3,0},{4,7},{5,6},{6,5},{7,4},{8,11},{9,10},{10,... | collective-permute-start | bytes 196616 | tf_op jit(solution)/shard_map/ppermute | solution.py:39

commit v8 on v7

--- a/solution.py
+++ b/solution.py
@@ -247,21 +247,17 @@
     return call(body, shape, [SMEM] * 2, "pair_up", out_specs=SMEM)(own_length, near_length)
 
 
-def own_part(facts_row, facts_of, queries, operands, tables, lens):
+def own_part(facts_row, facts_of, queries, operands, tables):
     rows = queries.shape[0]
     block_len = rows // 2
-    sizes = facts_of(None)
-    slots, residues, groups = sizes.slots, sizes.residues, sizes.groups
-    run = block_len // residues
-    cache_rows = 2 * slots * run
-
-    def body(facts_ref, here_ref, there_ref, q_hbm, kr_ref, v_ref, row_ref, blk_ref, *refs):
-        qr_ref, acc_ref, kept_ref, live_ref, angle_ref, q_ref, sem = refs
+    slots = facts_of(None).slots
+
+    def body(facts_ref, q_hbm, kr_ref, v_ref, row_ref, blk_ref, *refs):
+        qr_ref, acc_ref, angle_ref, q_ref, sem = refs
         copy = pltpu.make_async_copy(q_hbm, q_ref, sem.at[0])
         copy.start()
         facts = facts_of(facts_ref)
         slot = slot_and_head_group()[0]
-        group = lax.axis_index("req")
         copy.wait()
         for half in range(2):
             part = columns(half, block_len)
@@ -292,6 +288,29 @@
             acc_ref[low, both] = tile(low, low, True)
             acc_ref[high, both] = tile(high, high, True) + tile(high, low, False)
 
+    shapes = [
+        jax.ShapeDtypeStruct(queries.shape, bf16),
+        jax.ShapeDtypeStruct((rows, 2 * Q_DEV * HEAD_SIZE), f32),
+        jax.ShapeDtypeStruct((slots - 1, 2, 2, block_len, HEAD_SIZE), f32),
+    ]
+    scratch = [pltpu.VMEM(queries.shape, bf16), pltpu.SemaphoreType.DMA((1,))]
+    specs = [SMEM] + [HBM] + [VMEM] * 4
+    return call(body, shapes, specs, "own_part", scratch)(
+        facts_row, *in_hbm([queries]), *operands, *tables
+    )
+
+
+def masks_of(facts_row, facts_of, rows, lens):
+    block_len = rows // 2
+    sizes = facts_of(None)
+    slots, residues, groups = sizes.slots, sizes.residues, sizes.groups
+    run = block_len // residues
+    cache_rows = 2 * slots * run
+
+    def body(facts_ref, here_ref, there_ref, kept_ref, live_ref):
+        facts = facts_of(facts_ref)
+        slot = slot_and_head_group()[0]
+        group = lax.axis_index("req")
         col = lax.broadcasted_iota(jnp.int32, (1, cache_rows), 1)
         part, offset = col // run, col % run
         target = jnp.zeros_like(col)
@@ -318,17 +337,10 @@
             live_ref[columns(half, block_len)] = jnp.where(at < length, 1.0, 0.0)
 
     shapes = [
-        jax.ShapeDtypeStruct(queries.shape, bf16),
-        jax.ShapeDtypeStruct((rows, 2 * Q_DEV * HEAD_SIZE), f32),
         jax.ShapeDtypeStruct((cache_rows, cache_rows), bf16),
         jax.ShapeDtypeStruct((rows, HEAD_SIZE), f32),
-        jax.ShapeDtypeStruct((slots - 1, 2, 2, block_len, HEAD_SIZE), f32),
     ]
-    scratch = [pltpu.VMEM(queries.shape, bf16), pltpu.SemaphoreType.DMA((1,))]
-    specs = [SMEM] * 3 + [HBM] + [VMEM] * 4
-    return call(body, shapes, specs, "own_part", scratch)(
-        facts_row, *lens, *in_hbm([queries]), *operands, *tables
-    )
+    return call(body, shapes, [SMEM] * 3, "masks")(facts_row, *lens)
 
 
 def tiles_of(facts, slot, source):
@@ -532,11 +544,12 @@
         )
         span = 2 * span
     lens = (block, crossed(block, "req", span))
-    query_rot, acc, kept, live, angles = own_part(facts_row, facts_of, q, operands, tables, lens)
+    query_rot, acc, angles = own_part(facts_row, facts_of, q, operands, tables)
+    kept, live = masks_of(facts_row, facts_of, q.shape[0], lens)
     key_rot, chosen = receive_keys(key_in, select, order, angles)
     weights, tails = weigh(facts_row, facts_of, query_rot, key_rot, sent[1::2])
     tails = to_slots(tails)
-    late = hand_on(late_pieces(heads, chosen, early[1:]))
+    late = hand_on(late_pieces(heads, chosen, early[1:] + [live]))
     attended, mark = attend(facts_row, facts_of, weights, acc, heads, tails, live)
     cache = cache_part(early, late, kept, mark)
     return (attended[None, None], cache[None])

time: 33.8 us -> 35.5 us (1.050)
  waiting for transfers between devices: 5.97 us -> 7.22 us
  Pallas kernels: 11.5 us -> 12.1 us
    ppermute x3, waiting for transfers between devices: 3.47 us -> 6.21 us  [shifted(): lax.ppermute(shard, axis, [(i, (i + by) % peers) for i in range(peers)])]
    ppermute x3, starting transfers between devices: 6.16 us -> 4.34 us  [shifted(): lax.ppermute(shard, axis, [(i, (i + by) % peers) for i in range(peers)])]
    ppermute x8, starting transfers between devices: 8.6 us -> 10.3 us  [crossed(): return lax.ppermute(shard, axis, [(i, i ^ by) for i in range(peers)])]
    ppermute x8, waiting for transfers between devices: 2.5 us -> 1.01 us  [crossed(): return lax.ppermute(shard, axis, [(i, i ^ by) for i in range(peers)])]
    pallas_call x0 -> x1, Pallas kernels: none -> 0.62 us  [masks_of(): return call(body, shapes, [SMEM] * 3, 'masks')(facts_row, *lens)]
where the time goes in v8:
time: 35.5 us; the launch traced here: 35.3 us
  starting transfers between devices  14.6 us (41%)
  Pallas kernels  12.1 us (34%)
  waiting for transfers between devices  7.22 us (20%)
  between operations  1.4 us (4%)
    ppermute x8, starting transfers between devices, crossed(): return lax.ppermute(shard, axis, [(i, i ^ by) for i in range(peers)])  10.3 us
    ppermute x3, waiting for transfers between devices, shifted(): lax.ppermute(shard, axis, [(i, (i + by) % peers) for i in range(peers)])  6.21 us
    ppermute x3, starting transfers between devices, shifted(): lax.ppermute(shard, axis, [(i, (i + by) % peers) for i in range(peers)])  4.34 us
    pallas_call x1, Pallas kernels, own_part(): call(body, shapes, specs, 'own_part', scratch)  3.47 us
    pallas_call x1, Pallas kernels, prepare(): call(body, shapes, [HBM] * count, 'prepare', scratch, out_specs=[SMEM] +...  2.13 us
    pallas_call x1, Pallas kernels, attend(): call(body, shape, specs, 'attend', scratch)  1.9 us
    pallas_call x1, Pallas kernels, weigh(): call(body, shapes, [SMEM] + [VMEM] * (1 + 2 * others), 'weigh')  1.28 us
    pallas_call x1, Pallas kernels, pair_up(): call(body, shape, [SMEM] * 2, 'pair_up', out_specs=SMEM)  1.15 us
  transfers between devices with their start and end apart: 11, of which 4 were waited for; matrix products, arithmetic and copies ran while one was open for 0% of the time, Pallas kernels for 31%

profile of v8, /device:TPU:0, one launch (start us, length us, event | category | flops | bytes accessed | tf_op | source)
XLA Modules:
  0.0 35.3 jit_solution(10575425391247670384)
XLA Ops:
  0.6 4.1 %collective-permute-start.2 = (bf16[512,256]{1,0:T(8,128)(2,1)}, bf16[512,256]{1,0:T(8,128)(2,1)S(1)}, u32[]{:S(2)}, u32[]{:S(2)}) collective-permute-start(bf16[512,256]{1,0:T(8,128)(2,1)} %bitcast.8), channel_id=1, source_target_pairs={{0,4},{1,5},{2,6},{3,7},{4,0},{5,1},{6,2},{7,3},{8,12},{9,13},{10,... | collective-permute-start | bytes 786440 | tf_op jit(solution)/shard_map/ppermute | solution.py:34
  4.7 0.0 collective-permute-start
  4.7 2.1 %prepare.1 = (s32[1,16]{1,0:T(1,128)S(1)}, bf16[512,256]{1,0:T(8,128)(2,1)S(1)}, bf16[512,256]{1,0:T(8,128)(2,1)S(1)}, f32[2,256,128]{2,1,0:T(8,128)S(1)}, f32[2...) custom-call(bf16[512,256]{1,0:T(8,128)(2,1)} %bitcast.9, ...), custom_call_target="tpu_custom_call" | custom-call | flops 1000 | bytes 1000 | tf_op jit(solution)/shard_map/prepare/pallas_call | solution.py:229
  6.9 0.2 collective-permute-start.3
  7.0 1.8 %collective-permute-start.5 = (bf16[128,256]{1,0:T(8,128)(2,1)S(1)}, bf16[128,256]{1,0:T(8,128)(2,1)S(1)}, u32[]{:S(2)}, u32[]{:S(2)}) collective-permute-start(bf16[128,256]{1,0:T(8,128)(2,1)S(1)} %get-tuple-element.49), channel_id=1, source_target_pairs={{0,2},{1,3},{2,0},{3,1},{4,6},{5,7},{6,4},{7,5},{8,10},{9,11},{10,... | collective-permute-start | bytes 196616 | tf_op jit(solution)/shard_map/ppermute | solution.py:39
  8.9 1.4 %collective-permute-start.6 = (bf16[128,256]{1,0:T(8,128)(2,1)S(1)}, bf16[128,256]{1,0:T(8,128)(2,1)S(1)}, u32[]{:S(2)}, u32[]{:S(2)}) collective-permute-start(bf16[128,256]{1,0:T(8,128)(2,1)S(1)} %get-tuple-element.50), channel_id=1, source_target_pairs={{0,3},{1,2},{2,1},{3,0},{4,7},{5,6},{6,5},{7,4},{8,11},{9,10},{10,... | collective-permute-start | bytes 196616 | tf_op jit(solution)/shard_map/ppermute | solution.py:39
  10.3 3.5 %own_part.1 = (bf16[512,512]{1,0:T(8,128)(2,1)S(1)}, f32[512,1024]{1,0:T(8,128)S(1)}, f32[1,2,2,256,128]{4,3,2,1,0:T(8,128)S(1)}) custom-call(s32[1,16]{1,0:T(1,128)S(1)} %get-tuple-element.30.facts_ref, bf16[512,512]{1,0:T(8,128)(2,1)} %bitcast.5, bf16[512,256]{1,0:T(8,128)(2,1)S(1)} %get-tuple-element.31.kr_ref, ...), custom_call_target="tpu_custom_call" | custom-call | flops 1000 | bytes 1000 | tf_op jit(solution)/shard_map/own_part/pallas_call | solution.py:298
  14.4 0.0 collective-permute-done.near_ref
  14.4 0.3 collective-permute-start.7
  14.7 1.2 %pair_up.1.here_ref = s32[2]{0:T(128)S(1)} custom-call(s32[1]{0:T(128)S(6)} %copy.11.own_ref, s32[1]{0:T(128)} %collective-permute-done.near_ref), custom_call_target="tpu_custom_call" | custom-call | flops 1000 | bytes 1000 | tf_op jit(solution)/shard_map/pair_up/pallas_call | solution.py:247
  15.9 4.6 %collective-permute-done.2.refs_0_ = bf16[512,256]{1,0:T(8,128)(2,1)S(1)} collective-permute-done((bf16[512,256]{1,0:T(8,128)(2,1)}, bf16[512,256]{1,0:T(8,128)(2,1)S(1)}, u32[]{:S(2)}, u32[]{:S(2)}) %collective-permute-start.2) | collective-permute-done | bytes 262176 | tf_op jit(solution)/shard_map/ppermute | solution.py:34
  20.5 1.8 %collective-permute-start.1 = (s32[2]{0:T(128)S(1)}, s32[2]{0:T(128)S(1)}, u32[]{:S(2)}, u32[]{:S(2)}) collective-permute-start(s32[2]{0:T(128)S(1)} %pair_up.1.here_ref), channel_id=1, source_target_pairs={{0,16},{8,24},{16,0},{24,8},{1,17},{9,25},{17,1},{25,9},{2,18},{10... | collective-permute-start | bytes 32 | tf_op jit(solution)/shard_map/ppermute | solution.py:39
  22.3 0.4 %receive_keys.1 = (bf16[512,256]{1,0:T(8,128)(2,1)S(1)}, bf16[1,256,256]{2,1,0:T(8,128)(2,1)S(1)}) custom-call(bf16[256,512]{1,0:T(8,128)(2,1)S(1)} %get-tuple-element.38.select_ref, bf16[256,256]{1,0:T(8,128)(2,1)S(1)} %get-tuple-element.39.order_ref, f32[1,2,2,256,128]{4,3,2,1,0:T(8,128)S(1)} %get-tuple-element.40.angle_ref, ...), custom_call_target="tpu_custom_call" | custom-call | flops 10000000000 | bytes 1000 | tf_op jit(solution)/shard_map/receive_keys/pallas_call | solution.py:377
  22.8 1.3 %weigh.1 = (bf16[2,4,256,256]{3,2,1,0:T(8,128)(2,1)S(1)}, bf16[256,256]{1,0:T(8,128)(2,1)S(1)}) custom-call(s32[1,16]{1,0:T(1,128)S(1)} %get-tuple-element.30.facts_ref, bf16[512,512]{1,0:T(8,128)(2,1)S(1)} %get-tuple-element.37.q_ref, bf16[512,256]{1,0:T(8,128)(2,1)S(1)} %get-tuple-element.41.refs_0_, bf16[256,256]{1,0:T(8,128)(2,1)S(1)} %get-tuple-element.42.refs_1_), custom_call_target="tpu_custom_call" | custom-call | flops 1000 | bytes 1000 | tf_op jit(solution)/shard_map/weigh/pallas_call | solution.py:409
  24.1 0.0 collective-permute-done.1.there_ref
  24.1 0.1 collective-permute-start.4
  24.1 0.6 %masks.1 = (bf16[128,128]{1,0:T(8,128)(2,1)S(1)}, f32[512,128]{1,0:T(8,128)S(1)}) custom-call(s32[1,16]{1,0:T(1,128)S(1)} %get-tuple-element.30.facts_ref, s32[2]{0:T(128)S(1)} %pair_up.1.here_ref, s32[2]{0:T(128)S(1)} %collective-permute-done.1.there_ref), custom_call_target="tpu_custom_call" | custom-call | flops 1000 | bytes 1000 | tf_op jit(solution)/shard_map/masks/pallas_call | solution.py:343
  24.8 0.0 collective-permute-done.5.refs_1_
  24.8 0.0 collective-permute-done.6.refs_2_
  24.8 0.0 collective-permute-done.7.refs_3_
  24.8 0.0 collective-permute-done.3.refs_1_.refs_0_
  24.8 3.3 %collective-permute-start.8 = (bf16[128,256]{1,0:T(8,128)(2,1)S(1)}, bf16[128,256]{1,0:T(8,128)(2,1)S(1)}, u32[]{:S(2)}, u32[]{:S(2)}) collective-permute-start(bf16[128,256]{1,0:T(8,128)(2,1)S(1)} %get-tuple-element.54), channel_id=1, source_target_pairs={{0,2},{1,3},{2,0},{3,1},{4,6},{5,7},{6,4},{7,5},{8,10},{9,11},{10,... | collective-permute-start | bytes 196616 | tf_op jit(solution)/shard_map/ppermute | solution.py:39
  28.2 1.0 %collective-permute-start.9 = (bf16[128,256]{1,0:T(8,128)(2,1)S(1)}, bf16[128,256]{1,0:T(8,128)(2,1)S(1)}, u32[]{:S(2)}, u32[]{:S(2)}) collective-permute-start(bf16[128,256]{1,0:T(8,128)(2,1)S(1)} %get-tuple-element.55), channel_id=1, source_target_pairs={{0,3},{1,2},{2,1},{3,0},{4,7},{5,6},{6,5},{7,4},{8,11},{9,10},{10,... | collective-permute-start | bytes 196616 | tf_op jit(solution)/shard_map/ppermute | solution.py:39
  29.2 0.5 %collective-permute-start.10 = (bf16[128,256]{1,0:T(8,128)(2,1)S(1)}, bf16[128,256]{1,0:T(8,128)(2,1)S(1)}, u32[]{:S(2)}, u32[]{:S(2)}) collective-permute-start(bf16[128,256]{1,0:T(8,128)(2,1)S(1)} %get-tuple-element.56), channel_id=1, source_target_pairs={{0,1},{1,0},{2,3},{3,2},{4,5},{5,4},{6,7},{7,6},{8,9},{9,8},{10,11... | collective-permute-start | bytes 196616 | tf_op jit(solution)/shard_map/ppermute | solution.py:39
  29.7 1.6 %collective-permute-done.4.refs_2_ = bf16[256,256]{1,0:T(8,128)(2,1)S(1)} collective-permute-done((bf16[256,256]{1,0:T(8,128)(2,1)S(1)}, bf16[256,256]{1,0:T(8,128)(2,1)S(1)}, u32[]{:S(2)}, u32[]{:S(2)}) %collective-permute-start.4) | collective-permute-done | bytes 131104 | tf_op jit(solution)/shard_map/ppermute | solution.py:34
  31.3 1.9 %attend.1 = (bf16[512,512]{1,0:T(8,128)(2,1)}, f32[8,128]{1,0:T(8,128)S(1)}) custom-call(s32[1,16]{1,0:T(1,128)S(1)} %get-tuple-element.30.facts_ref, f32[512,1024]{1,0:T(8,128)S(1)} %get-tuple-element.35.acc_ref, f32[512,128]{1,0:T(8,128)S(1)} %get-tuple-element.36.live_ref.refs_4_, bf16[2,4,256,256]{3,2,1,0:T(8,128)(2,1)S(1)} %get-tuple-element.43.refs_0_, ...), custom_call_target="tpu_custom_call" | custom-call | flops 1000 | bytes 1000 | tf_op jit(solution)/shard_map/attend/pallas_call | solution.py:491
  33.2 0.0 collective-permute-done.8.refs_5_
  33.2 0.5 %collective-permute-done.9.refs_6_ = bf16[128,256]{1,0:T(8,128)(2,1)S(1)} collective-permute-done((bf16[128,256]{1,0:T(8,128)(2,1)S(1)}, bf16[128,256]{1,0:T(8,128)(2,1)S(1)}, u32[]{:S(2)}, u32[]{:S(2)}) %collective-permute-start.9) | collective-permute-done | bytes 65568 | tf_op jit(solution)/shard_map/ppermute | solution.py:39
  33.8 0.5 %collective-permute-done.10.refs_7_ = bf16[128,256]{1,0:T(8,128)(2,1)S(1)} collective-permute-done((bf16[128,256]{1,0:T(8,128)(2,1)S(1)}, bf16[128,256]{1,0:T(8,128)(2,1)S(1)}, u32[]{:S(2)}, u32[]{:S(2)}) %collective-permute-start.10) | collective-permute-done | bytes 65568 | tf_op jit(solution)/shard_map/ppermute | solution.py:39
  34.2 1.1 %cache_part.1 = bf16[128,2048]{1,0:T(8,128)(2,1)} custom-call(bf16[128,128]{1,0:T(8,128)(2,1)S(1)} %get-tuple-element.47.kept_ref, bf16[128,256]{1,0:T(8,128)(2,1)S(1)} %get-tuple-element.48.refs_0_, bf16[128,256]{1,0:T(8,128)(2,1)S(1)} %collective-permute-done.5.refs_1_, bf16[128,256]{1,0:T(8,128)(2,1)S(1)} %collective-permute-done.6.refs_2_, ...), custom_call_target="tpu_custom_call" | custom-call | flops 1000 | bytes 1000 | tf_op jit(solution)/shard_map/cache_part/pallas_call | solution.py:516
  (1 shorter events, 0.0 us)
Async XLA Ops:
  0.6 19.9 %collective-permute-start.2 = (bf16[512,256]{1,0:T(8,128)(2,1)}, bf16[512,256]{1,0:T(8,128)(2,1)S(1)}, u32[]{:S(2)}, u32[]{:S(2)}) collective-permute-start(bf16[512,256]{1,0:T(8,128)(2,1)} %bitcast.8), channel_id=1, source_target_pairs={{0,4},{1,5},{2,6},{3,7},{4,0},{5,1},{6,2},{7,3},{8,12},{9,13},{10,... | collective-permute-start | bytes 786440 | tf_op jit(solution)/shard_map/ppermute | solution.py:34
  4.7 9.7 %collective-permute-start = (s32[1]{0:T(128)}, s32[1]{0:T(128)}, u32[]{:S(2)}, u32[]{:S(2)}) collective-permute-start(s32[1]{0:T(128)} %param.13), channel_id=1, source_target_pairs={{0,8},{8,0},{16,24},{24,16},{1,9},{9,1},{17,25},{25,17},{2,10},{10... | collective-permute-start | bytes 20 | tf_op jit(solution)/shard_map/ppermute | solution.py:39
  6.9 17.9 %collective-permute-start.3 = (bf16[256,256]{1,0:T(8,128)(2,1)S(1)}, bf16[256,256]{1,0:T(8,128)(2,1)S(1)}, u32[]{:S(2)}, u32[]{:S(2)}) collective-permute-start(bf16[256,256]{1,0:T(8,128)(2,1)S(1)} %get-tuple-element.44), channel_id=1, source_target_pairs={{0,4},{1,5},{2,6},{3,7},{4,0},{5,1},{6,2},{7,3},{8,12},{9,13},{10,... | collective-permute-start | bytes 393224 | tf_op jit(solution)/shard_map/ppermute | solution.py:34
  7.0 17.7 %collective-permute-start.5 = (bf16[128,256]{1,0:T(8,128)(2,1)S(1)}, bf16[128,256]{1,0:T(8,128)(2,1)S(1)}, u32[]{:S(2)}, u32[]{:S(2)}) collective-permute-start(bf16[128,256]{1,0:T(8,128)(2,1)S(1)} %get-tuple-element.49), channel_id=1, source_target_pairs={{0,2},{1,3},{2,0},{3,1},{4,6},{5,7},{6,4},{7,5},{8,10},{9,11},{10,... | collective-permute-start | bytes 196616 | tf_op jit(solution)/shard_map/ppermute | solution.py:39
  8.9 15.9 %collective-permute-start.6 = (bf16[128,256]{1,0:T(8,128)(2,1)S(1)}, bf16[128,256]{1,0:T(8,128)(2,1)S(1)}, u32[]{:S(2)}, u32[]{:S(2)}) collective-permute-start(bf16[128,256]{1,0:T(8,128)(2,1)S(1)} %get-tuple-element.50), channel_id=1, source_target_pairs={{0,3},{1,2},{2,1},{3,0},{4,7},{5,6},{6,5},{7,4},{8,11},{9,10},{10,... | collective-permute-start | bytes 196616 | tf_op jit(solution)/shard_map/ppermute | solution.py:39
  14.4 10.4 %collective-permute-start.7 = (bf16[128,256]{1,0:T(8,128)(2,1)S(1)}, bf16[128,256]{1,0:T(8,128)(2,1)S(1)}, u32[]{:S(2)}, u32[]{:S(2)}) collective-permute-start(bf16[128,256]{1,0:T(8,128)(2,1)S(1)} %get-tuple-element.51), channel_id=1, source_target_pairs={{0,1},{1,0},{2,3},{3,2},{4,5},{5,4},{6,7},{7,6},{8,9},{9,8},{10,11... | collective-permute-start | bytes 196616 | tf_op jit(solution)/shard_map/ppermute | solution.py:39
  20.5 3.6 %collective-permute-start.1 = (s32[2]{0:T(128)S(1)}, s32[2]{0:T(128)S(1)}, u32[]{:S(2)}, u32[]{:S(2)}) collective-permute-start(s32[2]{0:T(128)S(1)} %pair_up.1.here_ref), channel_id=1, source_target_pairs={{0,16},{8,24},{16,0},{24,8},{1,17},{9,25},{17,1},{25,9},{2,18},{10... | collective-permute-start | bytes 32 | tf_op jit(solution)/shard_map/ppermute | solution.py:39
  24.1 7.3 %collective-permute-start.4 = (bf16[256,256]{1,0:T(8,128)(2,1)S(1)}, bf16[256,256]{1,0:T(8,128)(2,1)S(1)}, u32[]{:S(2)}, u32[]{:S(2)}) collective-permute-start(bf16[256,256]{1,0:T(8,128)(2,1)S(1)} %get-tuple-element.45), channel_id=1, source_target_pairs={{0,4},{1,5},{2,6},{3,7},{4,0},{5,1},{6,2},{7,3},{8,12},{9,13},{10,... | collective-permute-start | bytes 393224 | tf_op jit(solution)/shard_map/ppermute | solution.py:34
  24.8 8.4 %collective-permute-start.8 = (bf16[128,256]{1,0:T(8,128)(2,1)S(1)}, bf16[128,256]{1,0:T(8,128)(2,1)S(1)}, u32[]{:S(2)}, u32[]{:S(2)}) collective-permute-start(bf16[128,256]{1,0:T(8,128)(2,1)S(1)} %get-tuple-element.54), channel_id=1, source_target_pairs={{0,2},{1,3},{2,0},{3,1},{4,6},{5,7},{6,4},{7,5},{8,10},{9,11},{10,... | collective-permute-start | bytes 196616 | tf_op jit(solution)/shard_map/ppermute | solution.py:39
  28.2 5.6 %collective-permute-start.9 = (bf16[128,256]{1,0:T(8,128)(2,1)S(1)}, bf16[128,256]{1,0:T(8,128)(2,1)S(1)}, u32[]{:S(2)}, u32[]{:S(2)}) collective-permute-start(bf16[128,256]{1,0:T(8,128)(2,1)S(1)} %get-tuple-element.55), channel_id=1, source_target_pairs={{0,3},{1,2},{2,1},{3,0},{4,7},{5,6},{6,5},{7,4},{8,11},{9,10},{10,... | collective-permute-start | bytes 196616 | tf_op jit(solution)/shard_map/ppermute | solution.py:39
  29.2 5.0 %collective-permute-start.10 = (bf16[128,256]{1,0:T(8,128)(2,1)S(1)}, bf16[128,256]{1,0:T(8,128)(2,1)S(1)}, u32[]{:S(2)}, u32[]{:S(2)}) collective-permute-start(bf16[128,256]{1,0:T(8,128)(2,1)S(1)} %get-tuple-element.56), channel_id=1, source_target_pairs={{0,1},{1,0},{2,3},{3,2},{4,5},{5,4},{6,7},{7,6},{8,9},{9,8},{10,11... | collective-permute-start | bytes 196616 | tf_op jit(solution)/shard_map/ppermute | solution.py:39

commit v9 on v8

--- a/solution.py
+++ b/solution.py
@@ -380,13 +380,13 @@
     return outs[:others], outs[others]
 
 
-def weigh(facts_row, facts_of, query_rot, key_rot, payload):
+def weigh(facts_row, facts_of, query_rot, key_rot, payload, after):
     others = len(key_rot)
     rows = query_rot.shape[0]
     block_len = rows // 2
     slots = facts_of(None).slots
 
-    def body(facts_ref, q_ref, *refs):
+    def body(facts_ref, _, q_ref, *refs):
         k_refs, pay_refs, refs = refs[:others], refs[others : 2 * others], refs[2 * others :]
         w_refs, out_refs = refs[:others], refs[others:]
         for pay_ref, out_ref in zip(pay_refs, out_refs):
@@ -406,8 +406,8 @@
         jax.ShapeDtypeStruct((2, Q_DEV, block_len, block_len), bf16) for _ in range(others)
     ]
     shapes += [jax.ShapeDtypeStruct(x.shape, bf16) for x in payload]
-    outs = call(body, shapes, [SMEM] + [VMEM] * (1 + 2 * others), "weigh")(
-        facts_row, query_rot, *key_rot, *payload
+    outs = call(body, shapes, [SMEM] + [VMEM] * (2 + 2 * others), "weigh")(
+        facts_row, after, query_rot, *key_rot, *payload
     )
     return outs[:others], outs[others:]
 
@@ -547,9 +547,9 @@
     query_rot, acc, angles = own_part(facts_row, facts_of, q, operands, tables)
     kept, live = masks_of(facts_row, facts_of, q.shape[0], lens)
     key_rot, chosen = receive_keys(key_in, select, order, angles)
-    weights, tails = weigh(facts_row, facts_of, query_rot, key_rot, sent[1::2])
+    weights, tails = weigh(facts_row, facts_of, query_rot, key_rot, sent[1::2], live)
     tails = to_slots(tails)
-    late = hand_on(late_pieces(heads, chosen, early[1:] + [live]))
+    late = hand_on(late_pieces(heads, chosen, early[1:]))
     attended, mark = attend(facts_row, facts_of, weights, acc, heads, tails, live)
     cache = cache_part(early, late, kept, mark)
     return (attended[None, None], cache[None])

time: 35.5 us -> 33.8 us (0.952)
  waiting for transfers between devices: 7.22 us -> 4.76 us
  starting transfers between devices: 14.6 us -> 15.3 us
    ppermute x3, waiting for transfers between devices: 6.21 us -> 2.33 us  [shifted(): lax.ppermute(shard, axis, [(i, (i + by) % peers) for i in range(peers)])]
    ppermute x3, starting transfers between devices: 4.34 us -> 6.73 us  [shifted(): lax.ppermute(shard, axis, [(i, (i + by) % peers) for i in range(peers)])]
    ppermute x8, starting transfers between devices: 10.3 us -> 8.61 us  [crossed(): return lax.ppermute(shard, axis, [(i, i ^ by) for i in range(peers)])]
    ppermute x8, waiting for transfers between devices: 1.01 us -> 2.43 us  [crossed(): return lax.ppermute(shard, axis, [(i, i ^ by) for i in range(peers)])]
  transfers between devices with their start and end apart: 11 -> 11, of which waited for: 4 -> 4; matrix products, arithmetic and copies ran while one was open for 0% -> 0% of each run, Pallas kernels for 31% -> 33%
where the time goes in v9:
time: 33.8 us; the launch traced here: 33.6 us
  starting transfers between devices  15.3 us (45%)
  Pallas kernels  12.1 us (36%)
  waiting for transfers between devices  4.76 us (14%)
  between operations  1.36 us (4%)
    ppermute x8, starting transfers between devices, crossed(): return lax.ppermute(shard, axis, [(i, i ^ by) for i in range(peers)])  8.61 us
    ppermute x3, starting transfers between devices, shifted(): lax.ppermute(shard, axis, [(i, (i + by) % peers) for i in range(peers)])  6.73 us
    pallas_call x1, Pallas kernels, own_part(): call(body, shapes, specs, 'own_part', scratch)  3.47 us
    ppermute x8, waiting for transfers between devices, crossed(): return lax.ppermute(shard, axis, [(i, i ^ by) for i in range(peers)])  2.43 us
    ppermute x3, waiting for transfers between devices, shifted(): lax.ppermute(shard, axis, [(i, (i + by) % peers) for i in range(peers)])  2.33 us
    pallas_call x1, Pallas kernels, prepare(): call(body, shapes, [HBM] * count, 'prepare', scratch, out_specs=[SMEM] +...  2.13 us
    pallas_call x1, Pallas kernels, attend(): call(body, shape, specs, 'attend', scratch)  1.9 us
    pallas_call x1, Pallas kernels, weigh(): call(body, shapes, [SMEM] + [VMEM] * (2 + 2 * others), 'weigh')  1.28 us
  transfers between devices with their start and end apart: 11, of which 4 were waited for; matrix products, arithmetic and copies ran while one was open for 0% of the time, Pallas kernels for 33%

profile of v9, /device:TPU:0, one launch (start us, length us, event | category | flops | bytes accessed | tf_op | source)
XLA Modules:
  0.0 33.6 jit_solution(13913222221127657886)
XLA Ops:
  0.6 4.1 %collective-permute-start.2 = (bf16[512,256]{1,0:T(8,128)(2,1)}, bf16[512,256]{1,0:T(8,128)(2,1)S(1)}, u32[]{:S(2)}, u32[]{:S(2)}) collective-permute-start(bf16[512,256]{1,0:T(8,128)(2,1)} %bitcast.8), channel_id=1, source_target_pairs={{0,4},{1,5},{2,6},{3,7},{4,0},{5,1},{6,2},{7,3},{8,12},{9,13},{10,... | collective-permute-start | bytes 786440 | tf_op jit(solution)/shard_map/ppermute | solution.py:34
  4.7 0.0 collective-permute-start
  4.7 2.1 %prepare.1 = (s32[1,16]{1,0:T(1,128)S(1)}, bf16[512,256]{1,0:T(8,128)(2,1)S(1)}, bf16[512,256]{1,0:T(8,128)(2,1)S(1)}, f32[2,256,128]{2,1,0:T(8,128)S(1)}, f32[2...) custom-call(bf16[512,256]{1,0:T(8,128)(2,1)} %bitcast.9, ...), custom_call_target="tpu_custom_call" | custom-call | flops 1000 | bytes 1000 | tf_op jit(solution)/shard_map/prepare/pallas_call | solution.py:229
  6.9 0.2 collective-permute-start.3
  7.0 1.8 %collective-permute-start.5 = (bf16[128,256]{1,0:T(8,128)(2,1)S(1)}, bf16[128,256]{1,0:T(8,128)(2,1)S(1)}, u32[]{:S(2)}, u32[]{:S(2)}) collective-permute-start(bf16[128,256]{1,0:T(8,128)(2,1)S(1)} %get-tuple-element.49), channel_id=1, source_target_pairs={{0,2},{1,3},{2,0},{3,1},{4,6},{5,7},{6,4},{7,5},{8,10},{9,11},{10,... | collective-permute-start | bytes 196616 | tf_op jit(solution)/shard_map/ppermute | solution.py:39
  8.9 1.4 %collective-permute-start.6 = (bf16[128,256]{1,0:T(8,128)(2,1)S(1)}, bf16[128,256]{1,0:T(8,128)(2,1)S(1)}, u32[]{:S(2)}, u32[]{:S(2)}) collective-permute-start(bf16[128,256]{1,0:T(8,128)(2,1)S(1)} %get-tuple-element.50), channel_id=1, source_target_pairs={{0,3},{1,2},{2,1},{3,0},{4,7},{5,6},{6,5},{7,4},{8,11},{9,10},{10,... | collective-permute-start | bytes 196616 | tf_op jit(solution)/shard_map/ppermute | solution.py:39
  10.3 3.5 %own_part.1 = (bf16[512,512]{1,0:T(8,128)(2,1)S(1)}, f32[512,1024]{1,0:T(8,128)S(1)}, f32[1,2,2,256,128]{4,3,2,1,0:T(8,128)S(1)}) custom-call(s32[1,16]{1,0:T(1,128)S(1)} %get-tuple-element.30.facts_ref, bf16[512,512]{1,0:T(8,128)(2,1)} %bitcast.5, bf16[512,256]{1,0:T(8,128)(2,1)S(1)} %get-tuple-element.31.kr_ref, ...), custom_call_target="tpu_custom_call" | custom-call | flops 1000 | bytes 1000 | tf_op jit(solution)/shard_map/own_part/pallas_call | solution.py:298
  14.4 0.0 collective-permute-done.near_ref
  14.4 1.2 %pair_up.1.here_ref = s32[2]{0:T(128)S(1)} custom-call(s32[1]{0:T(128)S(6)} %copy.11.own_ref, s32[1]{0:T(128)} %collective-permute-done.near_ref), custom_call_target="tpu_custom_call" | custom-call | flops 1000 | bytes 1000 | tf_op jit(solution)/shard_map/pair_up/pallas_call | solution.py:247
  15.6 1.6 %collective-permute-start.1 = (s32[2]{0:T(128)S(1)}, s32[2]{0:T(128)S(1)}, u32[]{:S(2)}, u32[]{:S(2)}) collective-permute-start(s32[2]{0:T(128)S(1)} %pair_up.1.here_ref), channel_id=1, source_target_pairs={{0,16},{8,24},{16,0},{24,8},{1,17},{9,25},{17,1},{25,9},{2,18},{10... | collective-permute-start | bytes 32 | tf_op jit(solution)/shard_map/ppermute | solution.py:39
  17.1 2.0 %collective-permute-done.1.there_ref = s32[2]{0:T(128)S(1)} collective-permute-done((s32[2]{0:T(128)S(1)}, s32[2]{0:T(128)S(1)}, u32[]{:S(2)}, u32[]{:S(2)}) %collective-permute-start.1) | collective-permute-done | bytes 40 | tf_op jit(solution)/shard_map/ppermute | solution.py:39
  19.2 0.3 collective-permute-start.7
  19.4 0.6 %masks.1 = (bf16[128,128]{1,0:T(8,128)(2,1)S(1)}, f32[512,128]{1,0:T(8,128)S(1)}) custom-call(s32[1,16]{1,0:T(1,128)S(1)} %get-tuple-element.30.facts_ref, s32[2]{0:T(128)S(1)} %pair_up.1.here_ref, s32[2]{0:T(128)S(1)} %collective-permute-done.1.there_ref), custom_call_target="tpu_custom_call" | custom-call | flops 1000 | bytes 1000 | tf_op jit(solution)/shard_map/masks/pallas_call | solution.py:343
  20.1 0.4 %collective-permute-done.2.refs_0_ = bf16[512,256]{1,0:T(8,128)(2,1)S(1)} collective-permute-done((bf16[512,256]{1,0:T(8,128)(2,1)}, bf16[512,256]{1,0:T(8,128)(2,1)S(1)}, u32[]{:S(2)}, u32[]{:S(2)}) %collective-permute-start.2) | collective-permute-done | bytes 262176 | tf_op jit(solution)/shard_map/ppermute | solution.py:34
  20.5 0.4 %receive_keys.1 = (bf16[512,256]{1,0:T(8,128)(2,1)S(1)}, bf16[1,256,256]{2,1,0:T(8,128)(2,1)S(1)}) custom-call(bf16[256,512]{1,0:T(8,128)(2,1)S(1)} %get-tuple-element.38.select_ref, bf16[256,256]{1,0:T(8,128)(2,1)S(1)} %get-tuple-element.39.order_ref, f32[1,2,2,256,128]{4,3,2,1,0:T(8,128)S(1)} %get-tuple-element.40.angle_ref, ...), custom_call_target="tpu_custom_call" | custom-call | flops 10000000000 | bytes 1000 | tf_op jit(solution)/shard_map/receive_keys/pallas_call | solution.py:377
  20.9 1.3 %weigh.1 = (bf16[2,4,256,256]{3,2,1,0:T(8,128)(2,1)S(1)}, bf16[256,256]{1,0:T(8,128)(2,1)S(1)}) custom-call(s32[1,16]{1,0:T(1,128)S(1)} %get-tuple-element.30.facts_ref, f32[512,128]{1,0:T(8,128)S(1)} %get-tuple-element.36._.live_ref, bf16[512,512]{1,0:T(8,128)(2,1)S(1)} %get-tuple-element.37.q_ref, bf16[512,256]{1,0:T(8,128)(2,1)S(1)} %get-tuple-element.41.refs_0_, ...), custom_call_target="tpu_custom_call" | custom-call | flops 1000 | bytes 1000 | tf_op jit(solution)/shard_map/weigh/pallas_call | solution.py:409
  22.2 2.5 %collective-permute-start.4 = (bf16[256,256]{1,0:T(8,128)(2,1)S(1)}, bf16[256,256]{1,0:T(8,128)(2,1)S(1)}, u32[]{:S(2)}, u32[]{:S(2)}) collective-permute-start(bf16[256,256]{1,0:T(8,128)(2,1)S(1)} %get-tuple-element.45), channel_id=1, source_target_pairs={{0,4},{1,5},{2,6},{3,7},{4,0},{5,1},{6,2},{7,3},{8,12},{9,13},{10,... | collective-permute-start | bytes 393224 | tf_op jit(solution)/shard_map/ppermute | solution.py:34
  24.7 0.0 collective-permute-done.5.refs_1_
  24.7 0.0 collective-permute-done.6.refs_2_
  24.7 0.0 collective-permute-done.7.refs_3_
  24.7 0.0 collective-permute-done.3.refs_1_.refs_0_
  24.7 1.6 %collective-permute-start.8 = (bf16[128,256]{1,0:T(8,128)(2,1)S(1)}, bf16[128,256]{1,0:T(8,128)(2,1)S(1)}, u32[]{:S(2)}, u32[]{:S(2)}) collective-permute-start(bf16[128,256]{1,0:T(8,128)(2,1)S(1)} %get-tuple-element.54), channel_id=1, source_target_pairs={{0,2},{1,3},{2,0},{3,1},{4,6},{5,7},{6,4},{7,5},{8,10},{9,11},{10,... | collective-permute-start | bytes 196616 | tf_op jit(solution)/shard_map/ppermute | solution.py:39
  26.4 1.4 %collective-permute-start.9 = (bf16[128,256]{1,0:T(8,128)(2,1)S(1)}, bf16[128,256]{1,0:T(8,128)(2,1)S(1)}, u32[]{:S(2)}, u32[]{:S(2)}) collective-permute-start(bf16[128,256]{1,0:T(8,128)(2,1)S(1)} %get-tuple-element.55), channel_id=1, source_target_pairs={{0,3},{1,2},{2,1},{3,0},{4,7},{5,6},{6,5},{7,4},{8,11},{9,10},{10,... | collective-permute-start | bytes 196616 | tf_op jit(solution)/shard_map/ppermute | solution.py:39
  27.8 0.5 %collective-permute-start.10 = (bf16[128,256]{1,0:T(8,128)(2,1)S(1)}, bf16[128,256]{1,0:T(8,128)(2,1)S(1)}, u32[]{:S(2)}, u32[]{:S(2)}) collective-permute-start(bf16[128,256]{1,0:T(8,128)(2,1)S(1)} %get-tuple-element.56), channel_id=1, source_target_pairs={{0,1},{1,0},{2,3},{3,2},{4,5},{5,4},{6,7},{7,6},{8,9},{9,8},{10,11... | collective-permute-start | bytes 196616 | tf_op jit(solution)/shard_map/ppermute | solution.py:39
  28.3 1.9 %collective-permute-done.4.refs_2_ = bf16[256,256]{1,0:T(8,128)(2,1)S(1)} collective-permute-done((bf16[256,256]{1,0:T(8,128)(2,1)S(1)}, bf16[256,256]{1,0:T(8,128)(2,1)S(1)}, u32[]{:S(2)}, u32[]{:S(2)}) %collective-permute-start.4) | collective-permute-done | bytes 131104 | tf_op jit(solution)/shard_map/ppermute | solution.py:34
  30.2 1.9 %attend.1 = (bf16[512,512]{1,0:T(8,128)(2,1)}, f32[8,128]{1,0:T(8,128)S(1)}) custom-call(s32[1,16]{1,0:T(1,128)S(1)} %get-tuple-element.30.facts_ref, f32[512,1024]{1,0:T(8,128)S(1)} %get-tuple-element.35.acc_ref, f32[512,128]{1,0:T(8,128)S(1)} %get-tuple-element.36._.live_ref, bf16[2,4,256,256]{3,2,1,0:T(8,128)(2,1)S(1)} %get-tuple-element.43.refs_0_, ...), custom_call_target="tpu_custom_call" | custom-call | flops 1000 | bytes 1000 | tf_op jit(solution)/shard_map/attend/pallas_call | solution.py:491
  32.1 0.0 collective-permute-done.8.refs_5_
  32.1 0.0 collective-permute-done.9.refs_6_
  32.1 0.4 %collective-permute-done.10.refs_7_ = bf16[128,256]{1,0:T(8,128)(2,1)S(1)} collective-permute-done((bf16[128,256]{1,0:T(8,128)(2,1)S(1)}, bf16[128,256]{1,0:T(8,128)(2,1)S(1)}, u32[]{:S(2)}, u32[]{:S(2)}) %collective-permute-start.10) | collective-permute-done | bytes 65568 | tf_op jit(solution)/shard_map/ppermute | solution.py:39
  32.5 1.1 %cache_part.1 = bf16[128,2048]{1,0:T(8,128)(2,1)} custom-call(bf16[128,128]{1,0:T(8,128)(2,1)S(1)} %get-tuple-element.47.kept_ref, bf16[128,256]{1,0:T(8,128)(2,1)S(1)} %get-tuple-element.48.refs_0_, bf16[128,256]{1,0:T(8,128)(2,1)S(1)} %collective-permute-done.5.refs_1_, bf16[128,256]{1,0:T(8,128)(2,1)S(1)} %collective-permute-done.6.refs_2_, ...), custom_call_target="tpu_custom_call" | custom-call | flops 1000 | bytes 1000 | tf_op jit(solution)/shard_map/cache_part/pallas_call | solution.py:516
  (1 shorter events, 0.0 us)
Async XLA Ops:
  0.6 19.9 %collective-permute-start.2 = (bf16[512,256]{1,0:T(8,128)(2,1)}, bf16[512,256]{1,0:T(8,128)(2,1)S(1)}, u32[]{:S(2)}, u32[]{:S(2)}) collective-permute-start(bf16[512,256]{1,0:T(8,128)(2,1)} %bitcast.8), channel_id=1, source_target_pairs={{0,4},{1,5},{2,6},{3,7},{4,0},{5,1},{6,2},{7,3},{8,12},{9,13},{10,... | collective-permute-start | bytes 786440 | tf_op jit(solution)/shard_map/ppermute | solution.py:34
  4.7 9.7 %collective-permute-start = (s32[1]{0:T(128)}, s32[1]{0:T(128)}, u32[]{:S(2)}, u32[]{:S(2)}) collective-permute-start(s32[1]{0:T(128)} %param.13), channel_id=1, source_target_pairs={{0,8},{8,0},{16,24},{24,16},{1,9},{9,1},{17,25},{25,17},{2,10},{10... | collective-permute-start | bytes 20 | tf_op jit(solution)/shard_map/ppermute | solution.py:39
  6.9 17.8 %collective-permute-start.3 = (bf16[256,256]{1,0:T(8,128)(2,1)S(1)}, bf16[256,256]{1,0:T(8,128)(2,1)S(1)}, u32[]{:S(2)}, u32[]{:S(2)}) collective-permute-start(bf16[256,256]{1,0:T(8,128)(2,1)S(1)} %get-tuple-element.44), channel_id=1, source_target_pairs={{0,4},{1,5},{2,6},{3,7},{4,0},{5,1},{6,2},{7,3},{8,12},{9,13},{10,... | collective-permute-start | bytes 393224 | tf_op jit(solution)/shard_map/ppermute | solution.py:34
  7.0 17.6 %collective-permute-start.5 = (bf16[128,256]{1,0:T(8,128)(2,1)S(1)}, bf16[128,256]{1,0:T(8,128)(2,1)S(1)}, u32[]{:S(2)}, u32[]{:S(2)}) collective-permute-start(bf16[128,256]{1,0:T(8,128)(2,1)S(1)} %get-tuple-element.49), channel_id=1, source_target_pairs={{0,2},{1,3},{2,0},{3,1},{4,6},{5,7},{6,4},{7,5},{8,10},{9,11},{10,... | collective-permute-start | bytes 196616 | tf_op jit(solution)/shard_map/ppermute | solution.py:39
  8.9 15.8 %collective-permute-start.6 = (bf16[128,256]{1,0:T(8,128)(2,1)S(1)}, bf16[128,256]{1,0:T(8,128)(2,1)S(1)}, u32[]{:S(2)}, u32[]{:S(2)}) collective-permute-start(bf16[128,256]{1,0:T(8,128)(2,1)S(1)} %get-tuple-element.50), channel_id=1, source_target_pairs={{0,3},{1,2},{2,1},{3,0},{4,7},{5,6},{6,5},{7,4},{8,11},{9,10},{10,... | collective-permute-start | bytes 196616 | tf_op jit(solution)/shard_map/ppermute | solution.py:39
  15.6 3.6 %collective-permute-start.1 = (s32[2]{0:T(128)S(1)}, s32[2]{0:T(128)S(1)}, u32[]{:S(2)}, u32[]{:S(2)}) collective-permute-start(s32[2]{0:T(128)S(1)} %pair_up.1.here_ref), channel_id=1, source_target_pairs={{0,16},{8,24},{16,0},{24,8},{1,17},{9,25},{17,1},{25,9},{2,18},{10... | collective-permute-start | bytes 32 | tf_op jit(solution)/shard_map/ppermute | solution.py:39
  19.2 5.5 %collective-permute-start.7 = (bf16[128,256]{1,0:T(8,128)(2,1)S(1)}, bf16[128,256]{1,0:T(8,128)(2,1)S(1)}, u32[]{:S(2)}, u32[]{:S(2)}) collective-permute-start(bf16[128,256]{1,0:T(8,128)(2,1)S(1)} %get-tuple-element.51), channel_id=1, source_target_pairs={{0,1},{1,0},{2,3},{3,2},{4,5},{5,4},{6,7},{7,6},{8,9},{9,8},{10,11... | collective-permute-start | bytes 196616 | tf_op jit(solution)/shard_map/ppermute | solution.py:39
  22.2 8.0 %collective-permute-start.4 = (bf16[256,256]{1,0:T(8,128)(2,1)S(1)}, bf16[256,256]{1,0:T(8,128)(2,1)S(1)}, u32[]{:S(2)}, u32[]{:S(2)}) collective-permute-start(bf16[256,256]{1,0:T(8,128)(2,1)S(1)} %get-tuple-element.45), channel_id=1, source_target_pairs={{0,4},{1,5},{2,6},{3,7},{4,0},{5,1},{6,2},{7,3},{8,12},{9,13},{10,... | collective-permute-start | bytes 393224 | tf_op jit(solution)/shard_map/ppermute | solution.py:34
  24.7 7.4 %collective-permute-start.8 = (bf16[128,256]{1,0:T(8,128)(2,1)S(1)}, bf16[128,256]{1,0:T(8,128)(2,1)S(1)}, u32[]{:S(2)}, u32[]{:S(2)}) collective-permute-start(bf16[128,256]{1,0:T(8,128)(2,1)S(1)} %get-tuple-element.54), channel_id=1, source_target_pairs={{0,2},{1,3},{2,0},{3,1},{4,6},{5,7},{6,4},{7,5},{8,10},{9,11},{10,... | collective-permute-start | bytes 196616 | tf_op jit(solution)/shard_map/ppermute | solution.py:39
  26.4 5.7 %collective-permute-start.9 = (bf16[128,256]{1,0:T(8,128)(2,1)S(1)}, bf16[128,256]{1,0:T(8,128)(2,1)S(1)}, u32[]{:S(2)}, u32[]{:S(2)}) collective-permute-start(bf16[128,256]{1,0:T(8,128)(2,1)S(1)} %get-tuple-element.55), channel_id=1, source_target_pairs={{0,3},{1,2},{2,1},{3,0},{4,7},{5,6},{6,5},{7,4},{8,11},{9,10},{10,... | collective-permute-start | bytes 196616 | tf_op jit(solution)/shard_map/ppermute | solution.py:39
  27.8 4.7 %collective-permute-start.10 = (bf16[128,256]{1,0:T(8,128)(2,1)S(1)}, bf16[128,256]{1,0:T(8,128)(2,1)S(1)}, u32[]{:S(2)}, u32[]{:S(2)}) collective-permute-start(bf16[128,256]{1,0:T(8,128)(2,1)S(1)} %get-tuple-element.56), channel_id=1, source_target_pairs={{0,1},{1,0},{2,3},{3,2},{4,5},{5,4},{6,7},{7,6},{8,9},{9,8},{10,11... | collective-permute-start | bytes 196616 | tf_op jit(solution)/shard_map/ppermute | solution.py:39

commit v10 on v9

--- a/solution.py
+++ b/solution.py
@@ -237,16 +237,6 @@
     return outs[0], facts_of, outs[1:3], outs[3:5], outs[5:7], outs[7:11], outs[11:]
 
 
-def pair_up(own_length, near_length):
-    def body(own_ref, near_ref, pair_ref):
-        odd = lax.axis_index("req") % 2 == 1
-        pair_ref[0] = jnp.where(odd, near_ref[0], own_ref[0])
-        pair_ref[1] = jnp.where(odd, own_ref[0], near_ref[0])
-
-    shape = jax.ShapeDtypeStruct((2,), jnp.int32)
-    return call(body, shape, [SMEM] * 2, "pair_up", out_specs=SMEM)(own_length, near_length)
-
-
 def own_part(facts_row, facts_of, queries, operands, tables):
     rows = queries.shape[0]
     block_len = rows // 2
@@ -307,7 +297,8 @@
     run = block_len // residues
     cache_rows = 2 * slots * run
 
-    def body(facts_ref, here_ref, there_ref, kept_ref, live_ref):
+    def body(facts_ref, *refs):
+        len_refs, kept_ref, live_ref = refs[:groups], refs[groups], refs[groups + 1]
         facts = facts_of(facts_ref)
         slot = slot_and_head_group()[0]
         group = lax.axis_index("req")
@@ -319,12 +310,9 @@
                 block = facts.block((slot - turn + slots) % slots, half)
                 target = jnp.where(part == 2 * turn + half, block * run + offset, target)
         length = 0
-        half_count = groups // 2
-        for index in range(half_count):
-            same = (group & half_count) | index
-            length = length + jnp.where(facts.owner(same) == group, here_ref[index], 0)
-            other = same ^ half_count
-            length = length + jnp.where(facts.owner(other) == group, there_ref[index], 0)
+        for turn in range(groups):
+            mine = facts.owner(lax.rem(group - turn + groups, groups)) == group
+            length = length + jnp.where(mine, len_refs[turn][0], 0)
         residue = 0
         for r in range(1, residues):
             residue = jnp.where(facts.rank(r) == lax.axis_index("blk"), r, residue)
@@ -340,7 +328,7 @@
         jax.ShapeDtypeStruct((cache_rows, cache_rows), bf16),
         jax.ShapeDtypeStruct((rows, HEAD_SIZE), f32),
     ]
-    return call(body, shapes, [SMEM] * 3, "masks")(facts_row, *lens)
+    return call(body, shapes, [SMEM] * (1 + groups), "masks")(facts_row, *lens)
 
 
 def tiles_of(facts, slot, source):
@@ -534,16 +522,8 @@
     )
     heads = to_slots(sent[0::2])
     early = hand_on(early)
-    block = pair_up(lengths, crossed(lengths, "req", 1))
-    span, groups = 2, lax.axis_size("req")
-    while 2 * span < groups:
-        other = crossed(block, "req", span)
-        upper = (lax.axis_index("req") & span) > 0
-        block = jnp.where(
-            upper, jnp.concatenate([other, block]), jnp.concatenate([block, other])
-        )
-        span = 2 * span
-    lens = (block, crossed(block, "req", span))
+    groups = lax.axis_size("req")
+    lens = [lengths] + [shifted(lengths, "req", t) for t in range(1, groups)]
     query_rot, acc, angles = own_part(facts_row, facts_of, q, operands, tables)
     kept, live = masks_of(facts_row, facts_of, q.shape[0], lens)
     key_rot, chosen = receive_keys(key_in, select, order, angles)

time: 33.8 us -> 34.6 us (1.024)
  starting transfers between devices: 15.3 us -> 17.1 us
  waiting for transfers between devices: 4.76 us -> 3.02 us
  Pallas kernels: 12.1 us -> 12.9 us
    ppermute x3 -> x6, starting transfers between devices: 6.73 us -> 10 us  [shifted(): lax.ppermute(shard, axis, [(i, (i + by) % peers) for i in range(peers)])]
    ppermute x3 -> x6, waiting for transfers between devices: 2.33 us -> 0.11 us  [shifted(): lax.ppermute(shard, axis, [(i, (i + by) % peers) for i in range(peers)])]
    ppermute x8 -> x6, starting transfers between devices: 8.61 us -> 7.1 us  [crossed(): return lax.ppermute(shard, axis, [(i, i ^ by) for i in range(peers)])]
    pallas_call x2 -> x1, Pallas kernels: 1.77 us -> 2.54 us  [masks_of(): return call(body, shapes, [SMEM] * (1 + groups), 'masks')(facts_row, *lens)]
    ppermute x8 -> x6, waiting for transfers between devices: 2.43 us -> 2.91 us  [crossed(): return lax.ppermute(shard, axis, [(i, i ^ by) for i in range(peers)])]
  transfers between devices with their start and end apart: 11 -> 12, of which waited for: 4 -> 3; matrix products, arithmetic and copies ran while one was open for 0% -> 0% of each run, Pallas kernels for 33% -> 34%
where the time goes in v10:
time: 34.6 us; the launch traced here: 34.4 us
  starting transfers between devices  17.1 us (49%)
  Pallas kernels  12.9 us (37%)
  waiting for transfers between devices  3.02 us (9%)
  between operations  1.35 us (4%)
    ppermute x6, starting transfers between devices, shifted(): lax.ppermute(shard, axis, [(i, (i + by) % peers) for i in range(peers)])  10 us
    ppermute x6, starting transfers between devices, crossed(): return lax.ppermute(shard, axis, [(i, i ^ by) for i in range(peers)])  7.1 us
    pallas_call x1, Pallas kernels, own_part(): call(body, shapes, specs, 'own_part', scratch)  3.47 us
    ppermute x6, waiting for transfers between devices, crossed(): return lax.ppermute(shard, axis, [(i, i ^ by) for i in range(peers)])  2.91 us
    pallas_call x1, Pallas kernels, masks_of(): return call(body, shapes, [SMEM] * (1 + groups), 'masks')(facts_row, *lens)  2.54 us
    pallas_call x1, Pallas kernels, prepare(): call(body, shapes, [HBM] * count, 'prepare', scratch, out_specs=[SMEM] +...  2.13 us
    pallas_call x1, Pallas kernels, attend(): call(body, shape, specs, 'attend', scratch)  1.9 us
    pallas_call x1, Pallas kernels, weigh(): call(body, shapes, [SMEM] + [VMEM] * (2 + 2 * others), 'weigh')  1.29 us
  transfers between devices with their start and end apart: 12, of which 3 were waited for; matrix products, arithmetic and copies ran while one was open for 0% of the time, Pallas kernels for 34%

profile of v10, /device:TPU:0, one launch (start us, length us, event | category | flops | bytes accessed | tf_op | source)
XLA Modules:
  0.0 34.4 jit_solution(9307432607159331153)
XLA Ops:
  0.6 4.1 %collective-permute-start.3 = (bf16[512,256]{1,0:T(8,128)(2,1)}, bf16[512,256]{1,0:T(8,128)(2,1)S(1)}, u32[]{:S(2)}, u32[]{:S(2)}) collective-permute-start(bf16[512,256]{1,0:T(8,128)(2,1)} %bitcast.8), channel_id=1, source_target_pairs={{0,4},{1,5},{2,6},{3,7},{4,0},{5,1},{6,2},{7,3},{8,12},{9,13},{10,... | collective-permute-start | bytes 786440 | tf_op jit(solution)/shard_map/ppermute | solution.py:34
  4.7 0.0 collective-permute-start
  4.7 1.5 %collective-permute-start.1 = (s32[1]{0:T(128)}, s32[1]{0:T(128)}, u32[]{:S(2)}, u32[]{:S(2)}) collective-permute-start(s32[1]{0:T(128)} %param.13), channel_id=1, source_target_pairs={{0,16},{8,24},{16,0},{24,8},{1,17},{9,25},{17,1},{25,9},{2,18},{10... | collective-permute-start | bytes 20 | tf_op jit(solution)/shard_map/ppermute | solution.py:34
  6.3 1.4 %collective-permute-start.2 = (s32[1]{0:T(128)}, s32[1]{0:T(128)}, u32[]{:S(2)}, u32[]{:S(2)}) collective-permute-start(s32[1]{0:T(128)} %param.13), channel_id=1, source_target_pairs={{0,24},{8,0},{16,8},{24,16},{1,25},{9,1},{17,9},{25,17},{2,26},{10... | collective-permute-start | bytes 20 | tf_op jit(solution)/shard_map/ppermute | solution.py:34
  7.7 2.1 %prepare.1 = (s32[1,16]{1,0:T(1,128)S(1)}, bf16[512,256]{1,0:T(8,128)(2,1)S(1)}, bf16[512,256]{1,0:T(8,128)(2,1)S(1)}, f32[2,256,128]{2,1,0:T(8,128)S(1)}, f32[2...) custom-call(bf16[512,256]{1,0:T(8,128)(2,1)} %bitcast.9, ...), custom_call_target="tpu_custom_call" | custom-call | flops 1000 | bytes 1000 | tf_op jit(solution)/shard_map/prepare/pallas_call | solution.py:229
  9.8 0.4 %collective-permute-start.4 = (bf16[256,256]{1,0:T(8,128)(2,1)S(1)}, bf16[256,256]{1,0:T(8,128)(2,1)S(1)}, u32[]{:S(2)}, u32[]{:S(2)}) collective-permute-start(bf16[256,256]{1,0:T(8,128)(2,1)S(1)} %get-tuple-element.44), channel_id=1, source_target_pairs={{0,4},{1,5},{2,6},{3,7},{4,0},{5,1},{6,2},{7,3},{8,12},{9,13},{10,... | collective-permute-start | bytes 393224 | tf_op jit(solution)/shard_map/ppermute | solution.py:34
  10.3 3.5 %own_part.1 = (bf16[512,512]{1,0:T(8,128)(2,1)S(1)}, f32[512,1024]{1,0:T(8,128)S(1)}, f32[1,2,2,256,128]{4,3,2,1,0:T(8,128)S(1)}) custom-call(s32[1,16]{1,0:T(1,128)S(1)} %get-tuple-element.30.facts_ref, bf16[512,512]{1,0:T(8,128)(2,1)} %bitcast.5, bf16[512,256]{1,0:T(8,128)(2,1)S(1)} %get-tuple-element.31.kr_ref, ...), custom_call_target="tpu_custom_call" | custom-call | flops 1000 | bytes 1000 | tf_op jit(solution)/shard_map/own_part/pallas_call | solution.py:288
  14.4 0.0 collective-permute-done.refs_1_
  14.4 1.6 %collective-permute-start.6 = (bf16[128,256]{1,0:T(8,128)(2,1)S(1)}, bf16[128,256]{1,0:T(8,128)(2,1)S(1)}, u32[]{:S(2)}, u32[]{:S(2)}) collective-permute-start(bf16[128,256]{1,0:T(8,128)(2,1)S(1)} %get-tuple-element.49), channel_id=1, source_target_pairs={{0,2},{1,3},{2,0},{3,1},{4,6},{5,7},{6,4},{7,5},{8,10},{9,11},{10,... | collective-permute-start | bytes 196616 | tf_op jit(solution)/shard_map/ppermute | solution.py:39
  16.0 0.0 collective-permute-done.1.refs_2_
  16.0 1.4 %collective-permute-start.7 = (bf16[128,256]{1,0:T(8,128)(2,1)S(1)}, bf16[128,256]{1,0:T(8,128)(2,1)S(1)}, u32[]{:S(2)}, u32[]{:S(2)}) collective-permute-start(bf16[128,256]{1,0:T(8,128)(2,1)S(1)} %get-tuple-element.50), channel_id=1, source_target_pairs={{0,3},{1,2},{2,1},{3,0},{4,7},{5,6},{6,5},{7,4},{8,11},{9,10},{10,... | collective-permute-start | bytes 196616 | tf_op jit(solution)/shard_map/ppermute | solution.py:39
  17.4 0.0 collective-permute-done.2.refs_3_
  17.4 0.5 %collective-permute-start.8 = (bf16[128,256]{1,0:T(8,128)(2,1)S(1)}, bf16[128,256]{1,0:T(8,128)(2,1)S(1)}, u32[]{:S(2)}, u32[]{:S(2)}) collective-permute-start(bf16[128,256]{1,0:T(8,128)(2,1)S(1)} %get-tuple-element.51), channel_id=1, source_target_pairs={{0,1},{1,0},{2,3},{3,2},{4,5},{5,4},{6,7},{7,6},{8,9},{9,8},{10,11... | collective-permute-start | bytes 196616 | tf_op jit(solution)/shard_map/ppermute | solution.py:39
  18.0 2.5 %masks.1 = (bf16[128,128]{1,0:T(8,128)(2,1)S(1)}, f32[512,128]{1,0:T(8,128)S(1)}) custom-call(s32[1,16]{1,0:T(1,128)S(1)} %get-tuple-element.30.facts_ref, s32[1]{0:T(128)S(6)} %copy.11.refs_0_, s32[1]{0:T(128)} %collective-permute-done.refs_1_, s32[1]{0:T(128)} %collective-permute-done.1.refs_2_, s32[1]{0:T(128)} %collective-permute-done.2.refs_3_), custom_call_target="tpu_custom_call" | custom-call | flops 1000 | bytes 1000 | tf_op jit(solution)/shard_map/masks/pallas_call | solution.py:331
  20.5 0.1 collective-permute-done.3.refs_0_
  20.6 0.4 %receive_keys.1 = (bf16[512,256]{1,0:T(8,128)(2,1)S(1)}, bf16[1,256,256]{2,1,0:T(8,128)(2,1)S(1)}) custom-call(bf16[256,512]{1,0:T(8,128)(2,1)S(1)} %get-tuple-element.38.select_ref, bf16[256,256]{1,0:T(8,128)(2,1)S(1)} %get-tuple-element.39.order_ref, f32[1,2,2,256,128]{4,3,2,1,0:T(8,128)S(1)} %get-tuple-element.40.angle_ref, ...), custom_call_target="tpu_custom_call" | custom-call | flops 10000000000 | bytes 1000 | tf_op jit(solution)/shard_map/receive_keys/pallas_call | solution.py:365
  21.0 1.3 %weigh.1 = (bf16[2,4,256,256]{3,2,1,0:T(8,128)(2,1)S(1)}, bf16[256,256]{1,0:T(8,128)(2,1)S(1)}) custom-call(s32[1,16]{1,0:T(1,128)S(1)} %get-tuple-element.30.facts_ref, f32[512,128]{1,0:T(8,128)S(1)} %get-tuple-element.36._.live_ref, bf16[512,512]{1,0:T(8,128)(2,1)S(1)} %get-tuple-element.37.q_ref, bf16[512,256]{1,0:T(8,128)(2,1)S(1)} %get-tuple-element.41.refs_0_, ...), custom_call_target="tpu_custom_call" | custom-call | flops 1000 | bytes 1000 | tf_op jit(solution)/shard_map/weigh/pallas_call | solution.py:397
  22.3 2.6 %collective-permute-start.5 = (bf16[256,256]{1,0:T(8,128)(2,1)S(1)}, bf16[256,256]{1,0:T(8,128)(2,1)S(1)}, u32[]{:S(2)}, u32[]{:S(2)}) collective-permute-start(bf16[256,256]{1,0:T(8,128)(2,1)S(1)} %get-tuple-element.45), channel_id=1, source_target_pairs={{0,4},{1,5},{2,6},{3,7},{4,0},{5,1},{6,2},{7,3},{8,12},{9,13},{10,... | collective-permute-start | bytes 393224 | tf_op jit(solution)/shard_map/ppermute | solution.py:34
  24.9 0.0 collective-permute-done.6.refs_1_
  24.9 2.1 %collective-permute-done.7.refs_2_ = bf16[128,256]{1,0:T(8,128)(2,1)S(1)} collective-permute-done((bf16[128,256]{1,0:T(8,128)(2,1)S(1)}, bf16[128,256]{1,0:T(8,128)(2,1)S(1)}, u32[]{:S(2)}, u32[]{:S(2)}) %collective-permute-start.7) | collective-permute-done | bytes 65568 | tf_op jit(solution)/shard_map/ppermute | solution.py:39
  27.0 0.0 collective-permute-done.8.refs_3_
  27.0 0.0 collective-permute-done.4.refs_1_.refs_0_
  27.0 0.1 collective-permute-start.9
  27.1 1.9 %collective-permute-start.10 = (bf16[128,256]{1,0:T(8,128)(2,1)S(1)}, bf16[128,256]{1,0:T(8,128)(2,1)S(1)}, u32[]{:S(2)}, u32[]{:S(2)}) collective-permute-start(bf16[128,256]{1,0:T(8,128)(2,1)S(1)} %get-tuple-element.55), channel_id=1, source_target_pairs={{0,3},{1,2},{2,1},{3,0},{4,7},{5,6},{6,5},{7,4},{8,11},{9,10},{10,... | collective-permute-start | bytes 196616 | tf_op jit(solution)/shard_map/ppermute | solution.py:39
  29.0 1.6 %collective-permute-start.11 = (bf16[128,256]{1,0:T(8,128)(2,1)S(1)}, bf16[128,256]{1,0:T(8,128)(2,1)S(1)}, u32[]{:S(2)}, u32[]{:S(2)}) collective-permute-start(bf16[128,256]{1,0:T(8,128)(2,1)S(1)} %get-tuple-element.56), channel_id=1, source_target_pairs={{0,1},{1,0},{2,3},{3,2},{4,5},{5,4},{6,7},{7,6},{8,9},{9,8},{10,11... | collective-permute-start | bytes 196616 | tf_op jit(solution)/shard_map/ppermute | solution.py:39
  30.6 0.0 collective-permute-done.5.refs_2_
  30.6 1.9 %attend.1 = (bf16[512,512]{1,0:T(8,128)(2,1)}, f32[8,128]{1,0:T(8,128)S(1)}) custom-call(s32[1,16]{1,0:T(1,128)S(1)} %get-tuple-element.30.facts_ref, f32[512,1024]{1,0:T(8,128)S(1)} %get-tuple-element.35.acc_ref, f32[512,128]{1,0:T(8,128)S(1)} %get-tuple-element.36._.live_ref, bf16[2,4,256,256]{3,2,1,0:T(8,128)(2,1)S(1)} %get-tuple-element.43.refs_0_, ...), custom_call_target="tpu_custom_call" | custom-call | flops 1000 | bytes 1000 | tf_op jit(solution)/shard_map/attend/pallas_call | solution.py:479
  32.5 0.0 collective-permute-done.9.refs_5_
  32.5 0.0 collective-permute-done.10.refs_6_
  32.5 0.8 %collective-permute-done.11.refs_7_ = bf16[128,256]{1,0:T(8,128)(2,1)S(1)} collective-permute-done((bf16[128,256]{1,0:T(8,128)(2,1)S(1)}, bf16[128,256]{1,0:T(8,128)(2,1)S(1)}, u32[]{:S(2)}, u32[]{:S(2)}) %collective-permute-start.11) | collective-permute-done | bytes 65568 | tf_op jit(solution)/shard_map/ppermute | solution.py:39
  33.3 1.1 %cache_part.1 = bf16[128,2048]{1,0:T(8,128)(2,1)} custom-call(bf16[128,128]{1,0:T(8,128)(2,1)S(1)} %get-tuple-element.47.kept_ref, bf16[128,256]{1,0:T(8,128)(2,1)S(1)} %get-tuple-element.48.refs_0_, bf16[128,256]{1,0:T(8,128)(2,1)S(1)} %collective-permute-done.6.refs_1_, bf16[128,256]{1,0:T(8,128)(2,1)S(1)} %collective-permute-done.7.refs_2_, ...), custom_call_target="tpu_custom_call" | custom-call | flops 1000 | bytes 1000 | tf_op jit(solution)/shard_map/cache_part/pallas_call | solution.py:504
  (1 shorter events, 0.0 us)
Async XLA Ops:
  0.6 20.0 %collective-permute-start.3 = (bf16[512,256]{1,0:T(8,128)(2,1)}, bf16[512,256]{1,0:T(8,128)(2,1)S(1)}, u32[]{:S(2)}, u32[]{:S(2)}) collective-permute-start(bf16[512,256]{1,0:T(8,128)(2,1)} %bitcast.8), channel_id=1, source_target_pairs={{0,4},{1,5},{2,6},{3,7},{4,0},{5,1},{6,2},{7,3},{8,12},{9,13},{10,... | collective-permute-start | bytes 786440 | tf_op jit(solution)/shard_map/ppermute | solution.py:34
  4.7 9.6 %collective-permute-start = (s32[1]{0:T(128)}, s32[1]{0:T(128)}, u32[]{:S(2)}, u32[]{:S(2)}) collective-permute-start(s32[1]{0:T(128)} %param.13), channel_id=1, source_target_pairs={{0,8},{8,16},{16,24},{24,0},{1,9},{9,17},{17,25},{25,1},{2,10},{10... | collective-permute-start | bytes 20 | tf_op jit(solution)/shard_map/ppermute | solution.py:34
  4.7 11.3 %collective-permute-start.1 = (s32[1]{0:T(128)}, s32[1]{0:T(128)}, u32[]{:S(2)}, u32[]{:S(2)}) collective-permute-start(s32[1]{0:T(128)} %param.13), channel_id=1, source_target_pairs={{0,16},{8,24},{16,0},{24,8},{1,17},{9,25},{17,1},{25,9},{2,18},{10... | collective-permute-start | bytes 20 | tf_op jit(solution)/shard_map/ppermute | solution.py:34
  6.3 11.2 %collective-permute-start.2 = (s32[1]{0:T(128)}, s32[1]{0:T(128)}, u32[]{:S(2)}, u32[]{:S(2)}) collective-permute-start(s32[1]{0:T(128)} %param.13), channel_id=1, source_target_pairs={{0,24},{8,0},{16,8},{24,16},{1,25},{9,1},{17,9},{25,17},{2,26},{10... | collective-permute-start | bytes 20 | tf_op jit(solution)/shard_map/ppermute | solution.py:34
  9.8 17.2 %collective-permute-start.4 = (bf16[256,256]{1,0:T(8,128)(2,1)S(1)}, bf16[256,256]{1,0:T(8,128)(2,1)S(1)}, u32[]{:S(2)}, u32[]{:S(2)}) collective-permute-start(bf16[256,256]{1,0:T(8,128)(2,1)S(1)} %get-tuple-element.44), channel_id=1, source_target_pairs={{0,4},{1,5},{2,6},{3,7},{4,0},{5,1},{6,2},{7,3},{8,12},{9,13},{10,... | collective-permute-start | bytes 393224 | tf_op jit(solution)/shard_map/ppermute | solution.py:34
  14.4 10.5 %collective-permute-start.6 = (bf16[128,256]{1,0:T(8,128)(2,1)S(1)}, bf16[128,256]{1,0:T(8,128)(2,1)S(1)}, u32[]{:S(2)}, u32[]{:S(2)}) collective-permute-start(bf16[128,256]{1,0:T(8,128)(2,1)S(1)} %get-tuple-element.49), channel_id=1, source_target_pairs={{0,2},{1,3},{2,0},{3,1},{4,6},{5,7},{6,4},{7,5},{8,10},{9,11},{10,... | collective-permute-start | bytes 196616 | tf_op jit(solution)/shard_map/ppermute | solution.py:39
  16.0 11.0 %collective-permute-start.7 = (bf16[128,256]{1,0:T(8,128)(2,1)S(1)}, bf16[128,256]{1,0:T(8,128)(2,1)S(1)}, u32[]{:S(2)}, u32[]{:S(2)}) collective-permute-start(bf16[128,256]{1,0:T(8,128)(2,1)S(1)} %get-tuple-element.50), channel_id=1, source_target_pairs={{0,3},{1,2},{2,1},{3,0},{4,7},{5,6},{6,5},{7,4},{8,11},{9,10},{10,... | collective-permute-start | bytes 196616 | tf_op jit(solution)/shard_map/ppermute | solution.py:39
  17.4 9.6 %collective-permute-start.8 = (bf16[128,256]{1,0:T(8,128)(2,1)S(1)}, bf16[128,256]{1,0:T(8,128)(2,1)S(1)}, u32[]{:S(2)}, u32[]{:S(2)}) collective-permute-start(bf16[128,256]{1,0:T(8,128)(2,1)S(1)} %get-tuple-element.51), channel_id=1, source_target_pairs={{0,1},{1,0},{2,3},{3,2},{4,5},{5,4},{6,7},{7,6},{8,9},{9,8},{10,11... | collective-permute-start | bytes 196616 | tf_op jit(solution)/shard_map/ppermute | solution.py:39
  22.3 8.3 %collective-permute-start.5 = (bf16[256,256]{1,0:T(8,128)(2,1)S(1)}, bf16[256,256]{1,0:T(8,128)(2,1)S(1)}, u32[]{:S(2)}, u32[]{:S(2)}) collective-permute-start(bf16[256,256]{1,0:T(8,128)(2,1)S(1)} %get-tuple-element.45), channel_id=1, source_target_pairs={{0,4},{1,5},{2,6},{3,7},{4,0},{5,1},{6,2},{7,3},{8,12},{9,13},{10,... | collective-permute-start | bytes 393224 | tf_op jit(solution)/shard_map/ppermute | solution.py:34
  27.0 5.5 %collective-permute-start.9 = (bf16[128,256]{1,0:T(8,128)(2,1)S(1)}, bf16[128,256]{1,0:T(8,128)(2,1)S(1)}, u32[]{:S(2)}, u32[]{:S(2)}) collective-permute-start(bf16[128,256]{1,0:T(8,128)(2,1)S(1)} %get-tuple-element.54), channel_id=1, source_target_pairs={{0,2},{1,3},{2,0},{3,1},{4,6},{5,7},{6,4},{7,5},{8,10},{9,11},{10,... | collective-permute-start | bytes 196616 | tf_op jit(solution)/shard_map/ppermute | solution.py:39
  27.1 5.4 %collective-permute-start.10 = (bf16[128,256]{1,0:T(8,128)(2,1)S(1)}, bf16[128,256]{1,0:T(8,128)(2,1)S(1)}, u32[]{:S(2)}, u32[]{:S(2)}) collective-permute-start(bf16[128,256]{1,0:T(8,128)(2,1)S(1)} %get-tuple-element.55), channel_id=1, source_target_pairs={{0,3},{1,2},{2,1},{3,0},{4,7},{5,6},{6,5},{7,4},{8,11},{9,10},{10,... | collective-permute-start | bytes 196616 | tf_op jit(solution)/shard_map/ppermute | solution.py:39
  29.0 4.3 %collective-permute-start.11 = (bf16[128,256]{1,0:T(8,128)(2,1)S(1)}, bf16[128,256]{1,0:T(8,128)(2,1)S(1)}, u32[]{:S(2)}, u32[]{:S(2)}) collective-permute-start(bf16[128,256]{1,0:T(8,128)(2,1)S(1)} %get-tuple-element.56), channel_id=1, source_target_pairs={{0,1},{1,0},{2,3},{3,2},{4,5},{5,4},{6,7},{7,6},{8,9},{9,8},{10,11... | collective-permute-start | bytes 196616 | tf_op jit(solution)/shard_map/ppermute | solution.py:39
